TPU v7x, 32 devices: a whole 2x2x4 slice. The times are simulated.
32 devices in a mesh: groups: 2 (over y), batch: 4 (over z), weight: 4 (over x, core).
Axes of the slice: x: 2, y: 2, z: 4, core: 2. Of those that a mesh axis runs over, the one named last changes fastest.
Arguments:
- tokens: bfloat16 [4096, 2048], P(('groups', 'batch'), 'weight'), parts along dimension 0, may hold values from -6 to 6
- gate_weight: bfloat16 [2048, 3072], P('batch', 'weight'), may hold values from -0.125 to 0.125
- up_weight: bfloat16 [2048, 3072], P('batch', 'weight'), may hold values from -0.125 to 0.125
- down_weight: bfloat16 [3072, 2048], P(None, ('weight', 'batch')), may hold values from -0.109375 to 0.109375
Outputs:
- layer_out: bfloat16 [4096, 2048], P(('groups', 'batch'), 'weight'), parts along dimension 0
There are 2 independent parts, one for each index of `groups`. A program takes and returns all parts, laid end to end along the dimension named above; an argument that names none is the same for every part. Nothing has to cross between parts.
All inputs are finite; a program needn't handle non-finite values.
Results may differ from a plain program's by a relative error of at most 0.0051.
Values may be sent and summed in bfloat16 or wider, within the bound.
No kernel may reach another device: no remote copies, remote signals or barrier semaphores. Data moves between devices by JAX's collectives and lax.ppermute only.
A program may use at most 64 MiB of HBM per device.

v0:
```python
import jax
import jax.numpy as jnp
from jax import lax
from jax.sharding import PartitionSpec as P


def shards(tokens, gate_weight, up_weight, down_weight):
    features_all = lax.all_gather(tokens, "weight", axis=1, tiled=True)
    gate_sum = jnp.dot(
        features_all,
        lax.all_gather(gate_weight, "batch", axis=0, tiled=True),
        preferred_element_type=jnp.float32,
    )
    up_sum = jnp.dot(
        features_all,
        lax.all_gather(up_weight, "batch", axis=0, tiled=True),
        preferred_element_type=jnp.float32,
    )
    hidden = (jax.nn.silu(gate_sum) * up_sum).astype(jnp.bfloat16)
    hidden_all = lax.all_gather(hidden, "weight", axis=1, tiled=True)
    return jnp.dot(
        hidden_all,
        lax.all_gather(down_weight, "batch", axis=1, tiled=True),
        preferred_element_type=jnp.float32,
    ).astype(jnp.bfloat16)


def solution(mesh):
    in_specs = (
        P(("groups", "batch"), "weight"),
        P("batch", "weight"),
        P("batch", "weight"),
        P(None, ("weight", "batch")),
    )
    out_specs = P(("groups", "batch"), "weight")
    return jax.shard_map(shards, mesh=mesh, in_specs=in_specs, out_specs=out_specs, check_vma=False)
```

profile of v0, /device:TPU:0, one launch (start us, length us, event | category | flops | bytes accessed | tf_op | source)
XLA Modules:
  0.0 266.7 jit_solution(15280983768284148116)
XLA Ops:
  6.5 0.0 all-gather.6.cloned.1.call-start
  6.5 0.7 all-gather.6.cloned.1.call-update
  7.3 0.0 all-gather.8.cloned.1.call-start
  7.3 0.7 all-gather.8.cloned.1.call-update
  8.0 0.0 all-gather.10.cloned.1.call-start
  8.1 0.7 all-gather.10.cloned.1.call-update
  8.7 0.0 all-gather.14.cloned.1.call-start
  8.8 0.5 all-gather.14.cloned.1.call-update
  9.3 0.0 all-gather.12.cloned.1.call-start
  9.4 24.9 %all-gather.6.cloned.1.call-done = bf16[512,2048]{1,0:T(8,128)(2,1)} async-done(((bf16[512,512]{1,0:T(8,128)(2,1)}), bf16[512,2048]{1,0:T(8,128)(2,1)}) %all-gather.6.cloned.1.call-update) | async-done | bytes 2097168 | tf_op jit(solution)/shard_map/all_gather | solution.py:8
  34.2 0.0 copy-start
  34.2 65.1 %all-gather.8.cloned.1.call-done = bf16[2048,768]{1,0:T(8,128)(2,1)} async-done(((bf16[512,768]{1,0:T(8,128)(2,1)}), bf16[2048,768]{1,0:T(8,128)(2,1)}) %all-gather.8.cloned.1.call-update) | async-done | bytes 3145744 | tf_op jit(solution)/shard_map/all_gather | solution.py:11
  99.3 5.5 %fusion = f32[512,768]{1,0:T(8,128)} fusion(bf16[512,2048]{1,0:T(8,128)(2,1)} %all-gather.6.cloned.1.call-done, bf16[2048,768]{1,0:T(8,128)(2,1)} %all-gather.8.cloned.1.call-done), kind=kOutput, calls=%fused_computation.2 | convolution fusion | flops 1610612736 | bytes 6815744 | tf_op jit(solution)/shard_map/dot_general | solution.py:9
  104.9 58.2 %all-gather.10.cloned.1.call-done = bf16[2048,768]{1,0:T(8,128)(2,1)} async-done(((bf16[512,768]{1,0:T(8,128)(2,1)}), bf16[2048,768]{1,0:T(8,128)(2,1)}) %all-gather.10.cloned.1.call-update) | async-done | bytes 3145744 | tf_op jit(solution)/shard_map/all_gather | solution.py:16
  163.1 0.0 copy-done
  163.1 5.1 %multiply_convert_fusion = bf16[512,768]{1,0:T(8,128)(2,1)} fusion(f32[512,768]{1,0:T(8,128)} %fusion, bf16[512,2048]{1,0:T(8,128)(2,1)S(1)} %copy-done, bf16[2048,768]{1,0:T(8,128)(2,1)} %all-gather.10.cloned.1.call-done), kind=kOutput, calls=%fused_computation | convolution fusion | flops 1612972032 | bytes 7602176 | tf_op jit(solution)/shard_map/dot_general | solution.py:14
  168.2 0.0 all-gather.12.cloned.1.call-update
  168.3 58.4 %all-gather.14.cloned.1.call-done = bf16[3072,512]{1,0:T(8,128)(2,1)} async-done(((bf16[3072,128]{1,0:T(8,128)(2,1)}), bf16[3072,512]{1,0:T(8,128)(2,1)}) %all-gather.14.cloned.1.call-update) | async-done | bytes 3145744 | tf_op jit(solution)/shard_map/all_gather | solution.py:23
  226.6 28.2 %all-gather.12.cloned.1.call-done = bf16[512,3072]{1,0:T(8,128)(2,1)} async-done(((bf16[512,768]{1,0:T(8,128)(2,1)}), bf16[512,3072]{1,0:T(8,128)(2,1)}) %all-gather.12.cloned.1.call-update) | async-done | bytes 3145744 | tf_op jit(solution)/shard_map/all_gather | solution.py:20
  254.8 5.4 %convolution_convert_fusion = bf16[512,512]{1,0:T(8,128)(2,1)} fusion(bf16[512,3072]{1,0:T(8,128)(2,1)} %all-gather.12.cloned.1.call-done, bf16[3072,512]{1,0:T(8,128)(2,1)} %all-gather.14.cloned.1.call-done), kind=kOutput, calls=%fused_computation.1 | convolution fusion | flops 1610874880 | bytes 6815744 | tf_op jit(solution)/shard_map/dot_general | solution.py:21
Async XLA Ops:
  6.5 27.7 %all-gather.6.cloned.1.call-start = ((), (), s32[]{:S(2)}) async-start(), calls=%async_computation | async-start | bytes 2621440 | tf_op jit(solution)/shard_map/all_gather | solution.py:8
  7.3 92.1 %all-gather.8.cloned.1.call-start = ((), (), s32[]{:S(2)}) async-start(), calls=%async_computation.1 | async-start | bytes 3932160 | tf_op jit(solution)/shard_map/all_gather | solution.py:11
  8.0 155.1 %all-gather.10.cloned.1.call-start = ((), (), s32[]{:S(2)}) async-start(), calls=%async_computation.2 | async-start | bytes 3932160 | tf_op jit(solution)/shard_map/all_gather | solution.py:16
  8.7 217.9 %all-gather.14.cloned.1.call-start = ((), (), s32[]{:S(2)}) async-start(), calls=%async_computation.4 | async-start | bytes 3932160 | tf_op jit(solution)/shard_map/all_gather | solution.py:23
  9.3 245.5 %all-gather.12.cloned.1.call-start = ((), (), s32[]{:S(2)}) async-start(), calls=%async_computation.3 | async-start | bytes 3932160 | tf_op jit(solution)/shard_map/all_gather | solution.py:20
  34.2 128.9 %copy-start = (bf16[512,2048]{1,0:T(8,128)(2,1)S(1)}, bf16[512,2048]{1,0:T(8,128)(2,1)}, u32[]{:S(2)}) copy-start(bf16[512,2048]{1,0:T(8,128)(2,1)} %all-gather.6.cloned.1.call-done) | copy-start | bytes 6291460
Sparse Core Ops, SparseCore 0:
  8.9 25.2 all-gather.5
  35.8 63.4 all-gather.7
  100.9 62.1 all-gather.9
  164.5 62.0 all-gather.13
  228.0 26.7 all-gather.11
where the time goes:
time: 267 us
  waiting for transfers between devices  237 us (89%)
  matrix products  16.1 us (6%)
  between operations  13.1 us (5%)
    all_gather x1, waiting for transfers between devices, shards(): lax.all_gather(gate_weight, 'batch', axis=0, tiled=True)  65.1 us
    all_gather x1, waiting for transfers between devices, shards(): lax.all_gather(down_weight, 'batch', axis=1, tiled=True)  58.4 us
    all_gather x1, waiting for transfers between devices, shards(): lax.all_gather(up_weight, 'batch', axis=0, tiled=True)  58.2 us
    all_gather x1, waiting for transfers between devices, shards(): hidden_all = lax.all_gather(hidden, 'weight', axis=1, tiled=True)  28.2 us
    all_gather x1, waiting for transfers between devices, shards(): features_all = lax.all_gather(tokens, 'weight', axis=1, tiled=True)  24.9 us
    dot_general x1, matrix products, shards(): jnp.dot(features_all, lax.all_gather(gate_weight, 'batch', axis=0, tiled=...  5.54 us
    dot_general x1, matrix products, shards(): jnp.dot(hidden_all, lax.all_gather(down_weight, 'batch', axis=1, tiled=Tr...  5.42 us
  transfers between devices with their start and end apart: 5, of which 5 were waited for; matrix products, arithmetic and copies ran while one was open for 4% of the time, Pallas kernels for 0%

commit v1 on v0

v1 whole, which is shorter than its diff:
```python
import jax
import jax.numpy as jnp
from jax import lax
from jax.sharding import PartitionSpec as P

F32 = jnp.float32
BF16 = jnp.bfloat16


def dot(a, b):
    return jnp.dot(a, b, preferred_element_type=F32)


def after(value, *earlier):
    return lax.optimization_barrier((value, *earlier))[0]


def shards(sizes, tokens, gate_weight, up_weight, down_weight):
    n_batch, n_weight = sizes["batch"], sizes["weight"]
    plane = lax.axis_index("batch")
    place = lax.axis_index("weight")
    first = lax.axis_index("groups") == 0
    even = plane % 2 == 0
    rows, features = tokens.shape
    depth, units = gate_weight.shape
    half = units // 2
    columns = down_weight.shape[1]
    few = n_batch == n_weight == 4

    def flip(x, axis, bits):
        return lax.ppermute(x, axis, [(i, i ^ bits) for i in range(sizes[axis])])

    def own_half(weight):
        return jnp.where(even, weight[:, :half], weight[:, half:])

    def other_half(weight):
        return jnp.where(even, weight[:, half:], weight[:, :half])

    def sorted_pair(mine, theirs):
        return jnp.where(first, mine, theirs), jnp.where(first, theirs, mine)

    down_blocks = down_weight.reshape(n_weight, 2, half, columns)
    down_own = jnp.where(even, down_blocks[:, 0], down_blocks[:, 1])
    down_other = jnp.where(even, down_blocks[:, 1], down_blocks[:, 0])

    pair_rows = flip(tokens, "batch", 1)
    if few:
        tokens_x = flip(tokens, "weight", 2)

        send_own = jnp.where(first, own_half(gate_weight), own_half(up_weight))
        send_other = jnp.where(first, other_half(gate_weight), other_half(up_weight))
        keep_own = jnp.where(first, own_half(up_weight), own_half(gate_weight))
        direct = {0: send_own, 2: flip(send_own, "batch", 2), 1: flip(send_other, "batch", 1)}
        pair_x = flip(pair_rows, "weight", 2)
        direct[3] = flip(after(send_other, tokens_x), "batch", 3)
        swapped = {0: keep_own}
        for j in (1, 2, 3):
            swapped[j] = flip(direct[j], "groups", 1)

        near = jnp.concatenate([pair_rows, tokens], axis=0)
        far = jnp.concatenate([pair_x, tokens_x], axis=0)
        token_blocks = jnp.stack([near, flip(near, "weight", 1), far, flip(far, "weight", 1)])

        sums = [0.0, 0.0]
        for j in (0, 1, 2, 3):
            t = lax.dynamic_index_in_dim(token_blocks, place ^ plane ^ j, 0, keepdims=False)
            sums[0] += dot(t, direct[j])
            sums[1] += dot(t, swapped[j])

        low, high = slice(0, n_weight // 2), slice(n_weight // 2, n_weight)
        down_all = jnp.zeros((n_weight, half, n_batch * columns), BF16)
        down_all = lax.dynamic_update_slice(down_all, down_own, (0, 0, plane * columns))
        for j in (2, 3, 1):
            source = down_own if j == 2 else down_other
            part = jnp.where(first, source[low], source[high])
            mine = flip(after(part, swapped[1]), "batch", j)
            block = jnp.concatenate(sorted_pair(mine, flip(mine, "groups", 1)), axis=0)
            down_all = lax.dynamic_update_slice(down_all, block, (0, 0, (plane ^ j) * columns))
    else:
        both = lax.all_gather(jnp.concatenate([pair_rows, tokens], axis=0), "weight", axis=1, tiled=True)
        mine = lax.all_gather(jnp.where(first, gate_weight, up_weight), "batch", axis=0, tiled=True)
        mine = own_half(mine)
        sums = [dot(both, mine), dot(both, flip(mine, "groups", 1))]
        down_all = lax.all_gather(down_weight, "batch", axis=1, tiled=True)
        down_all = down_all.reshape(n_weight, 2, half, n_batch * columns)
        down_all = jnp.where(even, down_all[:, 0], down_all[:, 1])
    down_all = jnp.concatenate(
        [lax.dynamic_index_in_dim(down_all, place ^ i, 0, keepdims=False) for i in range(n_weight)], axis=0
    )

    def part_of_output(part):
        mine, theirs = (lax.slice_in_dim(s, part * rows, (part + 1) * rows) for s in sums)
        gate_sum, up_sum = sorted_pair(mine, theirs)
        hidden = (jax.nn.silu(gate_sum) * up_sum).astype(BF16)
        far = flip(hidden, "weight", 2)
        hidden = jnp.concatenate([hidden, flip(hidden, "weight", 1), far, flip(far, "weight", 1)], axis=1)
        return dot(hidden, down_all)

    theirs = flip(part_of_output(0).astype(BF16), "batch", 1)
    return (part_of_output(1) + theirs).astype(BF16)


def solution(mesh):
    in_specs = (
        P(("groups", "batch"), "weight"),
        P("batch", "weight"),
        P("batch", "weight"),
        P(None, ("weight", "batch")),
    )
    out_specs = P(("groups", "batch"), "weight")
    sizes = dict(mesh.shape)

    def body(*args):
        return shards(sizes, *args)

    return jax.shard_map(body, mesh=mesh, in_specs=in_specs, out_specs=out_specs, check_vma=False)
```

time: 267 us -> 125 us (0.47)
  waiting for transfers between devices: 237 us -> 66.1 us
  starting transfers between devices: 0.15 us -> 33.3 us
  between operations: 13.1 us -> 0.31 us
  local copies, waits for them, and re-layouts: 0.01 us -> 7.71 us
  other arithmetic: 0 us -> 6.63 us
  matrix products: 16.1 us -> 10.9 us
    all_gather x5 -> x0, waiting for transfers between devices: 235 us -> none  [the longest x1 65.1 us: shards(): lax.all_gather(gate_weight, 'batch', axis=0, tiled=True)]
    ppermute x0 -> x24, waiting for transfers between devices: none -> 66.1 us  [flip(): return lax.ppermute(x, axis, [(i, i ^ bits) for i in range(sizes[axis])])]
    ppermute x0 -> x24, starting transfers between devices: none -> 33.3 us  [flip(): return lax.ppermute(x, axis, [(i, i ^ bits) for i in range(sizes[axis])])]
    dot_general x3 -> x10, matrix products: 16.1 us -> 10.9 us  [dot(): return jnp.dot(a, b, preferred_element_type=F32)]
    unnamed x2 -> x16, local copies, waits for them, and re-layouts: 0.01 us -> 4.53 us
  transfers between devices with their start and end apart: 5 -> 24, of which waited for: 5 -> 14; matrix products, arithmetic and copies ran while one was open for 4% -> 19% of each run, Pallas kernels for 0% -> 0%
where the time goes in v1:
time: 125 us
  waiting for transfers between devices  66.1 us (53%)
  starting transfers between devices  33.3 us (27%)
  matrix products  10.9 us (9%)
  local copies, waits for them, and re-layouts  7.71 us (6%)
  other arithmetic  6.63 us (5%)
    ppermute x24, waiting for transfers between devices, flip(): return lax.ppermute(x, axis, [(i, i ^ bits) for i in range(sizes[axis])])  66.1 us
    ppermute x24, starting transfers between devices, flip(): return lax.ppermute(x, axis, [(i, i ^ bits) for i in range(sizes[axis])])  33.3 us
    dot_general x10, matrix products, dot(): return jnp.dot(a, b, preferred_element_type=F32)  10.9 us
    unnamed x16, local copies, waits for them, and re-layouts  4.53 us
  transfers between devices with their start and end apart: 24, of which 14 were waited for; matrix products, arithmetic and copies ran while one was open for 19% of the time, Pallas kernels for 0%

profile of v1, /device:TPU:0, one launch (start us, length us, event | category | flops | bytes accessed | tf_op | source)
XLA Modules:
  0.0 125.0 jit_solution(2033873938720553259)
XLA Ops:
  0.0 3.0 %collective-permute-start = (bf16[512,512]{1,0:T(8,128)(2,1)}, bf16[512,512]{1,0:T(8,128)(2,1)}, u32[]{:S(2)}, u32[]{:S(2)}) collective-permute-start(bf16[512,512]{1,0:T(8,128)(2,1)} %param.4), channel_id=1, source_target_pairs={{0,4},{4,0},{8,12},{12,8},{1,5},{5,1},{9,13},{13,9},{2,6},{6,2},{1... | collective-permute-start | bytes 1572872 | tf_op jit(solution)/shard_map/ppermute | solution.py:31
  5.5 10.6 %collective-permute-done = bf16[512,512]{1,0:T(8,128)(2,1)} collective-permute-done((bf16[512,512]{1,0:T(8,128)(2,1)}, bf16[512,512]{1,0:T(8,128)(2,1)}, u32[]{:S(2)}, u32[]{:S(2)}) %collective-permute-start) | collective-permute-done | bytes 524320 | tf_op jit(solution)/shard_map/ppermute | solution.py:31
  16.1 2.0 %collective-permute-start.2 = (bf16[512,512]{1,0:T(8,128)(2,1)}, bf16[512,512]{1,0:T(8,128)(2,1)}, u32[]{:S(2)}, u32[]{:S(2)}) collective-permute-start(bf16[512,512]{1,0:T(8,128)(2,1)} %collective-permute-done), channel_id=1, source_target_pairs={{0,2},{1,3},{2,0},{3,1},{4,6},{5,7},{6,4},{7,5},{8,10},{9,11},{10,... | collective-permute-start | bytes 1572872 | tf_op jit(solution)/shard_map/ppermute | solution.py:31
  18.1 3.1 %collective-permute-start.6 = (bf16[512,384]{0,1:T(8,128)(2,1)S(1)}, bf16[512,384]{0,1:T(8,128)(2,1)}, u32[]{:S(2)}, u32[]{:S(2)}) collective-permute-start(bf16[512,384]{0,1:T(8,128)(2,1)S(1)} %get-tuple-element.20), channel_id=1, source_target_pairs={{0,8},{4,12},{8,0},{12,4},{1,9},{5,13},{9,1},{13,5},{2,10},{6,14},... | collective-permute-start | bytes 1179656 | tf_op jit(solution)/shard_map/ppermute | solution.py:31
  21.2 8.8 %collective-permute-done.5 = bf16[512,384]{0,1:T(8,128)(2,1)} collective-permute-done((bf16[512,384]{0,1:T(8,128)(2,1)S(1)}, bf16[512,384]{0,1:T(8,128)(2,1)}, u32[]{:S(2)}, u32[]{:S(2)}) %collective-permute-start.5) | collective-permute-done | bytes 393248 | tf_op jit(solution)/shard_map/ppermute | solution.py:31
  30.0 1.8 %collective-permute-start.8 = (bf16[512,384]{0,1:T(8,128)(2,1)}, bf16[512,384]{0,1:T(8,128)(2,1)}, u32[]{:S(2)}, u32[]{:S(2)}) collective-permute-start(bf16[512,384]{0,1:T(8,128)(2,1)} %collective-permute-done.5), channel_id=1, source_target_pairs={{0,16},{16,0},{1,17},{17,1},{2,18},{18,2},{3,19},{19,3},{4,20},{20... | collective-permute-start | bytes 1179656 | tf_op jit(solution)/shard_map/ppermute | solution.py:31
  31.9 1.9 %constant_dynamic-update-slice_fusion.1 = bf16[1024,512]{1,0:T(8,128)(2,1)} fusion(bf16[512,512]{1,0:T(8,128)(2,1)} %collective-permute-done), kind=kLoop, calls=%fused_computation.76 | loop fusion | bytes 1048576
  34.6 1.9 %constant_dynamic-update-slice_fusion.3 = bf16[1024,512]{1,0:T(8,128)(2,1)} fusion(bf16[512,512]{1,0:T(8,128)(2,1)} %collective-permute-done.2), kind=kLoop, calls=%fused_computation.78 | loop fusion | bytes 1048576
  36.5 3.4 %collective-permute-done.3 = bf16[512,512]{1,0:T(8,128)(2,1)S(1)} collective-permute-done((bf16[512,512]{1,0:T(8,128)(2,1)S(1)}, bf16[512,512]{1,0:T(8,128)(2,1)S(1)}, u32[]{:S(2)}, u32[]{:S(2)}) %collective-permute-start.3) | collective-permute-done | bytes 524320 | tf_op jit(solution)/shard_map/ppermute | solution.py:31
  42.9 2.5 %collective-permute-start.14 = (bf16[2,384,128]{2,1,0:T(8,128)(2,1)S(1)}, bf16[2,384,128]{2,1,0:T(8,128)(2,1)S(1)}, u32[]{:S(2)}, u32[]{:S(2)}) collective-permute-start(bf16[2,384,128]{2,1,0:T(8,128)(2,1)S(1)} %fusion.56), channel_id=1, source_target_pairs={{0,8},{4,12},{8,0},{12,4},{1,9},{5,13},{9,1},{13,5},{2,10},{6,14},... | collective-permute-start | bytes 589832 | tf_op jit(solution)/shard_map/ppermute | solution.py:31
  46.5 1.4 %collective-permute-start.7 = (bf16[512,384]{0,1:T(8,128)(2,1)S(1)}, bf16[512,384]{0,1:T(8,128)(2,1)S(1)}, u32[]{:S(2)}, u32[]{:S(2)}) collective-permute-start(bf16[512,384]{0,1:T(8,128)(2,1)S(1)} %copy-done.4), channel_id=1, source_target_pairs={{0,12},{4,8},{8,4},{12,0},{1,13},{5,9},{9,5},{13,1},{2,14},{6,10},... | collective-permute-start | bytes 1179656 | tf_op jit(solution)/shard_map/ppermute | solution.py:31
  47.9 16.2 %collective-permute-done.14 = bf16[2,384,128]{2,1,0:T(8,128)(2,1)S(1)} collective-permute-done((bf16[2,384,128]{2,1,0:T(8,128)(2,1)S(1)}, bf16[2,384,128]{2,1,0:T(8,128)(2,1)S(1)}, u32[]{:S(2)}, u32[]{:S(2)}) %collective-permute-start.14) | collective-permute-done | bytes 196640 | tf_op jit(solution)/shard_map/ppermute | solution.py:31
  65.6 3.2 %collective-permute-start.16 = (bf16[2,384,128]{2,1,0:T(8,128)(2,1)S(1)}, bf16[2,384,128]{2,1,0:T(8,128)(2,1)S(1)}, u32[]{:S(2)}, u32[]{:S(2)}) collective-permute-start(bf16[2,384,128]{2,1,0:T(8,128)(2,1)S(1)} %fusion.55), channel_id=1, source_target_pairs={{0,12},{4,8},{8,4},{12,0},{1,13},{5,9},{9,5},{13,1},{2,14},{6,10},... | collective-permute-start | bytes 589832 | tf_op jit(solution)/shard_map/ppermute | solution.py:31
  68.8 1.5 %collective-permute-done.15 = bf16[2,384,128]{2,1,0:T(8,128)(2,1)S(1)} collective-permute-done((bf16[2,384,128]{2,1,0:T(8,128)(2,1)S(1)}, bf16[2,384,128]{2,1,0:T(8,128)(2,1)S(1)}, u32[]{:S(2)}, u32[]{:S(2)}) %collective-permute-start.15) | collective-permute-done | bytes 196640 | tf_op jit(solution)/shard_map/ppermute | solution.py:31
  71.2 1.6 %collective-permute-start.9 = (bf16[512,384]{0,1:T(8,128)(2,1)}, bf16[512,384]{0,1:T(8,128)(2,1)S(1)}, u32[]{:S(2)}, u32[]{:S(2)}) collective-permute-start(bf16[512,384]{0,1:T(8,128)(2,1)} %collective-permute-done.6), channel_id=1, source_target_pairs={{0,16},{16,0},{1,17},{17,1},{2,18},{18,2},{3,19},{19,3},{4,20},{20... | collective-permute-start | bytes 1179656 | tf_op jit(solution)/shard_map/ppermute | solution.py:31
  74.6 3.3 %collective-permute-done.18 = bf16[2,384,128]{2,1,0:T(8,128)(2,1)S(1)} collective-permute-done((bf16[2,384,128]{2,1,0:T(8,128)(2,1)S(1)}, bf16[2,384,128]{2,1,0:T(8,128)(2,1)S(1)}, u32[]{:S(2)}, u32[]{:S(2)}) %collective-permute-start.18) | collective-permute-done | bytes 196640 | tf_op jit(solution)/shard_map/ppermute | solution.py:31
  78.4 1.5 %collective-permute-start.19 = (bf16[2,384,128]{2,1,0:T(8,128)(2,1)S(1)}, bf16[2,384,128]{2,1,0:T(8,128)(2,1)S(1)}, u32[]{:S(2)}, u32[]{:S(2)}) collective-permute-start(bf16[2,384,128]{2,1,0:T(8,128)(2,1)S(1)} %collective-permute-done.18), channel_id=1, source_target_pairs={{0,16},{16,0},{1,17},{17,1},{2,18},{18,2},{3,19},{19,3},{4,20},{20... | collective-permute-start | bytes 589832 | tf_op jit(solution)/shard_map/ppermute | solution.py:31
  79.9 2.4 %pad_maximum_fusion = bf16[4,1024,512]{2,1,0:T(8,128)(2,1)S(1)} fusion(bf16[1,1024,512]{2,1,0:T(8,128)(2,1)} %bitcast.3, bf16[1,1024,512]{2,1,0:T(8,128)(2,1)} %bitcast.2, bf16[1,1024,512]{2,1,0:T(8,128)(2,1)} %bitcast.1, bf16[1,1024,512]{2,1,0:T(8,128)(2,1)} %bitcast), kind=kLoop, calls=%fused_computation | loop fusion | flops 6291456 | bytes 8388608 | tf_op jit(solution)/shard_map/stack | solution.py:62
  83.0 1.6 %fusion.37 = f32[1024,384]{0,1:T(8,128)S(1)} fusion(bf16[512,384]{0,1:T(8,128)(2,1)} %collective-permute-done.8, bf16[4,1024,512]{2,1,0:T(8,128)(2,1)S(1)} %pad_maximum_fusion, s32[]{:T(128)S(6)} %select_n.170), kind=kOutput, calls=%fused_computation.31 | convolution fusion | flops 402653184 | bytes 3014660 | tf_op jit(solution)/shard_map/dot_general | solution.py:11
  84.6 1.6 %fusion.39 = f32[1024,384]{0,1:T(8,128)S(1)} fusion(bf16[512,384]{0,1:T(8,128)(2,1)} %collective-permute-done.5, bf16[4,1024,512]{2,1,0:T(8,128)(2,1)S(1)} %pad_maximum_fusion, s32[]{:T(128)S(6)} %select_n.170), kind=kOutput, calls=%fused_computation.33 | convolution fusion | flops 402653184 | bytes 3014660 | tf_op jit(solution)/shard_map/dot_general | solution.py:11
  86.2 1.6 %fusion.35 = f32[1024,384]{0,1:T(8,128)S(1)} fusion(bf16[512,384]{0,1:T(8,128)(2,1)} %collective-permute-done.6, bf16[4,1024,512]{2,1,0:T(8,128)(2,1)S(1)} %pad_maximum_fusion, s32[]{:T(128)S(6)} %select_n.174), kind=kOutput, calls=%fused_computation.29 | convolution fusion | flops 402653184 | bytes 3014660 | tf_op jit(solution)/shard_map/dot_general | solution.py:11
  89.8 2.2 %collective-permute-done.10 = bf16[512,384]{0,1:T(8,128)(2,1)S(1)} collective-permute-done((bf16[512,384]{0,1:T(8,128)(2,1)S(1)}, bf16[512,384]{0,1:T(8,128)(2,1)S(1)}, u32[]{:S(2)}, u32[]{:S(2)}) %collective-permute-start.10) | collective-permute-done | bytes 393248 | tf_op jit(solution)/shard_map/ppermute | solution.py:31
  93.2 1.6 %collective-permute-start.21 = (bf16[512,384]{0,1:T(8,128)(2,1)S(1)}, bf16[512,384]{0,1:T(8,128)(2,1)S(1)}, u32[]{:S(2)}, u32[]{:S(2)}) collective-permute-start(bf16[512,384]{0,1:T(8,128)(2,1)S(1)} %get-tuple-element.13), channel_id=1, source_target_pairs={{0,2},{1,3},{2,0},{3,1},{4,6},{5,7},{6,4},{7,5},{8,10},{9,11},{10,... | collective-permute-start | bytes 1179656 | tf_op jit(solution)/shard_map/ppermute | solution.py:31
  94.7 1.4 %collective-permute-done.17 = bf16[2,384,128]{2,1,0:T(8,128)(2,1)S(1)} collective-permute-done((bf16[2,384,128]{2,1,0:T(8,128)(2,1)S(1)}, bf16[2,384,128]{2,1,0:T(8,128)(2,1)S(1)}, u32[]{:S(2)}, u32[]{:S(2)}) %collective-permute-start.17) | collective-permute-done | bytes 196640 | tf_op jit(solution)/shard_map/ppermute | solution.py:31
  96.3 2.0 %collective-permute-done.19 = bf16[2,384,128]{2,1,0:T(8,128)(2,1)S(1)} collective-permute-done((bf16[2,384,128]{2,1,0:T(8,128)(2,1)S(1)}, bf16[2,384,128]{2,1,0:T(8,128)(2,1)S(1)}, u32[]{:S(2)}, u32[]{:S(2)}) %collective-permute-start.19) | collective-permute-done | bytes 196640 | tf_op jit(solution)/shard_map/ppermute | solution.py:31
  98.4 3.1 %collective-permute-done.21 = bf16[512,384]{0,1:T(8,128)(2,1)S(1)} collective-permute-done((bf16[512,384]{0,1:T(8,128)(2,1)S(1)}, bf16[512,384]{0,1:T(8,128)(2,1)S(1)}, u32[]{:S(2)}, u32[]{:S(2)}) %collective-permute-start.21) | collective-permute-done | bytes 393248 | tf_op jit(solution)/shard_map/ppermute | solution.py:31
  101.8 1.6 %collective-permute-start.12 = (bf16[512,384]{0,1:T(8,128)(2,1)S(1)}, bf16[512,384]{0,1:T(8,128)(2,1)S(1)}, u32[]{:S(2)}, u32[]{:S(2)}) collective-permute-start(bf16[512,384]{0,1:T(8,128)(2,1)S(1)} %get-tuple-element.14), channel_id=1, source_target_pairs={{0,2},{1,3},{2,0},{3,1},{4,6},{5,7},{6,4},{7,5},{8,10},{9,11},{10,... | collective-permute-start | bytes 1179656 | tf_op jit(solution)/shard_map/ppermute | solution.py:31
  104.5 6.4 %collective-permute-start.23 = (bf16[512,512]{1,0:T(8,128)(2,1)S(1)}, bf16[512,512]{1,0:T(8,128)(2,1)S(1)}, u32[]{:S(2)}, u32[]{:S(2)}) collective-permute-start(bf16[512,512]{1,0:T(8,128)(2,1)S(1)} %fusion.22), channel_id=1, source_target_pairs={{0,4},{4,0},{8,12},{12,8},{1,5},{5,1},{9,13},{13,9},{2,6},{6,2},{1... | collective-permute-start | bytes 1572872 | tf_op jit(solution)/shard_map/ppermute | solution.py:31
  110.8 2.6 %collective-permute-done.12 = bf16[512,384]{0,1:T(8,128)(2,1)S(1)} collective-permute-done((bf16[512,384]{0,1:T(8,128)(2,1)S(1)}, bf16[512,384]{0,1:T(8,128)(2,1)S(1)}, u32[]{:S(2)}, u32[]{:S(2)}) %collective-permute-start.12) | collective-permute-done | bytes 393248 | tf_op jit(solution)/shard_map/ppermute | solution.py:31
  113.4 1.7 %collective-permute-done.13 = bf16[512,384]{0,1:T(8,128)(2,1)S(1)} collective-permute-done((bf16[512,384]{0,1:T(8,128)(2,1)S(1)}, bf16[512,384]{0,1:T(8,128)(2,1)S(1)}, u32[]{:S(2)}, u32[]{:S(2)}) %collective-permute-start.13) | collective-permute-done | bytes 393248 | tf_op jit(solution)/shard_map/ppermute | solution.py:31
  115.1 8.0 %collective-permute-done.23 = bf16[512,512]{1,0:T(8,128)(2,1)S(1)} collective-permute-done((bf16[512,512]{1,0:T(8,128)(2,1)S(1)}, bf16[512,512]{1,0:T(8,128)(2,1)S(1)}, u32[]{:S(2)}, u32[]{:S(2)}) %collective-permute-start.23) | collective-permute-done | bytes 524320 | tf_op jit(solution)/shard_map/ppermute | solution.py:31
  123.2 1.8 %fusion.19 = bf16[512,512]{1,0:T(8,128)(2,1)} fusion(bf16[512,384]{0,1:T(8,128)(2,1)S(1)} %collective-permute-done.13, bf16[512,384]{0,1:T(8,128)(2,1)S(1)} %collective-permute-done.12, bf16[512,384]{0,1:T(8,128)(2,1)S(1)} %collective-permute-done.11, bf16[512,384]{0,1:T(8,128)(2,1)S(1)} %get-tuple-element.14, ...), kind=kOutput, calls=%fused_computation.21 | convolution fusion | flops 818675712 | bytes 4194304 | tf_op jit(solution)/shard_map/dot_general | solution.py:11
  (61 shorter events, 17.4 us)
Async XLA Ops:
  0.0 4.2 %copy-start.1 = (bf16[512,768]{1,0:T(8,128)(2,1)S(1)}, bf16[512,768]{1,0:T(8,128)(2,1)}, u32[]{:S(2)}) copy-start(bf16[512,768]{1,0:T(8,128)(2,1)} %param.5) | copy-start | bytes 2359300
  0.0 16.1 %collective-permute-start = (bf16[512,512]{1,0:T(8,128)(2,1)}, bf16[512,512]{1,0:T(8,128)(2,1)}, u32[]{:S(2)}, u32[]{:S(2)}) collective-permute-start(bf16[512,512]{1,0:T(8,128)(2,1)} %param.4), channel_id=1, source_target_pairs={{0,4},{4,0},{8,12},{12,8},{1,5},{5,1},{9,13},{13,9},{2,6},{6,2},{1... | collective-permute-start | bytes 1572872 | tf_op jit(solution)/shard_map/ppermute | solution.py:31
  4.9 13.2 %copy-start.2 = (bf16[512,512]{1,0:T(8,128)(2,1)S(1)}, bf16[512,512]{1,0:T(8,128)(2,1)}, u32[]{:S(2)}) copy-start(bf16[512,512]{1,0:T(8,128)(2,1)} %param.4) | copy-start | bytes 1572868
  5.2 31.2 %copy-start.3 = (bf16[512,384]{0,1:T(8,128)(2,1)}, bf16[512,384]{0,1:T(8,128)(2,1)S(1)}, u32[]{:S(2)}) copy-start(bf16[512,384]{0,1:T(8,128)(2,1)S(1)} %get-tuple-element.8) | copy-start | bytes 1179652
  5.3 24.8 %collective-permute-start.5 = (bf16[512,384]{0,1:T(8,128)(2,1)S(1)}, bf16[512,384]{0,1:T(8,128)(2,1)}, u32[]{:S(2)}, u32[]{:S(2)}) collective-permute-start(bf16[512,384]{0,1:T(8,128)(2,1)S(1)} %get-tuple-element.8), channel_id=1, source_target_pairs={{0,4},{4,0},{8,12},{12,8},{1,5},{5,1},{9,13},{13,9},{2,6},{6,2},{1... | collective-permute-start | bytes 1179656 | tf_op jit(solution)/shard_map/ppermute | solution.py:31
  16.1 18.5 %collective-permute-start.2 = (bf16[512,512]{1,0:T(8,128)(2,1)}, bf16[512,512]{1,0:T(8,128)(2,1)}, u32[]{:S(2)}, u32[]{:S(2)}) collective-permute-start(bf16[512,512]{1,0:T(8,128)(2,1)} %collective-permute-done), channel_id=1, source_target_pairs={{0,2},{1,3},{2,0},{3,1},{4,6},{5,7},{6,4},{7,5},{8,10},{9,11},{10,... | collective-permute-start | bytes 1572872 | tf_op jit(solution)/shard_map/ppermute | solution.py:31
  18.1 21.7 %collective-permute-start.3 = (bf16[512,512]{1,0:T(8,128)(2,1)S(1)}, bf16[512,512]{1,0:T(8,128)(2,1)S(1)}, u32[]{:S(2)}, u32[]{:S(2)}) collective-permute-start(bf16[512,512]{1,0:T(8,128)(2,1)S(1)} %copy-done.2), channel_id=1, source_target_pairs={{0,2},{1,3},{2,0},{3,1},{4,6},{5,7},{6,4},{7,5},{8,10},{9,11},{10,... | collective-permute-start | bytes 1572872 | tf_op jit(solution)/shard_map/ppermute | solution.py:31
  18.1 47.4 %collective-permute-start.6 = (bf16[512,384]{0,1:T(8,128)(2,1)S(1)}, bf16[512,384]{0,1:T(8,128)(2,1)}, u32[]{:S(2)}, u32[]{:S(2)}) collective-permute-start(bf16[512,384]{0,1:T(8,128)(2,1)S(1)} %get-tuple-element.20), channel_id=1, source_target_pairs={{0,8},{4,12},{8,0},{12,4},{1,9},{5,13},{9,1},{13,5},{2,10},{6,14},... | collective-permute-start | bytes 1179656 | tf_op jit(solution)/shard_map/ppermute | solution.py:31
  30.0 12.8 %collective-permute-start.8 = (bf16[512,384]{0,1:T(8,128)(2,1)}, bf16[512,384]{0,1:T(8,128)(2,1)}, u32[]{:S(2)}, u32[]{:S(2)}) collective-permute-start(bf16[512,384]{0,1:T(8,128)(2,1)} %collective-permute-done.5), channel_id=1, source_target_pairs={{0,16},{16,0},{1,17},{17,1},{2,18},{18,2},{3,19},{19,3},{4,20},{20... | collective-permute-start | bytes 1179656 | tf_op jit(solution)/shard_map/ppermute | solution.py:31
  34.6 43.8 %collective-permute-start.1 = (bf16[1024,512]{1,0:T(8,128)(2,1)}, bf16[1024,512]{1,0:T(8,128)(2,1)}, u32[]{:S(2)}, u32[]{:S(2)}) collective-permute-start(bf16[1024,512]{1,0:T(8,128)(2,1)} %constant_dynamic-update-slice_fusion), channel_id=1, source_target_pairs={{0,1},{1,0},{2,3},{3,2},{4,5},{5,4},{6,7},{7,6},{8,9},{9,8},{10,11... | collective-permute-start | bytes 3145736 | tf_op jit(solution)/shard_map/ppermute | solution.py:31
  36.5 4.3 %copy-start = (bf16[3072,128]{1,0:T(8,128)(2,1)S(1)}, bf16[3072,128]{1,0:T(8,128)(2,1)}, u32[]{:S(2)}) copy-start(bf16[3072,128]{1,0:T(8,128)(2,1)} %param.7) | copy-start | bytes 2359300
  40.6 39.3 %collective-permute-start.4 = (bf16[1024,512]{1,0:T(8,128)(2,1)}, bf16[1024,512]{1,0:T(8,128)(2,1)}, u32[]{:S(2)}, u32[]{:S(2)}) collective-permute-start(bf16[1024,512]{1,0:T(8,128)(2,1)} %constant_dynamic-update-slice_fusion.2), channel_id=1, source_target_pairs={{0,1},{1,0},{2,3},{3,2},{4,5},{5,4},{6,7},{7,6},{8,9},{9,8},{10,11... | collective-permute-start | bytes 3145736 | tf_op jit(solution)/shard_map/ppermute | solution.py:31
  41.7 4.8 %copy-start.4 = (bf16[512,384]{0,1:T(8,128)(2,1)S(1)}, bf16[512,384]{0,1:T(8,128)(2,1)}, u32[]{:S(2)}) copy-start(bf16[512,384]{0,1:T(8,128)(2,1)} %copy-done.3) | copy-start | bytes 1179652
  42.9 21.3 %collective-permute-start.14 = (bf16[2,384,128]{2,1,0:T(8,128)(2,1)S(1)}, bf16[2,384,128]{2,1,0:T(8,128)(2,1)S(1)}, u32[]{:S(2)}, u32[]{:S(2)}) collective-permute-start(bf16[2,384,128]{2,1,0:T(8,128)(2,1)S(1)} %fusion.56), channel_id=1, source_target_pairs={{0,8},{4,12},{8,0},{12,4},{1,9},{5,13},{9,1},{13,5},{2,10},{6,14},... | collective-permute-start | bytes 589832 | tf_op jit(solution)/shard_map/ppermute | solution.py:31
  46.5 24.7 %collective-permute-start.7 = (bf16[512,384]{0,1:T(8,128)(2,1)S(1)}, bf16[512,384]{0,1:T(8,128)(2,1)S(1)}, u32[]{:S(2)}, u32[]{:S(2)}) collective-permute-start(bf16[512,384]{0,1:T(8,128)(2,1)S(1)} %copy-done.4), channel_id=1, source_target_pairs={{0,12},{4,8},{8,4},{12,0},{1,13},{5,9},{9,5},{13,1},{2,14},{6,10},... | collective-permute-start | bytes 1179656 | tf_op jit(solution)/shard_map/ppermute | solution.py:31
  64.2 6.1 %collective-permute-start.15 = (bf16[2,384,128]{2,1,0:T(8,128)(2,1)S(1)}, bf16[2,384,128]{2,1,0:T(8,128)(2,1)S(1)}, u32[]{:S(2)}, u32[]{:S(2)}) collective-permute-start(bf16[2,384,128]{2,1,0:T(8,128)(2,1)S(1)} %collective-permute-done.14), channel_id=1, source_target_pairs={{0,16},{16,0},{1,17},{17,1},{2,18},{18,2},{3,19},{19,3},{4,20},{20... | collective-permute-start | bytes 589832 | tf_op jit(solution)/shard_map/ppermute | solution.py:31
  65.6 8.5 %collective-permute-start.16 = (bf16[2,384,128]{2,1,0:T(8,128)(2,1)S(1)}, bf16[2,384,128]{2,1,0:T(8,128)(2,1)S(1)}, u32[]{:S(2)}, u32[]{:S(2)}) collective-permute-start(bf16[2,384,128]{2,1,0:T(8,128)(2,1)S(1)} %fusion.55), channel_id=1, source_target_pairs={{0,12},{4,8},{8,4},{12,0},{1,13},{5,9},{9,5},{13,1},{2,14},{6,10},... | collective-permute-start | bytes 589832 | tf_op jit(solution)/shard_map/ppermute | solution.py:31
  70.3 7.6 %collective-permute-start.18 = (bf16[2,384,128]{2,1,0:T(8,128)(2,1)S(1)}, bf16[2,384,128]{2,1,0:T(8,128)(2,1)S(1)}, u32[]{:S(2)}, u32[]{:S(2)}) collective-permute-start(bf16[2,384,128]{2,1,0:T(8,128)(2,1)S(1)} %fusion.55), channel_id=1, source_target_pairs={{0,4},{4,0},{8,12},{12,8},{1,5},{5,1},{9,13},{13,9},{2,6},{6,2},{1... | collective-permute-start | bytes 589832 | tf_op jit(solution)/shard_map/ppermute | solution.py:31
  71.2 17.3 %collective-permute-start.9 = (bf16[512,384]{0,1:T(8,128)(2,1)}, bf16[512,384]{0,1:T(8,128)(2,1)S(1)}, u32[]{:S(2)}, u32[]{:S(2)}) collective-permute-start(bf16[512,384]{0,1:T(8,128)(2,1)} %collective-permute-done.6), channel_id=1, source_target_pairs={{0,16},{16,0},{1,17},{17,1},{2,18},{18,2},{3,19},{19,3},{4,20},{20... | collective-permute-start | bytes 1179656 | tf_op jit(solution)/shard_map/ppermute | solution.py:31
  74.1 17.9 %collective-permute-start.10 = (bf16[512,384]{0,1:T(8,128)(2,1)S(1)}, bf16[512,384]{0,1:T(8,128)(2,1)S(1)}, u32[]{:S(2)}, u32[]{:S(2)}) collective-permute-start(bf16[512,384]{0,1:T(8,128)(2,1)S(1)} %collective-permute-done.7), channel_id=1, source_target_pairs={{0,16},{16,0},{1,17},{17,1},{2,18},{18,2},{3,19},{19,3},{4,20},{20... | collective-permute-start | bytes 1179656 | tf_op jit(solution)/shard_map/ppermute | solution.py:31
  77.9 18.3 %collective-permute-start.17 = (bf16[2,384,128]{2,1,0:T(8,128)(2,1)S(1)}, bf16[2,384,128]{2,1,0:T(8,128)(2,1)S(1)}, u32[]{:S(2)}, u32[]{:S(2)}) collective-permute-start(bf16[2,384,128]{2,1,0:T(8,128)(2,1)S(1)} %collective-permute-done.16), channel_id=1, source_target_pairs={{0,16},{16,0},{1,17},{17,1},{2,18},{18,2},{3,19},{19,3},{4,20},{20... | collective-permute-start | bytes 589832 | tf_op jit(solution)/shard_map/ppermute | solution.py:31
  78.4 19.9 %collective-permute-start.19 = (bf16[2,384,128]{2,1,0:T(8,128)(2,1)S(1)}, bf16[2,384,128]{2,1,0:T(8,128)(2,1)S(1)}, u32[]{:S(2)}, u32[]{:S(2)}) collective-permute-start(bf16[2,384,128]{2,1,0:T(8,128)(2,1)S(1)} %collective-permute-done.18), channel_id=1, source_target_pairs={{0,16},{16,0},{1,17},{17,1},{2,18},{18,2},{3,19},{19,3},{4,20},{20... | collective-permute-start | bytes 589832 | tf_op jit(solution)/shard_map/ppermute | solution.py:31
  93.2 8.3 %collective-permute-start.21 = (bf16[512,384]{0,1:T(8,128)(2,1)S(1)}, bf16[512,384]{0,1:T(8,128)(2,1)S(1)}, u32[]{:S(2)}, u32[]{:S(2)}) collective-permute-start(bf16[512,384]{0,1:T(8,128)(2,1)S(1)} %get-tuple-element.13), channel_id=1, source_target_pairs={{0,2},{1,3},{2,0},{3,1},{4,6},{5,7},{6,4},{7,5},{8,10},{9,11},{10,... | collective-permute-start | bytes 1179656 | tf_op jit(solution)/shard_map/ppermute | solution.py:31
  98.3 5.2 %collective-permute-start.20 = (bf16[512,384]{0,1:T(8,128)(2,1)S(1)}, bf16[512,384]{0,1:T(8,128)(2,1)S(1)}, u32[]{:S(2)}, u32[]{:S(2)}) collective-permute-start(bf16[512,384]{0,1:T(8,128)(2,1)S(1)} %get-tuple-element.13), channel_id=1, source_target_pairs={{0,1},{1,0},{2,3},{3,2},{4,5},{5,4},{6,7},{7,6},{8,9},{9,8},{10,11... | collective-permute-start | bytes 1179656 | tf_op jit(solution)/shard_map/ppermute | solution.py:31
  101.5 2.0 %collective-permute-start.22 = (bf16[512,384]{0,1:T(8,128)(2,1)S(1)}, bf16[512,384]{0,1:T(8,128)(2,1)S(1)}, u32[]{:S(2)}, u32[]{:S(2)}) collective-permute-start(bf16[512,384]{0,1:T(8,128)(2,1)S(1)} %collective-permute-done.21), channel_id=1, source_target_pairs={{0,1},{1,0},{2,3},{3,2},{4,5},{5,4},{6,7},{7,6},{8,9},{9,8},{10,11... | collective-permute-start | bytes 1179656 | tf_op jit(solution)/shard_map/ppermute | solution.py:31
  101.8 11.6 %collective-permute-start.12 = (bf16[512,384]{0,1:T(8,128)(2,1)S(1)}, bf16[512,384]{0,1:T(8,128)(2,1)S(1)}, u32[]{:S(2)}, u32[]{:S(2)}) collective-permute-start(bf16[512,384]{0,1:T(8,128)(2,1)S(1)} %get-tuple-element.14), channel_id=1, source_target_pairs={{0,2},{1,3},{2,0},{3,1},{4,6},{5,7},{6,4},{7,5},{8,10},{9,11},{10,... | collective-permute-start | bytes 1179656 | tf_op jit(solution)/shard_map/ppermute | solution.py:31
  104.5 18.7 %collective-permute-start.23 = (bf16[512,512]{1,0:T(8,128)(2,1)S(1)}, bf16[512,512]{1,0:T(8,128)(2,1)S(1)}, u32[]{:S(2)}, u32[]{:S(2)}) collective-permute-start(bf16[512,512]{1,0:T(8,128)(2,1)S(1)} %fusion.22), channel_id=1, source_target_pairs={{0,4},{4,0},{8,12},{12,8},{1,5},{5,1},{9,13},{13,9},{2,6},{6,2},{1... | collective-permute-start | bytes 1572872 | tf_op jit(solution)/shard_map/ppermute | solution.py:31
  110.8 2.6 %collective-permute-start.11 = (bf16[512,384]{0,1:T(8,128)(2,1)S(1)}, bf16[512,384]{0,1:T(8,128)(2,1)S(1)}, u32[]{:S(2)}, u32[]{:S(2)}) collective-permute-start(bf16[512,384]{0,1:T(8,128)(2,1)S(1)} %get-tuple-element.14), channel_id=1, source_target_pairs={{0,1},{1,0},{2,3},{3,2},{4,5},{5,4},{6,7},{7,6},{8,9},{9,8},{10,11... | collective-permute-start | bytes 1179656 | tf_op jit(solution)/shard_map/ppermute | solution.py:31
  113.4 1.7 %collective-permute-start.13 = (bf16[512,384]{0,1:T(8,128)(2,1)S(1)}, bf16[512,384]{0,1:T(8,128)(2,1)S(1)}, u32[]{:S(2)}, u32[]{:S(2)}) collective-permute-start(bf16[512,384]{0,1:T(8,128)(2,1)S(1)} %collective-permute-done.12), channel_id=1, source_target_pairs={{0,1},{1,0},{2,3},{3,2},{4,5},{5,4},{6,7},{7,6},{8,9},{9,8},{10,11... | collective-permute-start | bytes 1179656 | tf_op jit(solution)/shard_map/ppermute | solution.py:31

commit v2 on v0

v2 whole, which is shorter than its diff:
```python
import functools

import jax
import jax.numpy as jnp
from jax import lax
from jax.experimental import pallas as pl
from jax.experimental.pallas import tpu as pltpu
from jax.sharding import PartitionSpec as P

F32 = jnp.float32
BF16 = jnp.bfloat16
VMEM = pl.BlockSpec(memory_space=pltpu.VMEM)
SMEM = pl.BlockSpec(memory_space=pltpu.SMEM)


def dot(a, b):
    return jnp.dot(a, b, preferred_element_type=F32)


def nothing(token_ref, out_ref):
    del token_ref, out_ref


def span(token, cost):
    return pl.pallas_call(
        nothing,
        out_shape=jax.ShapeDtypeStruct((8, 128), F32),
        in_specs=[pl.BlockSpec(memory_space=pl.ANY)],
        out_specs=pl.BlockSpec(memory_space=pl.ANY),
        input_output_aliases={0: 0},
        cost_estimate=pl.CostEstimate(flops=cost, bytes_accessed=8192, transcendentals=0),
        compiler_params=pltpu.CompilerParams(has_side_effects=True),
    )(token)


def stage(token, *values, cost=5 * 10**8):
    token, *values = lax.optimization_barrier((token, *values))
    return span(token, cost), *values


def hidden_kernel(tile, at_ref, *refs):
    *refs, out_ref = refs
    n = len(refs) // 3
    blocks, direct, swapped = refs[:n], refs[n : 2 * n], refs[2 * n :]
    rows, units = out_ref.shape
    gate_first = at_ref[1] == 1
    for shift in range(n):

        @pl.when(at_ref[0] == shift)
        def _(shift=shift):
            parts = [jnp.concatenate([direct[j][...], swapped[j][...]], axis=1) for j in range(n)]
            weights = jnp.concatenate(parts, axis=0)
            for r in range(0, rows, tile):
                cut = pl.ds(r, tile)
                sums = dot(jnp.concatenate([blocks[shift ^ j][cut, :] for j in range(n)], axis=1), weights)
                a, b = sums[:, :units], sums[:, units:]
                gate, up = jnp.where(gate_first, a, b), jnp.where(gate_first, b, a)
                out_ref[cut, :] = (gate / (1.0 + jnp.exp(-gate)) * up).astype(BF16)


def hidden_of(at, blocks, direct, swapped):
    rows, units = blocks[0].shape[0], direct[0].shape[1]
    return pl.pallas_call(
        functools.partial(hidden_kernel, rows // 2),
        out_shape=jax.ShapeDtypeStruct((rows, units), BF16),
        in_specs=[SMEM] + [VMEM] * (len(blocks) + len(direct) + len(swapped)),
        out_specs=VMEM,
        cost_estimate=pl.CostEstimate(flops=10**6, bytes_accessed=10**4, transcendentals=0),
        compiler_params=pltpu.CompilerParams(vmem_limit_bytes=16 * 2**20),
    )(at, *blocks, *direct, *swapped)


def down_kernel(at_ref, own_ref, *refs):
    *parts, out_ref = refs
    n = len(parts) // 2
    columns = own_ref.shape[2]
    for b in range(own_ref.shape[0]):
        cut = pl.ds(pl.multiple_of(at_ref[1] * columns, columns), columns)
        out_ref[at_ref[0] ^ b, :, cut] = own_ref[b]
        for j in range(1, n + 1):
            cut = pl.ds(pl.multiple_of((at_ref[1] ^ j) * columns, columns), columns)
            value = parts[j - 1][b] if b < 2 else parts[n + j - 1][b - 2]
            out_ref[at_ref[0] ^ at_ref[2] ^ b, :, cut] = value


def gather_down(at, own, direct, swapped):
    blocks, half, columns = own.shape
    return pl.pallas_call(
        down_kernel,
        out_shape=jax.ShapeDtypeStruct((blocks, half, (len(direct) + 1) * columns), BF16),
        in_specs=[SMEM] + [VMEM] * (1 + len(direct) + len(swapped)),
        out_specs=VMEM,
        compiler_params=pltpu.CompilerParams(vmem_limit_bytes=16 * 2**20),
    )(at, own, *direct, *swapped)


def shards(sizes, tokens, gate_weight, up_weight, down_weight):
    n_batch, n_weight = sizes["batch"], sizes["weight"]
    plane = lax.axis_index("batch")
    place = lax.axis_index("weight")
    group = lax.axis_index("groups")
    first = group == 0
    parity = plane % 2
    even = parity == 0
    rows, features = tokens.shape
    depth, units = gate_weight.shape
    half = units // 2
    columns = down_weight.shape[1]

    def flip(x, axis, bits):
        return lax.ppermute(x, axis, [(i, i ^ bits) for i in range(sizes[axis])])

    def half_of(weight, parity):
        return lax.dynamic_slice_in_dim(weight, parity * half, half, axis=1)

    down_blocks = down_weight.reshape(n_weight, 2, half, columns)

    if n_batch == n_weight == 4:
        mine = jnp.where(first, gate_weight, up_weight)
        send_own, send_other = half_of(mine, parity), half_of(mine, 1 - parity)
        keep_own = half_of(jnp.where(first, up_weight, gate_weight), parity)
        low, high = slice(0, n_weight // 2), slice(n_weight // 2, n_weight)
        down_own = jnp.where(even, down_blocks[:, 0], down_blocks[:, 1])
        down_other = jnp.where(even, down_blocks[:, 1], down_blocks[:, 0])
        down_send = {
            j: jnp.where(first, source[low], source[high])
            for j, source in ((1, down_other), (2, down_own), (3, down_other))
        }

        token = jnp.zeros((8, 128), F32)
        tokens_x = flip(tokens, "weight", 2)
        tokens_pair = flip(tokens, "batch", 1)
        direct_2 = flip(send_own, "batch", 2)
        token, tokens_x, send_other = stage(token, tokens_x, send_other)
        direct_1 = flip(send_other, "batch", 1)
        token, tokens_pair, direct_2, send_other = stage(token, tokens_pair, direct_2, send_other)
        direct_3 = flip(send_other, "batch", 3)
        swapped_2 = flip(direct_2, "groups", 1)
        tokens_pair_x = flip(tokens_pair, "weight", 2)
        token, direct_1 = stage(token, direct_1, cost=2 * 10**9)
        swapped_1 = flip(direct_1, "groups", 1)
        token, tokens_pair_x, swapped_2, *own = stage(token, tokens_pair_x, swapped_2, tokens, tokens_x)
        own_core = [flip(x, "weight", 1) for x in own]
        pair_core = [flip(x, "weight", 1) for x in (tokens_pair, tokens_pair_x)]
        token, direct_3, *parts = stage(token, direct_3, down_send[1], down_send[2])
        swapped_3 = flip(direct_3, "groups", 1)
        down_direct = [flip(part, "batch", j) for j, part in zip((1, 2), parts)]
        token, swapped_1, part = stage(token, swapped_1, down_send[3], cost=2 * 10**9)
        down_direct.append(flip(part, "batch", 3))
        token, swapped_3, *cores = stage(token, swapped_3, *own_core, *pair_core)
        own_core, pair_core = cores[:2], cores[2:]
        at = jnp.stack([place ^ plane, jnp.where(first, 1, 0)]).astype(jnp.int32)
        direct = [send_own, direct_1, direct_2, direct_3]
        swapped = [keep_own, swapped_1, swapped_2, swapped_3]
        hidden_pair = hidden_of(at, [tokens_pair, pair_core[0], tokens_pair_x, pair_core[1]], direct, swapped)
        far_pair = flip(hidden_pair, "weight", 2)
        hidden_own = hidden_of(at, [tokens, own_core[0], tokens_x, own_core[1]], direct, swapped)
        token, hidden_own, down_direct[0], down_direct[1] = stage(
            token, hidden_own, down_direct[0], down_direct[1], cost=4 * 10**9
        )
        down_swapped = [flip(x, "groups", 1) for x in down_direct[:2]]
        token, down_direct[2] = stage(token, down_direct[2], cost=4 * 10**9)
        down_swapped.append(flip(down_direct[2], "groups", 1))
        token, far_pair, hidden_pair, hidden_own = stage(token, far_pair, hidden_pair, hidden_own)
        far_own = flip(hidden_own, "weight", 2)
        core_pair = [flip(x, "weight", 1) for x in (hidden_pair, far_pair)]
        token, down_swapped[0], down_swapped[1] = stage(token, down_swapped[0], down_swapped[1], cost=2 * 10**9)
        token, down_swapped[2] = stage(token, down_swapped[2], cost=3 * 10**9)
        at = jnp.stack([place, plane, jnp.where(first, 0, 2)]).astype(jnp.int32)
        down_all = gather_down(at, down_own, down_direct, down_swapped)
        token, *core_pair = stage(token, *core_pair)
    else:
        tokens_pair = flip(tokens, "batch", 1)
        both = lax.all_gather(jnp.concatenate([tokens_pair, tokens], axis=0), "weight", axis=1, tiled=True)
        mine = lax.all_gather(jnp.where(first, gate_weight, up_weight), "batch", axis=0, tiled=True)
        mine = half_of(mine, parity)
        mine, theirs = dot(both, mine), dot(both, flip(mine, "groups", 1))
        gate_sum, up_sum = jnp.where(first, mine, theirs), jnp.where(first, theirs, mine)
        hidden = (jax.nn.silu(gate_sum) * up_sum).astype(BF16)
        hidden_pair, hidden_own = hidden[:rows], hidden[rows:]
        far_pair, far_own = flip(hidden_pair, "weight", 2), flip(hidden_own, "weight", 2)
        core_pair = [flip(x, "weight", 1) for x in (hidden_pair, far_pair)]
        down_all = lax.all_gather(down_weight, "batch", axis=1, tiled=True)
        down_all = down_all.reshape(n_weight, 2, half, n_batch * columns)
        down_all = jnp.where(even, down_all[:, 0], down_all[:, 1])
        down_all = jnp.stack(
            [lax.dynamic_index_in_dim(down_all, place ^ i, 0, keepdims=False) for i in range(n_weight)]
        )

    down_all = down_all.reshape(n_weight * half, n_batch * columns)

    def output_of(hidden, far, core):
        return dot(jnp.concatenate([hidden, core[0], far, core[1]], axis=1), down_all)

    theirs = flip(output_of(hidden_pair, far_pair, core_pair).astype(BF16), "batch", 1)
    core_own = [flip(x, "weight", 1) for x in (hidden_own, far_own)]
    mine, theirs = lax.optimization_barrier((output_of(hidden_own, far_own, core_own), theirs))
    return (mine + theirs).astype(BF16)


def solution(mesh):
    in_specs = (
        P(("groups", "batch"), "weight"),
        P("batch", "weight"),
        P("batch", "weight"),
        P(None, ("weight", "batch")),
    )
    out_specs = P(("groups", "batch"), "weight")
    sizes = dict(mesh.shape)

    def body(*args):
        return shards(sizes, *args)

    return jax.shard_map(body, mesh=mesh, in_specs=in_specs, out_specs=out_specs, check_vma=False)
```

time: 267 us -> 110 us (0.41)
  waiting for transfers between devices: 237 us -> 43.8 us
  starting transfers between devices: 0.15 us -> 39.9 us
  between operations: 13.1 us -> 0.16 us
  matrix products: 16.1 us -> 5.09 us
  Pallas kernels: 0 us -> 8.77 us
  other arithmetic: 0 us -> 6.87 us
  local copies, waits for them, and re-layouts: 0.01 us -> 4.83 us
    all_gather x5 -> x0, waiting for transfers between devices: 235 us -> none  [the longest x1 65.1 us: shards(): lax.all_gather(gate_weight, 'batch', axis=0, tiled=True)]
    ppermute x0 -> x26, waiting for transfers between devices: none -> 43.8 us  [flip(): return lax.ppermute(x, axis, [(i, i ^ bits) for i in range(sizes[axis])])]
    ppermute x0 -> x26, starting transfers between devices: none -> 39.9 us  [flip(): return lax.ppermute(x, axis, [(i, i ^ bits) for i in range(sizes[axis])])]
    dot_general x3 -> x2, matrix products: 16.1 us -> 5.09 us  [dot(): return jnp.dot(a, b, preferred_element_type=F32)]
    pallas_call x0 -> x16, Pallas kernels: none -> 8.77 us  [the longest x2 7.36 us: hidden_of(): pl.pallas_call(functools.partial(hidden_kernel, rows // 2), out_shape=jax...]
    select_n x0 -> x5, other arithmetic: none -> 5.73 us  [the longest x2 2.42 us: shards(): jnp.where(first, source[low], source[high])]
    unnamed x2 -> x16, local copies, waits for them, and re-layouts: 0.01 us -> 3.4 us
  transfers between devices with their start and end apart: 5 -> 26, of which waited for: 5 -> 12; matrix products, arithmetic and copies ran while one was open for 4% -> 11% of each run, Pallas kernels for 0% -> 8%
where the time goes in v2:
time: 110 us; the launch traced here: 109 us
  waiting for transfers between devices  43.8 us (40%)
  starting transfers between devices  39.9 us (36%)
  Pallas kernels  8.77 us (8%)
  other arithmetic  6.87 us (6%)
  matrix products  5.09 us (5%)
  local copies, waits for them, and re-layouts  4.83 us (4%)
    ppermute x26, waiting for transfers between devices, flip(): return lax.ppermute(x, axis, [(i, i ^ bits) for i in range(sizes[axis])])  43.8 us
    ppermute x26, starting transfers between devices, flip(): return lax.ppermute(x, axis, [(i, i ^ bits) for i in range(sizes[axis])])  39.9 us
    pallas_call x2, Pallas kernels, hidden_of(): pl.pallas_call(functools.partial(hidden_kernel, rows // 2), out_shape=jax...  7.36 us
    dot_general x2, matrix products, dot(): return jnp.dot(a, b, preferred_element_type=F32)  5.09 us
    unnamed x16, local copies, waits for them, and re-layouts  3.4 us
    select_n x2, other arithmetic, shards(): jnp.where(first, source[low], source[high])  2.42 us
  transfers between devices with their start and end apart: 26, of which 12 were waited for; matrix products, arithmetic and copies ran while one was open for 11% of the time, Pallas kernels for 8%

profile of v2, /device:TPU:0, one launch (start us, length us, event | category | flops | bytes accessed | tf_op | source)
XLA Modules:
  0.0 109.4 jit_solution(14012225386117680941)
XLA Ops:
  0.0 2.9 %collective-permute-start = (bf16[512,512]{1,0:T(8,128)(2,1)}, bf16[512,512]{1,0:T(8,128)(2,1)S(1)}, u32[]{:S(2)}, u32[]{:S(2)}) collective-permute-start(bf16[512,512]{1,0:T(8,128)(2,1)} %refs_0_.1), channel_id=1, source_target_pairs={{0,2},{1,3},{2,0},{3,1},{4,6},{5,7},{6,4},{7,5},{8,10},{9,11},{10,... | collective-permute-start | bytes 1572872 | tf_op jit(solution)/shard_map/ppermute | solution.py:111
  2.9 1.6 %collective-permute-start.1 = (bf16[512,512]{1,0:T(8,128)(2,1)}, bf16[512,512]{1,0:T(8,128)(2,1)}, u32[]{:S(2)}, u32[]{:S(2)}) collective-permute-start(bf16[512,512]{1,0:T(8,128)(2,1)} %refs_0_.1), channel_id=1, source_target_pairs={{0,4},{4,0},{8,12},{12,8},{1,5},{5,1},{9,13},{13,9},{2,6},{6,2},{1... | collective-permute-start | bytes 1572872 | tf_op jit(solution)/shard_map/ppermute | solution.py:111
  4.5 1.3 %broadcast_select_fusion = bf16[512,768]{1,0:T(8,128)(2,1)S(1)} fusion(bf16[512,768]{1,0:T(8,128)(2,1)} %param.5, bf16[512,768]{1,0:T(8,128)(2,1)} %param.6, pred[]{:T(512)S(6)} %eq.8), kind=kLoop, calls=%fused_computation.18 | loop fusion | flops 393216 | bytes 2359297 | tf_op jit(solution)/shard_map/jit(_where)/select_n | solution.py:119
  6.7 2.6 %collective-permute-start.2 = (bf16[512,384]{1,0:T(8,128)(2,1)S(1)}, bf16[512,384]{1,0:T(8,128)(2,1)S(1)}, u32[]{:S(2)}, u32[]{:S(2)}) collective-permute-start(bf16[512,384]{1,0:T(8,128)(2,1)S(1)} %get-tuple-element.101.refs_4_), channel_id=1, source_target_pairs={{0,8},{4,12},{8,0},{12,4},{1,9},{5,13},{9,1},{13,5},{2,10},{6,14},... | collective-permute-start | bytes 1179656 | tf_op jit(solution)/shard_map/ppermute | solution.py:111
  9.2 5.8 %collective-permute-done.refs_2_ = bf16[512,512]{1,0:T(8,128)(2,1)S(1)} collective-permute-done((bf16[512,512]{1,0:T(8,128)(2,1)}, bf16[512,512]{1,0:T(8,128)(2,1)S(1)}, u32[]{:S(2)}, u32[]{:S(2)}) %collective-permute-start) | collective-permute-done | bytes 524320 | tf_op jit(solution)/shard_map/ppermute | solution.py:111
  15.9 1.8 %collective-permute-start.3 = (bf16[512,384]{1,0:T(8,128)(2,1)}, bf16[512,384]{1,0:T(8,128)(2,1)S(1)}, u32[]{:S(2)}, u32[]{:S(2)}) collective-permute-start(bf16[512,384]{1,0:T(8,128)(2,1)} %get-tuple-element.60), channel_id=1, source_target_pairs={{0,4},{4,0},{8,12},{12,8},{1,5},{5,1},{9,13},{13,9},{2,6},{6,2},{1... | collective-permute-start | bytes 1179656 | tf_op jit(solution)/shard_map/ppermute | solution.py:111
  19.1 6.5 %collective-permute-done.2.refs_6_ = bf16[512,384]{1,0:T(8,128)(2,1)S(1)} collective-permute-done((bf16[512,384]{1,0:T(8,128)(2,1)S(1)}, bf16[512,384]{1,0:T(8,128)(2,1)S(1)}, u32[]{:S(2)}, u32[]{:S(2)}) %collective-permute-start.2) | collective-permute-done | bytes 393248 | tf_op jit(solution)/shard_map/ppermute | solution.py:111
  27.3 2.0 %collective-permute-start.5 = (bf16[512,384]{1,0:T(8,128)(2,1)S(1)}, bf16[512,384]{1,0:T(8,128)(2,1)S(1)}, u32[]{:S(2)}, u32[]{:S(2)}) collective-permute-start(bf16[512,384]{1,0:T(8,128)(2,1)S(1)} %collective-permute-done.2.refs_6_), channel_id=1, source_target_pairs={{0,16},{16,0},{1,17},{17,1},{2,18},{18,2},{3,19},{19,3},{4,20},{20... | collective-permute-start | bytes 1179656 | tf_op jit(solution)/shard_map/ppermute | solution.py:111
  29.3 3.6 %collective-permute-start.6 = (bf16[512,384]{1,0:T(8,128)(2,1)}, bf16[512,384]{1,0:T(8,128)(2,1)S(1)}, u32[]{:S(2)}, u32[]{:S(2)}) collective-permute-start(bf16[512,384]{1,0:T(8,128)(2,1)} %get-tuple-element.60), channel_id=1, source_target_pairs={{0,12},{4,8},{8,4},{12,0},{1,13},{5,9},{9,5},{13,1},{2,14},{6,10},... | collective-permute-start | bytes 1179656 | tf_op jit(solution)/shard_map/ppermute | solution.py:111
  32.9 1.2 %collective-permute-done.3.refs_5_ = bf16[512,384]{1,0:T(8,128)(2,1)S(1)} collective-permute-done((bf16[512,384]{1,0:T(8,128)(2,1)}, bf16[512,384]{1,0:T(8,128)(2,1)S(1)}, u32[]{:S(2)}, u32[]{:S(2)}) %collective-permute-start.3) | collective-permute-done | bytes 393248 | tf_op jit(solution)/shard_map/ppermute | solution.py:111
  34.1 1.5 %collective-permute-start.7 = (bf16[512,384]{1,0:T(8,128)(2,1)S(1)}, bf16[512,384]{1,0:T(8,128)(2,1)S(1)}, u32[]{:S(2)}, u32[]{:S(2)}) collective-permute-start(bf16[512,384]{1,0:T(8,128)(2,1)S(1)} %collective-permute-done.3.refs_5_), channel_id=1, source_target_pairs={{0,16},{16,0},{1,17},{17,1},{2,18},{18,2},{3,19},{19,3},{4,20},{20... | collective-permute-start | bytes 1179656 | tf_op jit(solution)/shard_map/ppermute | solution.py:111
  35.6 1.7 %fusion.20 = bf16[2,384,128]{2,1,0:T(8,128)(2,1)} fusion(bf16[4,1,384,128]{3,2,0,1:T(8,128)(2,1)} %get-tuple-element.100, pred[]{:T(512)S(6)} %eq.8), kind=kLoop, calls=%fused_computation.27 | loop fusion | flops 98304 | bytes 589825 | tf_op jit(solution)/shard_map/jit(_where)/select_n | solution.py:126
  38.6 5.4 %collective-permute-done.6.refs_7_ = bf16[512,384]{1,0:T(8,128)(2,1)S(1)} collective-permute-done((bf16[512,384]{1,0:T(8,128)(2,1)}, bf16[512,384]{1,0:T(8,128)(2,1)S(1)}, u32[]{:S(2)}, u32[]{:S(2)}) %collective-permute-start.6) | collective-permute-done | bytes 393248 | tf_op jit(solution)/shard_map/ppermute | solution.py:111
  43.9 1.5 %collective-permute-start.8 = (bf16[512,384]{1,0:T(8,128)(2,1)S(1)}, bf16[512,384]{1,0:T(8,128)(2,1)S(1)}, u32[]{:S(2)}, u32[]{:S(2)}) collective-permute-start(bf16[512,384]{1,0:T(8,128)(2,1)S(1)} %collective-permute-done.6.refs_7_), channel_id=1, source_target_pairs={{0,16},{16,0},{1,17},{17,1},{2,18},{18,2},{3,19},{19,3},{4,20},{20... | collective-permute-start | bytes 1179656 | tf_op jit(solution)/shard_map/ppermute | solution.py:111
  46.1 1.2 %dynamic-slice_select_fusion.refs_8_ = bf16[512,384]{1,0:T(8,128)(2,1)S(1)} fusion(bf16[512,768]{1,0:T(8,128)(2,1)} %param.5, s32[]{:T(128)S(6)} %select_n.72, bf16[512,768]{1,0:T(8,128)(2,1)} %param.6, pred[]{:T(512)S(6)} %eq.8), kind=kLoop, calls=%fused_computation.19 | loop fusion | flops 196608 | bytes 1179653 | tf_op jit(solution)/shard_map/jit(_where)/select_n | solution.py:121
  47.4 3.3 %collective-permute-start.13 = (bf16[2,384,128]{2,1,0:T(8,128)(2,1)}, bf16[2,384,128]{2,1,0:T(8,128)(2,1)}, u32[]{:S(2)}, u32[]{:S(2)}) collective-permute-start(bf16[2,384,128]{2,1,0:T(8,128)(2,1)} %fusion.20), channel_id=1, source_target_pairs={{0,4},{4,0},{8,12},{12,8},{1,5},{5,1},{9,13},{13,9},{2,6},{6,2},{1... | collective-permute-start | bytes 589832 | tf_op jit(solution)/shard_map/ppermute | solution.py:111
  50.7 2.9 %collective-permute-done.8.refs_11_ = bf16[512,384]{1,0:T(8,128)(2,1)S(1)} collective-permute-done((bf16[512,384]{1,0:T(8,128)(2,1)S(1)}, bf16[512,384]{1,0:T(8,128)(2,1)S(1)}, u32[]{:S(2)}, u32[]{:S(2)}) %collective-permute-start.8) | collective-permute-done | bytes 393248 | tf_op jit(solution)/shard_map/ppermute | solution.py:111
  53.5 2.3 %collective-permute-start.14 = (bf16[2,384,128]{2,1,0:T(8,128)(2,1)}, bf16[2,384,128]{2,1,0:T(8,128)(2,1)}, u32[]{:S(2)}, u32[]{:S(2)}) collective-permute-start(bf16[2,384,128]{2,1,0:T(8,128)(2,1)} %fusion.19), channel_id=1, source_target_pairs={{0,8},{4,12},{8,0},{12,4},{1,9},{5,13},{9,1},{13,5},{2,10},{6,14},... | collective-permute-start | bytes 589832 | tf_op jit(solution)/shard_map/ppermute | solution.py:111
  55.8 5.9 %collective-permute-start.15 = (bf16[2,384,128]{2,1,0:T(8,128)(2,1)}, bf16[2,384,128]{2,1,0:T(8,128)(2,1)}, u32[]{:S(2)}, u32[]{:S(2)}) collective-permute-start(bf16[2,384,128]{2,1,0:T(8,128)(2,1)} %fusion.20), channel_id=1, source_target_pairs={{0,12},{4,8},{8,4},{12,0},{1,13},{5,9},{9,5},{13,1},{2,14},{6,10},... | collective-permute-start | bytes 589832 | tf_op jit(solution)/shard_map/ppermute | solution.py:111
  62.8 4.0 %shard_map.56 = bf16[512,384]{1,0:T(8,128)(2,1)} custom-call(s32[2]{0:T(128)S(1)} %pad_add_fusion.at_ref, bf16[512,512]{1,0:T(8,128)(2,1)} %collective-permute-done.1.refs_0_, bf16[512,512]{1,0:T(8,128)(2,1)} %collective-permute-done.11.refs_1_, bf16[512,512]{1,0:T(8,128)(2,1)S(1)} %copy-done.4, bf16[512,512]{1,0:T(8,128)(2,1)} %collective-permute-done.12.refs_3_, ...), custom_call_target="tpu_custom_call" | custom-call | flops 1000000 | bytes 10000 | tf_op jit(solution)/shard_map/pallas_call | solution.py:63
  67.3 3.3 %shard_map.53 = bf16[512,384]{1,0:T(8,128)(2,1)S(1)} custom-call(s32[2]{0:T(128)S(1)} %pad_add_fusion.at_ref, bf16[512,512]{1,0:T(8,128)(2,1)S(1)} %copy-done, bf16[512,512]{1,0:T(8,128)(2,1)} %collective-permute-done.9.refs_1_, bf16[512,512]{1,0:T(8,128)(2,1)S(1)} %copy-done.2, bf16[512,512]{1,0:T(8,128)(2,1)} %collective-permute-done.10.refs_3_, ...), custom_call_target="tpu_custom_call" | custom-call | flops 1000000 | bytes 10000 | tf_op jit(solution)/shard_map/pallas_call | solution.py:63
  71.5 1.6 %collective-permute-start.17 = (bf16[2,384,128]{2,1,0:T(8,128)(2,1)}, bf16[2,384,128]{2,1,0:T(8,128)(2,1)S(1)}, u32[]{:S(2)}, u32[]{:S(2)}) collective-permute-start(bf16[2,384,128]{2,1,0:T(8,128)(2,1)} %collective-permute-done.13.refs_0_), channel_id=1, source_target_pairs={{0,16},{16,0},{1,17},{17,1},{2,18},{18,2},{3,19},{19,3},{4,20},{20... | collective-permute-start | bytes 589832 | tf_op jit(solution)/shard_map/ppermute | solution.py:111
  73.5 1.5 %collective-permute-start.19 = (bf16[2,384,128]{2,1,0:T(8,128)(2,1)}, bf16[2,384,128]{2,1,0:T(8,128)(2,1)S(1)}, u32[]{:S(2)}, u32[]{:S(2)}) collective-permute-start(bf16[2,384,128]{2,1,0:T(8,128)(2,1)} %collective-permute-done.15.refs_2_), channel_id=1, source_target_pairs={{0,16},{16,0},{1,17},{17,1},{2,18},{18,2},{3,19},{19,3},{4,20},{20... | collective-permute-start | bytes 589832 | tf_op jit(solution)/shard_map/ppermute | solution.py:111
  75.1 2.5 %collective-permute-done.16 = bf16[512,384]{1,0:T(8,128)(2,1)} collective-permute-done((bf16[512,384]{1,0:T(8,128)(2,1)}, bf16[512,384]{1,0:T(8,128)(2,1)}, u32[]{:S(2)}, u32[]{:S(2)}) %collective-permute-start.16) | collective-permute-done | bytes 393248 | tf_op jit(solution)/shard_map/ppermute | solution.py:111
  78.1 1.5 %collective-permute-done.17.refs_3_ = bf16[2,384,128]{2,1,0:T(8,128)(2,1)S(1)} collective-permute-done((bf16[2,384,128]{2,1,0:T(8,128)(2,1)}, bf16[2,384,128]{2,1,0:T(8,128)(2,1)S(1)}, u32[]{:S(2)}, u32[]{:S(2)}) %collective-permute-start.17) | collective-permute-done | bytes 196640 | tf_op jit(solution)/shard_map/ppermute | solution.py:111
  79.6 4.2 %collective-permute-done.18.refs_4_ = bf16[2,384,128]{2,1,0:T(8,128)(2,1)S(1)} collective-permute-done((bf16[2,384,128]{2,1,0:T(8,128)(2,1)}, bf16[2,384,128]{2,1,0:T(8,128)(2,1)S(1)}, u32[]{:S(2)}, u32[]{:S(2)}) %collective-permute-start.18) | collective-permute-done | bytes 196640 | tf_op jit(solution)/shard_map/ppermute | solution.py:111
  84.3 1.8 %collective-permute-done.19.refs_5_ = bf16[2,384,128]{2,1,0:T(8,128)(2,1)S(1)} collective-permute-done((bf16[2,384,128]{2,1,0:T(8,128)(2,1)}, bf16[2,384,128]{2,1,0:T(8,128)(2,1)S(1)}, u32[]{:S(2)}, u32[]{:S(2)}) %collective-permute-start.19) | collective-permute-done | bytes 196640 | tf_op jit(solution)/shard_map/ppermute | solution.py:111
  86.1 1.4 %shard_map.61 = bf16[4,384,512]{2,1,0:T(8,128)(2,1)S(1)} custom-call(s32[3]{0:T(128)S(1)} %pad_add_fusion.1.at_ref, bf16[4,384,128]{2,1,0:T(8,128)(2,1)S(1)} %bitcast.26, bf16[2,384,128]{2,1,0:T(8,128)(2,1)} %collective-permute-done.13.refs_0_, bf16[2,384,128]{2,1,0:T(8,128)(2,1)} %collective-permute-done.14.refs_1_, ...), custom_call_target="tpu_custom_call" | custom-call | tf_op jit(solution)/shard_map/pallas_call | solution.py:88
  87.6 3.0 %fusion.16 = bf16[512,512]{1,0:T(8,128)(2,1)} fusion(bf16[1536,512]{1,0:T(8,128)(2,1)S(1)} %bitcast.27, bf16[512,384]{1,0:T(8,128)(2,1)} %collective-permute-done.21, bf16[512,384]{1,0:T(8,128)(2,1)} %collective-permute-done.16, bf16[512,384]{1,0:T(8,128)(2,1)S(1)} %collective-permute-done.20, bf16[512,384]{1,0:T(8,128)(2,1)} %shard_map.56), kind=kOutput, calls=%fused_computation.16 | convolution fusion | flops 811859968 | bytes 3670016 | tf_op jit(solution)/shard_map/dot_general | solution.py:17
  90.6 5.1 %collective-permute-start.25 = (bf16[512,512]{1,0:T(8,128)(2,1)}, bf16[512,512]{1,0:T(8,128)(2,1)S(1)}, u32[]{:S(2)}, u32[]{:S(2)}) collective-permute-start(bf16[512,512]{1,0:T(8,128)(2,1)} %fusion.16), channel_id=1, source_target_pairs={{0,4},{4,0},{8,12},{12,8},{1,5},{5,1},{9,13},{13,9},{2,6},{6,2},{1... | collective-permute-start | bytes 1572872 | tf_op jit(solution)/shard_map/ppermute | solution.py:111
  95.7 2.1 %fusion = f32[512,512]{1,0:T(8,128)S(1)} fusion(bf16[1536,512]{1,0:T(8,128)(2,1)S(1)} %bitcast.28, bf16[512,384]{1,0:T(8,128)(2,1)S(1)} %collective-permute-done.24, bf16[512,384]{1,0:T(8,128)(2,1)} %collective-permute-done.23, bf16[512,384]{1,0:T(8,128)(2,1)} %collective-permute-done.22, bf16[512,384]{1,0:T(8,128)(2,1)S(1)} %copy-done.6), kind=kOutput, calls=%fused_computation | convolution fusion | flops 811597824 | bytes 4194304 | tf_op jit(solution)/shard_map/dot_general | solution.py:17
  97.8 10.7 %collective-permute-done.25 = bf16[512,512]{1,0:T(8,128)(2,1)S(1)} collective-permute-done((bf16[512,512]{1,0:T(8,128)(2,1)}, bf16[512,512]{1,0:T(8,128)(2,1)S(1)}, u32[]{:S(2)}, u32[]{:S(2)}) %collective-permute-start.25) | collective-permute-done | bytes 524320 | tf_op jit(solution)/shard_map/ppermute | solution.py:111
  (64 shorter events, 11.7 us)
Async XLA Ops:
  0.0 15.1 %collective-permute-start = (bf16[512,512]{1,0:T(8,128)(2,1)}, bf16[512,512]{1,0:T(8,128)(2,1)S(1)}, u32[]{:S(2)}, u32[]{:S(2)}) collective-permute-start(bf16[512,512]{1,0:T(8,128)(2,1)} %refs_0_.1), channel_id=1, source_target_pairs={{0,2},{1,3},{2,0},{3,1},{4,6},{5,7},{6,4},{7,5},{8,10},{9,11},{10,... | collective-permute-start | bytes 1572872 | tf_op jit(solution)/shard_map/ppermute | solution.py:111
  2.9 23.6 %collective-permute-start.1 = (bf16[512,512]{1,0:T(8,128)(2,1)}, bf16[512,512]{1,0:T(8,128)(2,1)}, u32[]{:S(2)}, u32[]{:S(2)}) collective-permute-start(bf16[512,512]{1,0:T(8,128)(2,1)} %refs_0_.1), channel_id=1, source_target_pairs={{0,4},{4,0},{8,12},{12,8},{1,5},{5,1},{9,13},{13,9},{2,6},{6,2},{1... | collective-permute-start | bytes 1572872 | tf_op jit(solution)/shard_map/ppermute | solution.py:111
  4.5 13.2 %copy-start.7 = (bf16[3072,128]{1,0:T(8,128)(2,1)S(1)}, bf16[3072,128]{1,0:T(8,128)(2,1)}, u32[]{:S(2)}) copy-start(bf16[3072,128]{1,0:T(8,128)(2,1)} %param.7) | copy-start | bytes 2359300
  6.7 18.9 %collective-permute-start.2 = (bf16[512,384]{1,0:T(8,128)(2,1)S(1)}, bf16[512,384]{1,0:T(8,128)(2,1)S(1)}, u32[]{:S(2)}, u32[]{:S(2)}) collective-permute-start(bf16[512,384]{1,0:T(8,128)(2,1)S(1)} %get-tuple-element.101.refs_4_), channel_id=1, source_target_pairs={{0,8},{4,12},{8,0},{12,4},{1,9},{5,13},{9,1},{13,5},{2,10},{6,14},... | collective-permute-start | bytes 1179656 | tf_op jit(solution)/shard_map/ppermute | solution.py:111
  15.9 18.2 %collective-permute-start.3 = (bf16[512,384]{1,0:T(8,128)(2,1)}, bf16[512,384]{1,0:T(8,128)(2,1)S(1)}, u32[]{:S(2)}, u32[]{:S(2)}) collective-permute-start(bf16[512,384]{1,0:T(8,128)(2,1)} %get-tuple-element.60), channel_id=1, source_target_pairs={{0,4},{4,0},{8,12},{12,8},{1,5},{5,1},{9,13},{13,9},{2,6},{6,2},{1... | collective-permute-start | bytes 1179656 | tf_op jit(solution)/shard_map/ppermute | solution.py:111
  26.5 11.2 %collective-permute-start.4 = (bf16[512,512]{1,0:T(8,128)(2,1)}, bf16[512,512]{1,0:T(8,128)(2,1)S(1)}, u32[]{:S(2)}, u32[]{:S(2)}) collective-permute-start(bf16[512,512]{1,0:T(8,128)(2,1)} %collective-permute-done.1.refs_0_), channel_id=1, source_target_pairs={{0,2},{1,3},{2,0},{3,1},{4,6},{5,7},{6,4},{7,5},{8,10},{9,11},{10,... | collective-permute-start | bytes 1572872 | tf_op jit(solution)/shard_map/ppermute | solution.py:111
  27.3 10.0 %collective-permute-start.5 = (bf16[512,384]{1,0:T(8,128)(2,1)S(1)}, bf16[512,384]{1,0:T(8,128)(2,1)S(1)}, u32[]{:S(2)}, u32[]{:S(2)}) collective-permute-start(bf16[512,384]{1,0:T(8,128)(2,1)S(1)} %collective-permute-done.2.refs_6_), channel_id=1, source_target_pairs={{0,16},{16,0},{1,17},{17,1},{2,18},{18,2},{3,19},{19,3},{4,20},{20... | collective-permute-start | bytes 1179656 | tf_op jit(solution)/shard_map/ppermute | solution.py:111
  29.3 14.7 %collective-permute-start.6 = (bf16[512,384]{1,0:T(8,128)(2,1)}, bf16[512,384]{1,0:T(8,128)(2,1)S(1)}, u32[]{:S(2)}, u32[]{:S(2)}) collective-permute-start(bf16[512,384]{1,0:T(8,128)(2,1)} %get-tuple-element.60), channel_id=1, source_target_pairs={{0,12},{4,8},{8,4},{12,0},{1,13},{5,9},{9,5},{13,1},{2,14},{6,10},... | collective-permute-start | bytes 1179656 | tf_op jit(solution)/shard_map/ppermute | solution.py:111
  34.1 11.9 %collective-permute-start.7 = (bf16[512,384]{1,0:T(8,128)(2,1)S(1)}, bf16[512,384]{1,0:T(8,128)(2,1)S(1)}, u32[]{:S(2)}, u32[]{:S(2)}) collective-permute-start(bf16[512,384]{1,0:T(8,128)(2,1)S(1)} %collective-permute-done.3.refs_5_), channel_id=1, source_target_pairs={{0,16},{16,0},{1,17},{17,1},{2,18},{18,2},{3,19},{19,3},{4,20},{20... | collective-permute-start | bytes 1179656 | tf_op jit(solution)/shard_map/ppermute | solution.py:111
  37.3 10.0 %collective-permute-start.11 = (bf16[512,512]{1,0:T(8,128)(2,1)}, bf16[512,512]{1,0:T(8,128)(2,1)}, u32[]{:S(2)}, u32[]{:S(2)}) collective-permute-start(bf16[512,512]{1,0:T(8,128)(2,1)} %collective-permute-done.1.refs_0_), channel_id=1, source_target_pairs={{0,1},{1,0},{2,3},{3,2},{4,5},{5,4},{6,7},{7,6},{8,9},{9,8},{10,11... | collective-permute-start | bytes 1572872 | tf_op jit(solution)/shard_map/ppermute | solution.py:111
  37.8 0.8 copy-start.3
  43.9 9.6 %collective-permute-start.8 = (bf16[512,384]{1,0:T(8,128)(2,1)S(1)}, bf16[512,384]{1,0:T(8,128)(2,1)S(1)}, u32[]{:S(2)}, u32[]{:S(2)}) collective-permute-start(bf16[512,384]{1,0:T(8,128)(2,1)S(1)} %collective-permute-done.6.refs_7_), channel_id=1, source_target_pairs={{0,16},{16,0},{1,17},{17,1},{2,18},{18,2},{3,19},{19,3},{4,20},{20... | collective-permute-start | bytes 1179656 | tf_op jit(solution)/shard_map/ppermute | solution.py:111
  45.5 10.4 %collective-permute-start.10 = (bf16[512,512]{1,0:T(8,128)(2,1)}, bf16[512,512]{1,0:T(8,128)(2,1)}, u32[]{:S(2)}, u32[]{:S(2)}) collective-permute-start(bf16[512,512]{1,0:T(8,128)(2,1)} %copy-done.1), channel_id=1, source_target_pairs={{0,1},{1,0},{2,3},{3,2},{4,5},{5,4},{6,7},{7,6},{8,9},{9,8},{10,11... | collective-permute-start | bytes 1572872 | tf_op jit(solution)/shard_map/ppermute | solution.py:111
  45.5 16.2 %collective-permute-start.12 = (bf16[512,512]{1,0:T(8,128)(2,1)}, bf16[512,512]{1,0:T(8,128)(2,1)}, u32[]{:S(2)}, u32[]{:S(2)}) collective-permute-start(bf16[512,512]{1,0:T(8,128)(2,1)} %copy-done.3), channel_id=1, source_target_pairs={{0,1},{1,0},{2,3},{3,2},{4,5},{5,4},{6,7},{7,6},{8,9},{9,8},{10,11... | collective-permute-start | bytes 1572872 | tf_op jit(solution)/shard_map/ppermute | solution.py:111
  46.0 15.7 %collective-permute-start.9 = (bf16[512,512]{1,0:T(8,128)(2,1)}, bf16[512,512]{1,0:T(8,128)(2,1)}, u32[]{:S(2)}, u32[]{:S(2)}) collective-permute-start(bf16[512,512]{1,0:T(8,128)(2,1)} %refs_0_.1), channel_id=1, source_target_pairs={{0,1},{1,0},{2,3},{3,2},{4,5},{5,4},{6,7},{7,6},{8,9},{9,8},{10,11... | collective-permute-start | bytes 1572872 | tf_op jit(solution)/shard_map/ppermute | solution.py:111
  47.4 24.1 %collective-permute-start.13 = (bf16[2,384,128]{2,1,0:T(8,128)(2,1)}, bf16[2,384,128]{2,1,0:T(8,128)(2,1)}, u32[]{:S(2)}, u32[]{:S(2)}) collective-permute-start(bf16[2,384,128]{2,1,0:T(8,128)(2,1)} %fusion.20), channel_id=1, source_target_pairs={{0,4},{4,0},{8,12},{12,8},{1,5},{5,1},{9,13},{13,9},{2,6},{6,2},{1... | collective-permute-start | bytes 589832 | tf_op jit(solution)/shard_map/ppermute | solution.py:111
  53.5 17.9 %collective-permute-start.14 = (bf16[2,384,128]{2,1,0:T(8,128)(2,1)}, bf16[2,384,128]{2,1,0:T(8,128)(2,1)}, u32[]{:S(2)}, u32[]{:S(2)}) collective-permute-start(bf16[2,384,128]{2,1,0:T(8,128)(2,1)} %fusion.19), channel_id=1, source_target_pairs={{0,8},{4,12},{8,0},{12,4},{1,9},{5,13},{9,1},{13,5},{2,10},{6,14},... | collective-permute-start | bytes 589832 | tf_op jit(solution)/shard_map/ppermute | solution.py:111
  55.8 11.5 %copy-start = (bf16[512,512]{1,0:T(8,128)(2,1)S(1)}, bf16[512,512]{1,0:T(8,128)(2,1)}, u32[]{:S(2)}) copy-start(bf16[512,512]{1,0:T(8,128)(2,1)} %refs_0_.1) | copy-start | bytes 1572868
  55.8 11.5 %copy-start.2 = (bf16[512,512]{1,0:T(8,128)(2,1)S(1)}, bf16[512,512]{1,0:T(8,128)(2,1)}, u32[]{:S(2)}) copy-start(bf16[512,512]{1,0:T(8,128)(2,1)} %copy-done.1) | copy-start | bytes 1572868
  55.8 15.6 %collective-permute-start.15 = (bf16[2,384,128]{2,1,0:T(8,128)(2,1)}, bf16[2,384,128]{2,1,0:T(8,128)(2,1)}, u32[]{:S(2)}, u32[]{:S(2)}) collective-permute-start(bf16[2,384,128]{2,1,0:T(8,128)(2,1)} %fusion.20), channel_id=1, source_target_pairs={{0,12},{4,8},{8,4},{12,0},{1,13},{5,9},{9,5},{13,1},{2,14},{6,10},... | collective-permute-start | bytes 589832 | tf_op jit(solution)/shard_map/ppermute | solution.py:111
  61.7 1.0 copy-start.4
  66.8 10.7 %collective-permute-start.16 = (bf16[512,384]{1,0:T(8,128)(2,1)}, bf16[512,384]{1,0:T(8,128)(2,1)}, u32[]{:S(2)}, u32[]{:S(2)}) collective-permute-start(bf16[512,384]{1,0:T(8,128)(2,1)} %shard_map.56), channel_id=1, source_target_pairs={{0,2},{1,3},{2,0},{3,1},{4,6},{5,7},{6,4},{7,5},{8,10},{9,11},{10,... | collective-permute-start | bytes 1179656 | tf_op jit(solution)/shard_map/ppermute | solution.py:111
  71.4 6.1 %copy-start.6 = (bf16[512,384]{1,0:T(8,128)(2,1)S(1)}, bf16[512,384]{1,0:T(8,128)(2,1)}, u32[]{:S(2)}) copy-start(bf16[512,384]{1,0:T(8,128)(2,1)} %copy-done.5) | copy-start | bytes 1179652
  71.5 8.1 %collective-permute-start.17 = (bf16[2,384,128]{2,1,0:T(8,128)(2,1)}, bf16[2,384,128]{2,1,0:T(8,128)(2,1)S(1)}, u32[]{:S(2)}, u32[]{:S(2)}) collective-permute-start(bf16[2,384,128]{2,1,0:T(8,128)(2,1)} %collective-permute-done.13.refs_0_), channel_id=1, source_target_pairs={{0,16},{16,0},{1,17},{17,1},{2,18},{18,2},{3,19},{19,3},{4,20},{20... | collective-permute-start | bytes 589832 | tf_op jit(solution)/shard_map/ppermute | solution.py:111
  73.0 10.7 %collective-permute-start.18 = (bf16[2,384,128]{2,1,0:T(8,128)(2,1)}, bf16[2,384,128]{2,1,0:T(8,128)(2,1)S(1)}, u32[]{:S(2)}, u32[]{:S(2)}) collective-permute-start(bf16[2,384,128]{2,1,0:T(8,128)(2,1)} %collective-permute-done.14.refs_1_), channel_id=1, source_target_pairs={{0,16},{16,0},{1,17},{17,1},{2,18},{18,2},{3,19},{19,3},{4,20},{20... | collective-permute-start | bytes 589832 | tf_op jit(solution)/shard_map/ppermute | solution.py:111
  73.5 12.5 %collective-permute-start.19 = (bf16[2,384,128]{2,1,0:T(8,128)(2,1)}, bf16[2,384,128]{2,1,0:T(8,128)(2,1)S(1)}, u32[]{:S(2)}, u32[]{:S(2)}) collective-permute-start(bf16[2,384,128]{2,1,0:T(8,128)(2,1)} %collective-permute-done.15.refs_2_), channel_id=1, source_target_pairs={{0,16},{16,0},{1,17},{17,1},{2,18},{18,2},{3,19},{19,3},{4,20},{20... | collective-permute-start | bytes 589832 | tf_op jit(solution)/shard_map/ppermute | solution.py:111
  77.5 10.0 %collective-permute-start.23 = (bf16[512,384]{1,0:T(8,128)(2,1)S(1)}, bf16[512,384]{1,0:T(8,128)(2,1)}, u32[]{:S(2)}, u32[]{:S(2)}) collective-permute-start(bf16[512,384]{1,0:T(8,128)(2,1)S(1)} %copy-done.6), channel_id=1, source_target_pairs={{0,2},{1,3},{2,0},{3,1},{4,6},{5,7},{6,4},{7,5},{8,10},{9,11},{10,... | collective-permute-start | bytes 1179656 | tf_op jit(solution)/shard_map/ppermute | solution.py:111
  78.1 17.6 %collective-permute-start.22 = (bf16[512,384]{1,0:T(8,128)(2,1)S(1)}, bf16[512,384]{1,0:T(8,128)(2,1)}, u32[]{:S(2)}, u32[]{:S(2)}) collective-permute-start(bf16[512,384]{1,0:T(8,128)(2,1)S(1)} %copy-done.6), channel_id=1, source_target_pairs={{0,1},{1,0},{2,3},{3,2},{4,5},{5,4},{6,7},{7,6},{8,9},{9,8},{10,11... | collective-permute-start | bytes 1179656 | tf_op jit(solution)/shard_map/ppermute | solution.py:111
  83.8 3.7 %collective-permute-start.20 = (bf16[512,384]{1,0:T(8,128)(2,1)}, bf16[512,384]{1,0:T(8,128)(2,1)S(1)}, u32[]{:S(2)}, u32[]{:S(2)}) collective-permute-start(bf16[512,384]{1,0:T(8,128)(2,1)} %shard_map.56), channel_id=1, source_target_pairs={{0,1},{1,0},{2,3},{3,2},{4,5},{5,4},{6,7},{7,6},{8,9},{9,8},{10,11... | collective-permute-start | bytes 1179656 | tf_op jit(solution)/shard_map/ppermute | solution.py:111
  83.8 3.7 %collective-permute-start.21 = (bf16[512,384]{1,0:T(8,128)(2,1)}, bf16[512,384]{1,0:T(8,128)(2,1)}, u32[]{:S(2)}, u32[]{:S(2)}) collective-permute-start(bf16[512,384]{1,0:T(8,128)(2,1)} %collective-permute-done.16), channel_id=1, source_target_pairs={{0,1},{1,0},{2,3},{3,2},{4,5},{5,4},{6,7},{7,6},{8,9},{9,8},{10,11... | collective-permute-start | bytes 1179656 | tf_op jit(solution)/shard_map/ppermute | solution.py:111
  87.5 8.1 %collective-permute-start.24 = (bf16[512,384]{1,0:T(8,128)(2,1)}, bf16[512,384]{1,0:T(8,128)(2,1)S(1)}, u32[]{:S(2)}, u32[]{:S(2)}) collective-permute-start(bf16[512,384]{1,0:T(8,128)(2,1)} %collective-permute-done.23), channel_id=1, source_target_pairs={{0,1},{1,0},{2,3},{3,2},{4,5},{5,4},{6,7},{7,6},{8,9},{9,8},{10,11... | collective-permute-start | bytes 1179656 | tf_op jit(solution)/shard_map/ppermute | solution.py:111
  90.6 17.8 %collective-permute-start.25 = (bf16[512,512]{1,0:T(8,128)(2,1)}, bf16[512,512]{1,0:T(8,128)(2,1)S(1)}, u32[]{:S(2)}, u32[]{:S(2)}) collective-permute-start(bf16[512,512]{1,0:T(8,128)(2,1)} %fusion.16), channel_id=1, source_target_pairs={{0,4},{4,0},{8,12},{12,8},{1,5},{5,1},{9,13},{13,9},{2,6},{6,2},{1... | collective-permute-start | bytes 1572872 | tf_op jit(solution)/shard_map/ppermute | solution.py:111
  (2 other events, 1.5 us)

commit v3 on v2

v3 whole, which is shorter than its diff:
```python
import functools

import jax
import jax.numpy as jnp
from jax import lax
from jax.experimental import pallas as pl
from jax.experimental.pallas import tpu as pltpu
from jax.sharding import PartitionSpec as P

F32 = jnp.float32
BF16 = jnp.bfloat16
VMEM = pl.BlockSpec(memory_space=pltpu.VMEM)
SMEM = pl.BlockSpec(memory_space=pltpu.SMEM)


def dot(a, b):
    return jnp.dot(a, b, preferred_element_type=F32)


def nothing(token_ref, out_ref):
    del token_ref, out_ref


def span(token, cost):
    return pl.pallas_call(
        nothing,
        out_shape=jax.ShapeDtypeStruct((8, 128), F32),
        in_specs=[pl.BlockSpec(memory_space=pl.ANY)],
        out_specs=pl.BlockSpec(memory_space=pl.ANY),
        input_output_aliases={0: 0},
        cost_estimate=pl.CostEstimate(flops=cost, bytes_accessed=8192, transcendentals=0),
        compiler_params=pltpu.CompilerParams(has_side_effects=True),
    )(token)


def stage(token, *values, cost=5 * 10**8):
    token, *values = lax.optimization_barrier((token, *values))
    return span(token, cost), *values


def hidden_kernel(tile, at_ref, *refs):
    *refs, out_ref = refs
    n = len(refs) // 3
    blocks, direct, swapped = refs[:n], refs[n : 2 * n], refs[2 * n :]
    rows, units = out_ref.shape
    gate_first = at_ref[1] == 1
    for shift in range(n):

        @pl.when(at_ref[0] == shift)
        def _(shift=shift):
            parts = [jnp.concatenate([direct[j][...], swapped[j][...]], axis=1) for j in range(n)]
            weights = jnp.concatenate(parts, axis=0)
            for r in range(0, rows, tile):
                cut = pl.ds(r, tile)
                sums = dot(jnp.concatenate([blocks[shift ^ j][cut, :] for j in range(n)], axis=1), weights)
                a, b = sums[:, :units], sums[:, units:]
                gate, up = jnp.where(gate_first, a, b), jnp.where(gate_first, b, a)
                out_ref[cut, :] = (gate / (1.0 + jnp.exp(-gate)) * up).astype(BF16)


def hidden_of(at, blocks, direct, swapped):
    rows, units = blocks[0].shape[0], direct[0].shape[1]
    size = sum(x.size for x in (*blocks, *direct, *swapped)) * 2
    return pl.pallas_call(
        functools.partial(hidden_kernel, rows // 2),
        out_shape=jax.ShapeDtypeStruct((rows, units), BF16),
        in_specs=[SMEM] + [VMEM] * (len(blocks) + len(direct) + len(swapped)),
        out_specs=VMEM,
        cost_estimate=pl.CostEstimate(flops=0, bytes_accessed=size, transcendentals=0),
        compiler_params=pltpu.CompilerParams(vmem_limit_bytes=16 * 2**20),
    )(at, *blocks, *direct, *swapped)


def output_kernel(at_ref, *refs):
    n = 4
    hidden, refs, out_ref = refs[:n], refs[n:-1], refs[-1]
    whole = [ref for ref in refs if ref.shape[0] == n]
    split = [ref for ref in refs if ref.shape[0] != n]
    split = list(zip(split[::2], split[1::2]))
    for shift in range(n):

        @pl.when(at_ref[1] == shift)
        def _(shift=shift):
            parts = []
            for i in range(n):
                part = [ref[at_ref[0] ^ i] for ref in whole]
                b = shift ^ i
                part += [pair[b // (n // 2)][b % (n // 2)] for pair in split]
                parts.append(jnp.concatenate(part, axis=1) if len(part) > 1 else part[0])
            rows = jnp.concatenate([ref[...] for ref in hidden], axis=1)
            out_ref[...] = dot(rows, jnp.concatenate(parts, axis=0)).astype(out_ref.dtype)


def output_of(at, hidden, down, kind):
    columns = sum(part.shape[2] * part.shape[0] for part in down) // len(hidden)
    size = sum(x.size for x in (*hidden, *down)) * 2
    return pl.pallas_call(
        output_kernel,
        out_shape=jax.ShapeDtypeStruct((hidden[0].shape[0], columns), kind),
        in_specs=[SMEM] + [VMEM] * (len(hidden) + len(down)),
        out_specs=VMEM,
        cost_estimate=pl.CostEstimate(flops=0, bytes_accessed=size, transcendentals=0),
        compiler_params=pltpu.CompilerParams(vmem_limit_bytes=16 * 2**20),
    )(at, *hidden, *down)


def add_kernel(columns, at_ref, mine_ref, theirs_ref, out_ref):
    for j in range(out_ref.shape[1] // columns):
        mine, theirs = (pl.ds(i * columns, columns) for i in (j, j ^ 1))
        cut = pl.ds(pl.multiple_of((at_ref[0] ^ j) * columns, columns), columns)
        out_ref[:, cut] = (mine_ref[:, mine] + theirs_ref[:, theirs]).astype(BF16)


def add(at, columns, mine, theirs):
    return pl.pallas_call(
        functools.partial(add_kernel, columns),
        out_shape=jax.ShapeDtypeStruct(mine.shape, BF16),
        in_specs=[SMEM] + [VMEM] * 2,
        out_specs=VMEM,
        compiler_params=pltpu.CompilerParams(vmem_limit_bytes=16 * 2**20),
    )(at, mine, theirs)


def shards(sizes, tokens, gate_weight, up_weight, down_weight):
    n_batch, n_weight = sizes["batch"], sizes["weight"]
    plane = lax.axis_index("batch")
    place = lax.axis_index("weight")
    group = lax.axis_index("groups")
    first = group == 0
    parity = plane % 2
    even = parity == 0
    rows, features = tokens.shape
    depth, units = gate_weight.shape
    half = units // 2
    columns = down_weight.shape[1]

    def flip(x, axis, bits):
        return lax.ppermute(x, axis, [(i, i ^ bits) for i in range(sizes[axis])])

    def half_of(weight, parity):
        return lax.dynamic_slice_in_dim(weight, parity * half, half, axis=1)

    down_blocks = down_weight.reshape(n_weight, 2, half, columns)

    if n_batch == n_weight == 4:
        send_own = jnp.where(first, half_of(gate_weight, parity), half_of(up_weight, parity))
        token = jnp.zeros((8, 128), F32)
        tokens_x = flip(tokens, "weight", 2)
        tokens_pair = flip(tokens, "batch", 1)
        tokens_core = flip(tokens, "weight", 1)
        token, gate_weight, up_weight, send_own = stage(token, gate_weight, up_weight, send_own, cost=0)
        direct_2 = flip(send_own, "batch", 2)
        send_other = jnp.where(first, half_of(gate_weight, 1 - parity), half_of(up_weight, 1 - parity))
        keep_own = jnp.where(first, half_of(up_weight, parity), half_of(gate_weight, parity))
        low, high = slice(0, n_weight // 2), slice(n_weight // 2, n_weight)
        down_own = jnp.where(even, down_blocks[:, 0], down_blocks[:, 1])
        down_other = jnp.where(even, down_blocks[:, 1], down_blocks[:, 0])
        down_send_2 = jnp.where(first, down_own[low], down_own[high])
        down_send_3 = jnp.where(first, down_other[low], down_other[high])
        token, tokens_x, tokens_core, send_other = stage(token, tokens_x, tokens_core, send_other)
        direct_1 = flip(send_other, "batch", 1)
        token, tokens_pair, direct_2, send_other, tokens_x = stage(token, tokens_pair, direct_2, send_other, tokens_x)
        direct_3 = flip(send_other, "batch", 3)
        swapped_2 = flip(direct_2, "groups", 1)
        tokens_pair_x = flip(tokens_pair, "weight", 2)
        tokens_x_core = flip(tokens_x, "weight", 1)
        token, direct_1, keep_own, down_own, down_other, down_send_2, down_send_3 = stage(
            token, direct_1, keep_own, down_own, down_other, down_send_2, down_send_3, cost=2 * 10**9
        )
        swapped_1 = flip(direct_1, "groups", 1)
        token, tokens_pair_x, swapped_2, tokens_x_core = stage(token, tokens_pair_x, swapped_2, tokens_x_core)
        token, direct_3, x, y = stage(token, direct_3, tokens_pair, tokens_pair_x)
        swapped_3 = flip(direct_3, "groups", 1)
        pair_core = [flip(x, "weight", 1), flip(y, "weight", 1)]
        token, swapped_1, x, y = stage(token, swapped_1, down_other, down_send_2, cost=2 * 10**9)
        down_1 = flip(x, "batch", 1)
        down_2 = flip(y, "batch", 2)
        token, x, *pair_core = stage(token, down_send_3, *pair_core)
        down_3 = flip(x, "batch", 3)
        token, swapped_3 = stage(token, swapped_3, cost=0)
        at = jnp.stack([place ^ plane, jnp.where(first, 1, 0)]).astype(jnp.int32)
        direct = [send_own, direct_1, direct_2, direct_3]
        swapped = [keep_own, swapped_1, swapped_2, swapped_3]
        hidden_pair = hidden_of(at, [tokens_pair, pair_core[0], tokens_pair_x, pair_core[1]], direct, swapped)
        far_pair = flip(hidden_pair, "weight", 2)
        token, hidden_pair = stage(token, hidden_pair, cost=0)
        token, down_2, x = stage(token, down_2, tokens)
        swapped_down_2 = flip(down_2, "groups", 1)
        hidden_own = hidden_of(at, [x, tokens_core, tokens_x, tokens_x_core], direct, swapped)
        token, down_1, down_3, hidden_own = stage(token, down_1, down_3, hidden_own, cost=45 * 10**8)
        swapped_down_3 = flip(down_3, "groups", 1)
        token, far_pair, hidden_pair = stage(token, far_pair, hidden_pair)
        core_pair = [flip(x, "weight", 1) for x in (hidden_pair, far_pair)]
        far_own = flip(hidden_own, "weight", 2)
        token, swapped_down_2 = stage(token, swapped_down_2)
        token, swapped_down_3 = stage(token, swapped_down_3, cost=3 * 10**9)
        token, *core_pair = stage(token, *core_pair)
        at = jnp.stack([place, place ^ jnp.where(first, 0, 2)]).astype(jnp.int32)
        down = [down_own, down_1, down_2, swapped_down_2, down_3, swapped_down_3]
        part = output_of(at, [hidden_pair, core_pair[0], far_pair, core_pair[1]], down, BF16)
        theirs = flip(part, "batch", 1)
        token, far_own, x = stage(token, far_own, hidden_own)
        core_own = [flip(x, "weight", 1) for x in (x, far_own)]
        token, *core_own = stage(token, *core_own)
        mine = output_of(at, [hidden_own, core_own[0], far_own, core_own[1]], down, F32)
        token, mine, theirs = stage(token, mine, theirs)
        return add(plane.astype(jnp.int32).reshape(1), columns, mine, theirs)

    tokens_pair = flip(tokens, "batch", 1)
    both = lax.all_gather(jnp.concatenate([tokens_pair, tokens], axis=0), "weight", axis=1, tiled=True)
    mine = lax.all_gather(jnp.where(first, gate_weight, up_weight), "batch", axis=0, tiled=True)
    mine = half_of(mine, parity)
    mine, theirs = dot(both, mine), dot(both, flip(mine, "groups", 1))
    gate_sum, up_sum = jnp.where(first, mine, theirs), jnp.where(first, theirs, mine)
    hidden = lax.all_gather((jax.nn.silu(gate_sum) * up_sum).astype(BF16), "weight", axis=1, tiled=True)
    down_all = lax.all_gather(down_weight, "batch", axis=1, tiled=True)
    down_all = down_all.reshape(n_weight, 2, half, n_batch * columns)
    down_all = jnp.where(even, down_all[:, 0], down_all[:, 1]).reshape(n_weight * half, n_batch * columns)
    theirs = flip(dot(hidden[:rows], down_all).astype(BF16), "batch", 1)
    return (dot(hidden[rows:], down_all) + theirs).astype(BF16)


def solution(mesh):
    in_specs = (
        P(("groups", "batch"), "weight"),
        P("batch", "weight"),
        P("batch", "weight"),
        P(None, ("weight", "batch")),
    )
    out_specs = P(("groups", "batch"), "weight")
    sizes = dict(mesh.shape)

    def body(*args):
        return shards(sizes, *args)

    return jax.shard_map(body, mesh=mesh, in_specs=in_specs, out_specs=out_specs, check_vma=False)
```

time: 110 us -> 94.5 us (0.86)
  waiting for transfers between devices: 43.8 us -> 36.2 us
  starting transfers between devices: 39.9 us -> 32.9 us
  matrix products: 5.09 us -> 0 us
  Pallas kernels: 8.77 us -> 13.3 us
  other arithmetic: 6.87 us -> 3.52 us
  local copies, waits for them, and re-layouts: 4.83 us -> 7.97 us
    ppermute x26 -> x25, waiting for transfers between devices: 43.8 us -> 36.2 us  [flip(): return lax.ppermute(x, axis, [(i, i ^ bits) for i in range(sizes[axis])])]
    ppermute x26 -> x25, starting transfers between devices: 39.9 us -> 32.9 us  [flip(): return lax.ppermute(x, axis, [(i, i ^ bits) for i in range(sizes[axis])])]
    dot_general x2 -> x0, matrix products: 5.09 us -> none  [dot(): return jnp.dot(a, b, preferred_element_type=F32)]
    pallas_call x1 -> x3, Pallas kernels: 1.4 us -> 5.63 us  [the longest x2 4.68 us: output_of(): pl.pallas_call(output_kernel, out_shape=jax.ShapeDtypeStruct((hidden[0].s...]
    unnamed x16 -> x24, local copies, waits for them, and re-layouts: 3.4 us -> 7.37 us
    select_n x5 -> x4, other arithmetic: 5.73 us -> 3.37 us  [the longest x1 1.32 us: shards(): jnp.where(first, half_of(up_weight, parity), half_of(gate_weight, parity))]
  transfers between devices with their start and end apart: 26 -> 25, of which waited for: 12 -> 13; matrix products, arithmetic and copies ran while one was open for 11% -> 4% of each run, Pallas kernels for 8% -> 13%
where the time goes in v3:
time: 94.5 us; the launch traced here: 94 us
  waiting for transfers between devices  36.2 us (38%)
  starting transfers between devices  32.9 us (35%)
  Pallas kernels  13.3 us (14%)
  local copies, waits for them, and re-layouts  7.97 us (8%)
  other arithmetic  3.52 us (4%)
    ppermute x25, waiting for transfers between devices, flip(): return lax.ppermute(x, axis, [(i, i ^ bits) for i in range(sizes[axis])])  36.2 us
    ppermute x25, starting transfers between devices, flip(): return lax.ppermute(x, axis, [(i, i ^ bits) for i in range(sizes[axis])])  32.9 us
    pallas_call x2, Pallas kernels, hidden_of(): pl.pallas_call(functools.partial(hidden_kernel, rows // 2), out_shape=jax...  7.65 us
    unnamed x24, local copies, waits for them, and re-layouts  7.37 us
    pallas_call x2, Pallas kernels, output_of(): pl.pallas_call(output_kernel, out_shape=jax.ShapeDtypeStruct((hidden[0].s...  4.68 us
  transfers between devices with their start and end apart: 25, of which 13 were waited for; matrix products, arithmetic and copies ran while one was open for 4% of the time, Pallas kernels for 13%

profile of v3, /device:TPU:0, one launch (start us, length us, event | category | flops | bytes accessed | tf_op | source)
XLA Modules:
  0.0 94.0 jit_solution(7660879171301103030)
XLA Ops:
  0.5 2.5 %collective-permute-start = (bf16[512,512]{1,0:T(8,128)(2,1)}, bf16[512,512]{1,0:T(8,128)(2,1)}, u32[]{:S(2)}, u32[]{:S(2)}) collective-permute-start(bf16[512,512]{1,0:T(8,128)(2,1)} %refs_0_), channel_id=1, source_target_pairs={{0,2},{1,3},{2,0},{3,1},{4,6},{5,7},{6,4},{7,5},{8,10},{9,11},{10,... | collective-permute-start | bytes 1572872 | tf_op jit(solution)/shard_map/ppermute | solution.py:138
  3.0 1.6 %collective-permute-start.2 = (bf16[512,512]{1,0:T(8,128)(2,1)}, bf16[512,512]{1,0:T(8,128)(2,1)}, u32[]{:S(2)}, u32[]{:S(2)}) collective-permute-start(bf16[512,512]{1,0:T(8,128)(2,1)} %refs_0_), channel_id=1, source_target_pairs={{0,4},{4,0},{8,12},{12,8},{1,5},{5,1},{9,13},{13,9},{2,6},{6,2},{1... | collective-permute-start | bytes 1572872 | tf_op jit(solution)/shard_map/ppermute | solution.py:138
  4.6 1.2 %dynamic-slice_select_fusion.2.refs_4_ = bf16[512,384]{1,0:T(8,128)(2,1)S(1)} fusion(bf16[512,768]{1,0:T(8,128)(2,1)} %param.6, s32[]{:T(128)S(6)} %select_n.78, bf16[512,768]{1,0:T(8,128)(2,1)} %param.5, pred[]{:T(512)S(6)} %eq.8), kind=kLoop, calls=%fused_computation.4 | loop fusion | flops 196608 | bytes 1179653 | tf_op jit(solution)/shard_map/jit(_where)/select_n | solution.py:146
  5.8 2.7 %collective-permute-start.3 = (bf16[512,384]{1,0:T(8,128)(2,1)S(1)}, bf16[512,384]{1,0:T(8,128)(2,1)S(1)}, u32[]{:S(2)}, u32[]{:S(2)}) collective-permute-start(bf16[512,384]{1,0:T(8,128)(2,1)S(1)} %dynamic-slice_select_fusion.2.refs_4_), channel_id=1, source_target_pairs={{0,8},{4,12},{8,0},{12,4},{1,9},{5,13},{9,1},{13,5},{2,10},{6,14},... | collective-permute-start | bytes 1179656 | tf_op jit(solution)/shard_map/ppermute | solution.py:138
  9.0 1.3 %dynamic-slice_select_fusion = (bf16[512,384]{1,0:T(8,128)(2,1)S(1)}, bf16[512,384]{1,0:T(8,128)(2,1)S(1)}) fusion(bf16[512,768]{1,0:T(8,128)(2,1)} %param.5, s32[]{:T(128)S(6)} %select_n.78, bf16[512,768]{1,0:T(8,128)(2,1)S(1)} %copy-done.9, pred[]{:T(512)S(6)} %eq.8, s32[]{:T(128)S(6)} %select_n.80), kind=kLoop, calls=%fused_computation.2 | loop fusion | flops 393216 | bytes 2359305 | tf_op jit(solution)/shard_map/jit(_where)/select_n | solution.py:154
  11.2 4.7 %collective-permute-done.refs_2_ = bf16[512,512]{1,0:T(8,128)(2,1)} collective-permute-done((bf16[512,512]{1,0:T(8,128)(2,1)}, bf16[512,512]{1,0:T(8,128)(2,1)}, u32[]{:S(2)}, u32[]{:S(2)}) %collective-permute-start) | collective-permute-done | bytes 524320 | tf_op jit(solution)/shard_map/ppermute | solution.py:138
  15.9 1.8 %collective-permute-start.4 = (bf16[512,384]{1,0:T(8,128)(2,1)S(1)}, bf16[512,384]{1,0:T(8,128)(2,1)S(1)}, u32[]{:S(2)}, u32[]{:S(2)}) collective-permute-start(bf16[512,384]{1,0:T(8,128)(2,1)S(1)} %get-tuple-element.84), channel_id=1, source_target_pairs={{0,4},{4,0},{8,12},{12,8},{1,5},{5,1},{9,13},{13,9},{2,6},{6,2},{1... | collective-permute-start | bytes 1179656 | tf_op jit(solution)/shard_map/ppermute | solution.py:138
  17.7 7.8 %collective-permute-done.3.refs_6_ = bf16[512,384]{1,0:T(8,128)(2,1)S(1)} collective-permute-done((bf16[512,384]{1,0:T(8,128)(2,1)S(1)}, bf16[512,384]{1,0:T(8,128)(2,1)S(1)}, u32[]{:S(2)}, u32[]{:S(2)}) %collective-permute-start.3) | collective-permute-done | bytes 393248 | tf_op jit(solution)/shard_map/ppermute | solution.py:138
  25.5 1.0 %collective-permute-done.2.refs_0_ = bf16[512,512]{1,0:T(8,128)(2,1)} collective-permute-done((bf16[512,512]{1,0:T(8,128)(2,1)}, bf16[512,512]{1,0:T(8,128)(2,1)}, u32[]{:S(2)}, u32[]{:S(2)}) %collective-permute-start.2) | collective-permute-done | bytes 524320 | tf_op jit(solution)/shard_map/ppermute | solution.py:138
  26.7 4.1 %collective-permute-start.8 = (bf16[512,384]{1,0:T(8,128)(2,1)S(1)}, bf16[512,384]{1,0:T(8,128)(2,1)S(1)}, u32[]{:S(2)}, u32[]{:S(2)}) collective-permute-start(bf16[512,384]{1,0:T(8,128)(2,1)S(1)} %get-tuple-element.84), channel_id=1, source_target_pairs={{0,12},{4,8},{8,4},{12,0},{1,13},{5,9},{9,5},{13,1},{2,14},{6,10},... | collective-permute-start | bytes 1179656 | tf_op jit(solution)/shard_map/ppermute | solution.py:138
  30.8 1.5 %collective-permute-start.6 = (bf16[512,384]{1,0:T(8,128)(2,1)S(1)}, bf16[512,384]{1,0:T(8,128)(2,1)S(1)}, u32[]{:S(2)}, u32[]{:S(2)}) collective-permute-start(bf16[512,384]{1,0:T(8,128)(2,1)S(1)} %collective-permute-done.3.refs_6_), channel_id=1, source_target_pairs={{0,16},{16,0},{1,17},{17,1},{2,18},{18,2},{3,19},{19,3},{4,20},{20... | collective-permute-start | bytes 1179656 | tf_op jit(solution)/shard_map/ppermute | solution.py:138
  34.1 1.5 %collective-permute-start.9 = (bf16[512,384]{1,0:T(8,128)(2,1)S(1)}, bf16[512,384]{1,0:T(8,128)(2,1)S(1)}, u32[]{:S(2)}, u32[]{:S(2)}) collective-permute-start(bf16[512,384]{1,0:T(8,128)(2,1)S(1)} %collective-permute-done.4.refs_5_), channel_id=1, source_target_pairs={{0,16},{16,0},{1,17},{17,1},{2,18},{18,2},{3,19},{19,3},{4,20},{20... | collective-permute-start | bytes 1179656 | tf_op jit(solution)/shard_map/ppermute | solution.py:138
  35.6 7.2 %collective-permute-done.6.refs_10_ = bf16[512,384]{1,0:T(8,128)(2,1)S(1)} collective-permute-done((bf16[512,384]{1,0:T(8,128)(2,1)S(1)}, bf16[512,384]{1,0:T(8,128)(2,1)S(1)}, u32[]{:S(2)}, u32[]{:S(2)}) %collective-permute-start.6) | collective-permute-done | bytes 393248 | tf_op jit(solution)/shard_map/ppermute | solution.py:138
  42.8 1.8 %collective-permute-done.8.refs_7_ = bf16[512,384]{1,0:T(8,128)(2,1)S(1)} collective-permute-done((bf16[512,384]{1,0:T(8,128)(2,1)S(1)}, bf16[512,384]{1,0:T(8,128)(2,1)S(1)}, u32[]{:S(2)}, u32[]{:S(2)}) %collective-permute-start.8) | collective-permute-done | bytes 393248 | tf_op jit(solution)/shard_map/ppermute | solution.py:138
  45.1 1.5 %collective-permute-start.12 = (bf16[512,384]{1,0:T(8,128)(2,1)S(1)}, bf16[512,384]{1,0:T(8,128)(2,1)S(1)}, u32[]{:S(2)}, u32[]{:S(2)}) collective-permute-start(bf16[512,384]{1,0:T(8,128)(2,1)S(1)} %collective-permute-done.8.refs_7_), channel_id=1, source_target_pairs={{0,16},{16,0},{1,17},{17,1},{2,18},{18,2},{3,19},{19,3},{4,20},{20... | collective-permute-start | bytes 1179656 | tf_op jit(solution)/shard_map/ppermute | solution.py:138
  46.7 4.6 %collective-permute-done.9.refs_9_ = bf16[512,384]{1,0:T(8,128)(2,1)S(1)} collective-permute-done((bf16[512,384]{1,0:T(8,128)(2,1)S(1)}, bf16[512,384]{1,0:T(8,128)(2,1)S(1)}, u32[]{:S(2)}, u32[]{:S(2)}) %collective-permute-start.9) | collective-permute-done | bytes 393248 | tf_op jit(solution)/shard_map/ppermute | solution.py:138
  51.3 6.2 %collective-permute-start.14 = (bf16[4,384,128]{2,1,0:T(8,128)(2,1)}, bf16[4,384,128]{2,1,0:T(8,128)(2,1)}, u32[]{:S(2)}, u32[]{:S(2)}) collective-permute-start(bf16[4,384,128]{2,1,0:T(8,128)(2,1)} %bitcast.26), channel_id=1, source_target_pairs={{0,4},{4,0},{8,12},{12,8},{1,5},{5,1},{9,13},{13,9},{2,6},{6,2},{1... | collective-permute-start | bytes 1179656 | tf_op jit(solution)/shard_map/ppermute | solution.py:138
  57.6 1.1 %collective-permute-done.12.refs_11_ = bf16[512,384]{1,0:T(8,128)(2,1)S(1)} collective-permute-done((bf16[512,384]{1,0:T(8,128)(2,1)S(1)}, bf16[512,384]{1,0:T(8,128)(2,1)S(1)}, u32[]{:S(2)}, u32[]{:S(2)}) %collective-permute-start.12) | collective-permute-done | bytes 393248 | tf_op jit(solution)/shard_map/ppermute | solution.py:138
  58.6 4.3 %shard_map.55.refs_0_ = bf16[512,384]{1,0:T(8,128)(2,1)} custom-call(s32[2]{0:T(128)S(1)} %pad_add_fusion.at_ref, bf16[512,512]{1,0:T(8,128)(2,1)} %collective-permute-done.2.refs_0_, bf16[512,512]{1,0:T(8,128)(2,1)} %collective-permute-done.10.refs_1_, bf16[512,512]{1,0:T(8,128)(2,1)} %collective-permute-done.5.refs_2_, ...), custom_call_target="tpu_custom_call" | custom-call | bytes 5242880 | tf_op jit(solution)/shard_map/pallas_call | solution.py:64
  62.9 1.5 %collective-permute-start.16 = (bf16[512,384]{1,0:T(8,128)(2,1)}, bf16[512,384]{1,0:T(8,128)(2,1)}, u32[]{:S(2)}, u32[]{:S(2)}) collective-permute-start(bf16[512,384]{1,0:T(8,128)(2,1)} %shard_map.55.refs_0_), channel_id=1, source_target_pairs={{0,2},{1,3},{2,0},{3,1},{4,6},{5,7},{6,4},{7,5},{8,10},{9,11},{10,... | collective-permute-start | bytes 1179656 | tf_op jit(solution)/shard_map/ppermute | solution.py:138
  64.4 1.6 %collective-permute-start.17 = (bf16[2,384,128]{2,1,0:T(8,128)(2,1)}, bf16[2,384,128]{2,1,0:T(8,128)(2,1)}, u32[]{:S(2)}, u32[]{:S(2)}) collective-permute-start(bf16[2,384,128]{2,1,0:T(8,128)(2,1)} %collective-permute-done.13.refs_6_), channel_id=1, source_target_pairs={{0,16},{16,0},{1,17},{17,1},{2,18},{18,2},{3,19},{19,3},{4,20},{20... | collective-permute-start | bytes 589832 | tf_op jit(solution)/shard_map/ppermute | solution.py:138
  67.0 1.0 %copy-done.2 = bf16[512,512]{1,0:T(8,128)(2,1)S(1)} copy-done((bf16[512,512]{1,0:T(8,128)(2,1)S(1)}, bf16[512,512]{1,0:T(8,128)(2,1)}, u32[]{:S(2)}) %copy-start.2) | copy-done | bytes 524312
  68.1 1.0 %copy-done.4 = bf16[512,512]{1,0:T(8,128)(2,1)S(1)} copy-done((bf16[512,512]{1,0:T(8,128)(2,1)S(1)}, bf16[512,512]{1,0:T(8,128)(2,1)}, u32[]{:S(2)}) %copy-start.4) | copy-done | bytes 524312
  69.1 3.3 %shard_map.58.refs_0_ = bf16[512,384]{1,0:T(8,128)(2,1)S(1)} custom-call(s32[2]{0:T(128)S(1)} %pad_add_fusion.at_ref, bf16[512,512]{1,0:T(8,128)(2,1)S(1)} %copy-done.2, bf16[512,512]{1,0:T(8,128)(2,1)S(1)} %copy-done.4, bf16[512,512]{1,0:T(8,128)(2,1)} %collective-permute-done.refs_2_, bf16[512,512]{1,0:T(8,128)(2,1)} %collective-permute-done.7.refs_3_, ...), custom_call_target="tpu_custom_call" | custom-call | bytes 5242880 | tf_op jit(solution)/shard_map/pallas_call | solution.py:64
  74.1 1.5 %collective-permute-start.21 = (bf16[512,384]{1,0:T(8,128)(2,1)S(1)}, bf16[512,384]{1,0:T(8,128)(2,1)S(1)}, u32[]{:S(2)}, u32[]{:S(2)}) collective-permute-start(bf16[512,384]{1,0:T(8,128)(2,1)S(1)} %shard_map.58.refs_0_), channel_id=1, source_target_pairs={{0,2},{1,3},{2,0},{3,1},{4,6},{5,7},{6,4},{7,5},{8,10},{9,11},{10,... | collective-permute-start | bytes 1179656 | tf_op jit(solution)/shard_map/ppermute | solution.py:138
  75.5 2.9 %collective-permute-done.18.refs_9_ = bf16[2,384,128]{2,1,0:T(8,128)(2,1)S(1)} collective-permute-done((bf16[2,384,128]{2,1,0:T(8,128)(2,1)}, bf16[2,384,128]{2,1,0:T(8,128)(2,1)S(1)}, u32[]{:S(2)}, u32[]{:S(2)}) %collective-permute-start.18) | collective-permute-done | bytes 196640 | tf_op jit(solution)/shard_map/ppermute | solution.py:138
  78.5 2.5 %shard_map.67 = bf16[512,512]{1,0:T(8,128)(2,1)S(1)} custom-call(s32[2]{0:T(128)S(1)} %pad_add_fusion.1.at_ref, bf16[512,384]{1,0:T(8,128)(2,1)} %shard_map.55.refs_0_, bf16[512,384]{1,0:T(8,128)(2,1)S(1)} %collective-permute-done.19.refs_1_, bf16[512,384]{1,0:T(8,128)(2,1)} %collective-permute-done.16.refs_2_, ...), custom_call_target="tpu_custom_call" | custom-call | bytes 3145728 | tf_op jit(solution)/shard_map/pallas_call | solution.py:97
  80.9 2.2 %collective-permute-start.24 = (bf16[512,512]{1,0:T(8,128)(2,1)S(1)}, bf16[512,512]{1,0:T(8,128)(2,1)S(1)}, u32[]{:S(2)}, u32[]{:S(2)}) collective-permute-start(bf16[512,512]{1,0:T(8,128)(2,1)S(1)} %shard_map.67), channel_id=1, source_target_pairs={{0,4},{4,0},{8,12},{12,8},{1,5},{5,1},{9,13},{13,9},{2,6},{6,2},{1... | collective-permute-start | bytes 1572872 | tf_op jit(solution)/shard_map/ppermute | solution.py:138
  83.2 1.9 %collective-permute-done.21.refs_2_ = bf16[512,384]{1,0:T(8,128)(2,1)S(1)} collective-permute-done((bf16[512,384]{1,0:T(8,128)(2,1)S(1)}, bf16[512,384]{1,0:T(8,128)(2,1)S(1)}, u32[]{:S(2)}, u32[]{:S(2)}) %collective-permute-start.21) | collective-permute-done | bytes 393248 | tf_op jit(solution)/shard_map/ppermute | solution.py:138
  85.6 1.2 %collective-permute-done.22.refs_1_ = bf16[512,384]{1,0:T(8,128)(2,1)S(1)} collective-permute-done((bf16[512,384]{1,0:T(8,128)(2,1)S(1)}, bf16[512,384]{1,0:T(8,128)(2,1)S(1)}, u32[]{:S(2)}, u32[]{:S(2)}) %collective-permute-start.22) | collective-permute-done | bytes 393248 | tf_op jit(solution)/shard_map/ppermute | solution.py:138
  89.3 1.0 %copy-done.8 = bf16[512,384]{1,0:T(8,128)(2,1)S(1)} copy-done((bf16[512,384]{1,0:T(8,128)(2,1)S(1)}, bf16[512,384]{1,0:T(8,128)(2,1)}, u32[]{:S(2)}) %copy-start.8) | copy-done | bytes 393240
  90.3 2.2 %shard_map.66.mine_ref = f32[512,512]{1,0:T(8,128)S(1)} custom-call(s32[2]{0:T(128)S(1)} %pad_add_fusion.1.at_ref, bf16[512,384]{1,0:T(8,128)(2,1)S(1)} %shard_map.58.refs_0_, bf16[512,384]{1,0:T(8,128)(2,1)S(1)} %copy-done.6, bf16[512,384]{1,0:T(8,128)(2,1)S(1)} %collective-permute-done.21.refs_2_, bf16[512,384]{1,0:T(8,128)(2,1)S(1)} %copy-done.8, ...), custom_call_target="tpu_custom_call" | custom-call | bytes 3145728 | tf_op jit(solution)/shard_map/pallas_call | solution.py:97
  (73 shorter events, 11.4 us)
Async XLA Ops:
  0.0 9.0 %copy-start.9 = (bf16[512,768]{1,0:T(8,128)(2,1)S(1)}, bf16[512,768]{1,0:T(8,128)(2,1)}, u32[]{:S(2)}) copy-start(bf16[512,768]{1,0:T(8,128)(2,1)} %param.6) | copy-start | bytes 2359300
  0.0 10.4 %collective-permute-start.1 = (bf16[512,512]{1,0:T(8,128)(2,1)}, bf16[512,512]{1,0:T(8,128)(2,1)S(1)}, u32[]{:S(2)}, u32[]{:S(2)}) collective-permute-start(bf16[512,512]{1,0:T(8,128)(2,1)} %refs_0_), channel_id=1, source_target_pairs={{0,1},{1,0},{2,3},{3,2},{4,5},{5,4},{6,7},{7,6},{8,9},{9,8},{10,11... | collective-permute-start | bytes 1572872 | tf_op jit(solution)/shard_map/ppermute | solution.py:138
  0.5 15.4 %collective-permute-start = (bf16[512,512]{1,0:T(8,128)(2,1)}, bf16[512,512]{1,0:T(8,128)(2,1)}, u32[]{:S(2)}, u32[]{:S(2)}) collective-permute-start(bf16[512,512]{1,0:T(8,128)(2,1)} %refs_0_), channel_id=1, source_target_pairs={{0,2},{1,3},{2,0},{3,1},{4,6},{5,7},{6,4},{7,5},{8,10},{9,11},{10,... | collective-permute-start | bytes 1572872 | tf_op jit(solution)/shard_map/ppermute | solution.py:138
  3.0 23.5 %collective-permute-start.2 = (bf16[512,512]{1,0:T(8,128)(2,1)}, bf16[512,512]{1,0:T(8,128)(2,1)}, u32[]{:S(2)}, u32[]{:S(2)}) collective-permute-start(bf16[512,512]{1,0:T(8,128)(2,1)} %refs_0_), channel_id=1, source_target_pairs={{0,4},{4,0},{8,12},{12,8},{1,5},{5,1},{9,13},{13,9},{2,6},{6,2},{1... | collective-permute-start | bytes 1572872 | tf_op jit(solution)/shard_map/ppermute | solution.py:138
  5.8 19.7 %collective-permute-start.3 = (bf16[512,384]{1,0:T(8,128)(2,1)S(1)}, bf16[512,384]{1,0:T(8,128)(2,1)S(1)}, u32[]{:S(2)}, u32[]{:S(2)}) collective-permute-start(bf16[512,384]{1,0:T(8,128)(2,1)S(1)} %dynamic-slice_select_fusion.2.refs_4_), channel_id=1, source_target_pairs={{0,8},{4,12},{8,0},{12,4},{1,9},{5,13},{9,1},{13,5},{2,10},{6,14},... | collective-permute-start | bytes 1179656 | tf_op jit(solution)/shard_map/ppermute | solution.py:138
  15.9 10.7 %copy-start.11 = (bf16[3072,128]{1,0:T(8,128)(2,1)S(1)}, bf16[3072,128]{1,0:T(8,128)(2,1)}, u32[]{:S(2)}) copy-start(bf16[3072,128]{1,0:T(8,128)(2,1)} %param.7) | copy-start | bytes 2359300
  15.9 18.2 %collective-permute-start.4 = (bf16[512,384]{1,0:T(8,128)(2,1)S(1)}, bf16[512,384]{1,0:T(8,128)(2,1)S(1)}, u32[]{:S(2)}, u32[]{:S(2)}) collective-permute-start(bf16[512,384]{1,0:T(8,128)(2,1)S(1)} %get-tuple-element.84), channel_id=1, source_target_pairs={{0,4},{4,0},{8,12},{12,8},{1,5},{5,1},{9,13},{13,9},{2,6},{6,2},{1... | collective-permute-start | bytes 1179656 | tf_op jit(solution)/shard_map/ppermute | solution.py:138
  26.5 16.3 %collective-permute-start.7 = (bf16[512,512]{1,0:T(8,128)(2,1)}, bf16[512,512]{1,0:T(8,128)(2,1)}, u32[]{:S(2)}, u32[]{:S(2)}) collective-permute-start(bf16[512,512]{1,0:T(8,128)(2,1)} %collective-permute-done.refs_2_), channel_id=1, source_target_pairs={{0,1},{1,0},{2,3},{3,2},{4,5},{5,4},{6,7},{7,6},{8,9},{9,8},{10,11... | collective-permute-start | bytes 1572872 | tf_op jit(solution)/shard_map/ppermute | solution.py:138
  26.5 16.3 %collective-permute-start.5 = (bf16[512,512]{1,0:T(8,128)(2,1)}, bf16[512,512]{1,0:T(8,128)(2,1)}, u32[]{:S(2)}, u32[]{:S(2)}) collective-permute-start(bf16[512,512]{1,0:T(8,128)(2,1)} %collective-permute-done.2.refs_0_), channel_id=1, source_target_pairs={{0,2},{1,3},{2,0},{3,1},{4,6},{5,7},{6,4},{7,5},{8,10},{9,11},{10,... | collective-permute-start | bytes 1572872 | tf_op jit(solution)/shard_map/ppermute | solution.py:138
  26.7 6.4 %copy-start.10 = (bf16[4,1,384,128]{3,2,0,1:T(8,128)(2,1)}, bf16[4,1,384,128]{3,2,0,1:T(8,128)(2,1)S(1)}, u32[]{:S(2)}) copy-start(bf16[4,1,384,128]{3,2,0,1:T(8,128)(2,1)S(1)} %get-tuple-element.139) | copy-start | bytes 1179652
  26.7 18.0 %collective-permute-start.8 = (bf16[512,384]{1,0:T(8,128)(2,1)S(1)}, bf16[512,384]{1,0:T(8,128)(2,1)S(1)}, u32[]{:S(2)}, u32[]{:S(2)}) collective-permute-start(bf16[512,384]{1,0:T(8,128)(2,1)S(1)} %get-tuple-element.84), channel_id=1, source_target_pairs={{0,12},{4,8},{8,4},{12,0},{1,13},{5,9},{9,5},{13,1},{2,14},{6,10},... | collective-permute-start | bytes 1179656 | tf_op jit(solution)/shard_map/ppermute | solution.py:138
  30.8 12.0 %collective-permute-start.6 = (bf16[512,384]{1,0:T(8,128)(2,1)S(1)}, bf16[512,384]{1,0:T(8,128)(2,1)S(1)}, u32[]{:S(2)}, u32[]{:S(2)}) collective-permute-start(bf16[512,384]{1,0:T(8,128)(2,1)S(1)} %collective-permute-done.3.refs_6_), channel_id=1, source_target_pairs={{0,16},{16,0},{1,17},{17,1},{2,18},{18,2},{3,19},{19,3},{4,20},{20... | collective-permute-start | bytes 1179656 | tf_op jit(solution)/shard_map/ppermute | solution.py:138
  34.1 17.1 %collective-permute-start.9 = (bf16[512,384]{1,0:T(8,128)(2,1)S(1)}, bf16[512,384]{1,0:T(8,128)(2,1)S(1)}, u32[]{:S(2)}, u32[]{:S(2)}) collective-permute-start(bf16[512,384]{1,0:T(8,128)(2,1)S(1)} %collective-permute-done.4.refs_5_), channel_id=1, source_target_pairs={{0,16},{16,0},{1,17},{17,1},{2,18},{18,2},{3,19},{19,3},{4,20},{20... | collective-permute-start | bytes 1179656 | tf_op jit(solution)/shard_map/ppermute | solution.py:138
  44.6 12.8 %collective-permute-start.10 = (bf16[512,512]{1,0:T(8,128)(2,1)}, bf16[512,512]{1,0:T(8,128)(2,1)}, u32[]{:S(2)}, u32[]{:S(2)}) collective-permute-start(bf16[512,512]{1,0:T(8,128)(2,1)} %collective-permute-done.2.refs_0_), channel_id=1, source_target_pairs={{0,1},{1,0},{2,3},{3,2},{4,5},{5,4},{6,7},{7,6},{8,9},{9,8},{10,11... | collective-permute-start | bytes 1572872 | tf_op jit(solution)/shard_map/ppermute | solution.py:138
  44.6 12.8 %collective-permute-start.11 = (bf16[512,512]{1,0:T(8,128)(2,1)}, bf16[512,512]{1,0:T(8,128)(2,1)}, u32[]{:S(2)}, u32[]{:S(2)}) collective-permute-start(bf16[512,512]{1,0:T(8,128)(2,1)} %collective-permute-done.5.refs_2_), channel_id=1, source_target_pairs={{0,1},{1,0},{2,3},{3,2},{4,5},{5,4},{6,7},{7,6},{8,9},{9,8},{10,11... | collective-permute-start | bytes 1572872 | tf_op jit(solution)/shard_map/ppermute | solution.py:138
  45.1 13.5 %collective-permute-start.12 = (bf16[512,384]{1,0:T(8,128)(2,1)S(1)}, bf16[512,384]{1,0:T(8,128)(2,1)S(1)}, u32[]{:S(2)}, u32[]{:S(2)}) collective-permute-start(bf16[512,384]{1,0:T(8,128)(2,1)S(1)} %collective-permute-done.8.refs_7_), channel_id=1, source_target_pairs={{0,16},{16,0},{1,17},{17,1},{2,18},{18,2},{3,19},{19,3},{4,20},{20... | collective-permute-start | bytes 1179656 | tf_op jit(solution)/shard_map/ppermute | solution.py:138
  51.2 13.2 %collective-permute-start.13 = (bf16[2,384,128]{2,1,0:T(8,128)(2,1)}, bf16[2,384,128]{2,1,0:T(8,128)(2,1)}, u32[]{:S(2)}, u32[]{:S(2)}) collective-permute-start(bf16[2,384,128]{2,1,0:T(8,128)(2,1)} %get-tuple-element.104), channel_id=1, source_target_pairs={{0,8},{4,12},{8,0},{12,4},{1,9},{5,13},{9,1},{13,5},{2,10},{6,14},... | collective-permute-start | bytes 589832 | tf_op jit(solution)/shard_map/ppermute | solution.py:138
  51.3 21.2 %collective-permute-start.14 = (bf16[4,384,128]{2,1,0:T(8,128)(2,1)}, bf16[4,384,128]{2,1,0:T(8,128)(2,1)}, u32[]{:S(2)}, u32[]{:S(2)}) collective-permute-start(bf16[4,384,128]{2,1,0:T(8,128)(2,1)} %bitcast.26), channel_id=1, source_target_pairs={{0,4},{4,0},{8,12},{12,8},{1,5},{5,1},{9,13},{13,9},{2,6},{6,2},{1... | collective-permute-start | bytes 1179656 | tf_op jit(solution)/shard_map/ppermute | solution.py:138
  57.5 15.0 %collective-permute-start.15 = (bf16[2,384,128]{2,1,0:T(8,128)(2,1)}, bf16[2,384,128]{2,1,0:T(8,128)(2,1)}, u32[]{:S(2)}, u32[]{:S(2)}) collective-permute-start(bf16[2,384,128]{2,1,0:T(8,128)(2,1)} %get-tuple-element.107), channel_id=1, source_target_pairs={{0,12},{4,8},{8,4},{12,0},{1,13},{5,9},{9,5},{13,1},{2,14},{6,10},... | collective-permute-start | bytes 589832 | tf_op jit(solution)/shard_map/ppermute | solution.py:138
  58.6 4.3 %copy-start = (bf16[512,384]{1,0:T(8,128)(2,1)}, bf16[512,384]{1,0:T(8,128)(2,1)S(1)}, u32[]{:S(2)}) copy-start(bf16[512,384]{1,0:T(8,128)(2,1)S(1)} %collective-permute-done.12.refs_11_) | copy-start | bytes 1179652
  62.9 10.5 %collective-permute-start.16 = (bf16[512,384]{1,0:T(8,128)(2,1)}, bf16[512,384]{1,0:T(8,128)(2,1)}, u32[]{:S(2)}, u32[]{:S(2)}) collective-permute-start(bf16[512,384]{1,0:T(8,128)(2,1)} %shard_map.55.refs_0_), channel_id=1, source_target_pairs={{0,2},{1,3},{2,0},{3,1},{4,6},{5,7},{6,4},{7,5},{8,10},{9,11},{10,... | collective-permute-start | bytes 1179656 | tf_op jit(solution)/shard_map/ppermute | solution.py:138
  64.4 11.1 %collective-permute-start.17 = (bf16[2,384,128]{2,1,0:T(8,128)(2,1)}, bf16[2,384,128]{2,1,0:T(8,128)(2,1)}, u32[]{:S(2)}, u32[]{:S(2)}) collective-permute-start(bf16[2,384,128]{2,1,0:T(8,128)(2,1)} %collective-permute-done.13.refs_6_), channel_id=1, source_target_pairs={{0,16},{16,0},{1,17},{17,1},{2,18},{18,2},{3,19},{19,3},{4,20},{20... | collective-permute-start | bytes 589832 | tf_op jit(solution)/shard_map/ppermute | solution.py:138
  67.0 1.0 %copy-start.2 = (bf16[512,512]{1,0:T(8,128)(2,1)S(1)}, bf16[512,512]{1,0:T(8,128)(2,1)}, u32[]{:S(2)}) copy-start(bf16[512,512]{1,0:T(8,128)(2,1)} %refs_0_) | copy-start | bytes 1572868
  68.1 1.0 %copy-start.4 = (bf16[512,512]{1,0:T(8,128)(2,1)S(1)}, bf16[512,512]{1,0:T(8,128)(2,1)}, u32[]{:S(2)}) copy-start(bf16[512,512]{1,0:T(8,128)(2,1)} %copy-done.3) | copy-start | bytes 1572868
  72.5 5.9 %collective-permute-start.18 = (bf16[2,384,128]{2,1,0:T(8,128)(2,1)}, bf16[2,384,128]{2,1,0:T(8,128)(2,1)S(1)}, u32[]{:S(2)}, u32[]{:S(2)}) collective-permute-start(bf16[2,384,128]{2,1,0:T(8,128)(2,1)} %collective-permute-done.15.refs_8_), channel_id=1, source_target_pairs={{0,16},{16,0},{1,17},{17,1},{2,18},{18,2},{3,19},{19,3},{4,20},{20... | collective-permute-start | bytes 589832 | tf_op jit(solution)/shard_map/ppermute | solution.py:138
  73.5 5.0 %collective-permute-start.19 = (bf16[512,384]{1,0:T(8,128)(2,1)}, bf16[512,384]{1,0:T(8,128)(2,1)S(1)}, u32[]{:S(2)}, u32[]{:S(2)}) collective-permute-start(bf16[512,384]{1,0:T(8,128)(2,1)} %shard_map.55.refs_0_), channel_id=1, source_target_pairs={{0,1},{1,0},{2,3},{3,2},{4,5},{5,4},{6,7},{7,6},{8,9},{9,8},{10,11... | collective-permute-start | bytes 1179656 | tf_op jit(solution)/shard_map/ppermute | solution.py:138
  73.5 5.0 %collective-permute-start.20 = (bf16[512,384]{1,0:T(8,128)(2,1)}, bf16[512,384]{1,0:T(8,128)(2,1)S(1)}, u32[]{:S(2)}, u32[]{:S(2)}) collective-permute-start(bf16[512,384]{1,0:T(8,128)(2,1)} %collective-permute-done.16.refs_2_), channel_id=1, source_target_pairs={{0,1},{1,0},{2,3},{3,2},{4,5},{5,4},{6,7},{7,6},{8,9},{9,8},{10,11... | collective-permute-start | bytes 1179656 | tf_op jit(solution)/shard_map/ppermute | solution.py:138
  74.1 11.0 %collective-permute-start.21 = (bf16[512,384]{1,0:T(8,128)(2,1)S(1)}, bf16[512,384]{1,0:T(8,128)(2,1)S(1)}, u32[]{:S(2)}, u32[]{:S(2)}) collective-permute-start(bf16[512,384]{1,0:T(8,128)(2,1)S(1)} %shard_map.58.refs_0_), channel_id=1, source_target_pairs={{0,2},{1,3},{2,0},{3,1},{4,6},{5,7},{6,4},{7,5},{8,10},{9,11},{10,... | collective-permute-start | bytes 1179656 | tf_op jit(solution)/shard_map/ppermute | solution.py:138
  80.9 12.1 %collective-permute-start.24 = (bf16[512,512]{1,0:T(8,128)(2,1)S(1)}, bf16[512,512]{1,0:T(8,128)(2,1)S(1)}, u32[]{:S(2)}, u32[]{:S(2)}) collective-permute-start(bf16[512,512]{1,0:T(8,128)(2,1)S(1)} %shard_map.67), channel_id=1, source_target_pairs={{0,4},{4,0},{8,12},{12,8},{1,5},{5,1},{9,13},{13,9},{2,6},{6,2},{1... | collective-permute-start | bytes 1572872 | tf_op jit(solution)/shard_map/ppermute | solution.py:138
  85.1 1.7 %collective-permute-start.22 = (bf16[512,384]{1,0:T(8,128)(2,1)S(1)}, bf16[512,384]{1,0:T(8,128)(2,1)S(1)}, u32[]{:S(2)}, u32[]{:S(2)}) collective-permute-start(bf16[512,384]{1,0:T(8,128)(2,1)S(1)} %shard_map.58.refs_0_), channel_id=1, source_target_pairs={{0,1},{1,0},{2,3},{3,2},{4,5},{5,4},{6,7},{7,6},{8,9},{9,8},{10,11... | collective-permute-start | bytes 1179656 | tf_op jit(solution)/shard_map/ppermute | solution.py:138
  85.1 2.5 %collective-permute-start.23 = (bf16[512,384]{1,0:T(8,128)(2,1)S(1)}, bf16[512,384]{1,0:T(8,128)(2,1)S(1)}, u32[]{:S(2)}, u32[]{:S(2)}) collective-permute-start(bf16[512,384]{1,0:T(8,128)(2,1)S(1)} %collective-permute-done.21.refs_2_), channel_id=1, source_target_pairs={{0,1},{1,0},{2,3},{3,2},{4,5},{5,4},{6,7},{7,6},{8,9},{9,8},{10,11... | collective-permute-start | bytes 1179656 | tf_op jit(solution)/shard_map/ppermute | solution.py:138
  88.3 1.0 %copy-start.6 = (bf16[512,384]{1,0:T(8,128)(2,1)S(1)}, bf16[512,384]{1,0:T(8,128)(2,1)}, u32[]{:S(2)}) copy-start(bf16[512,384]{1,0:T(8,128)(2,1)} %copy-done.5) | copy-start | bytes 1179652
  (5 other events, 4.3 us)

commit v4 on v3

--- a/solution.py
+++ b/solution.py
@@ -29,7 +29,7 @@
         out_specs=pl.BlockSpec(memory_space=pl.ANY),
         input_output_aliases={0: 0},
         cost_estimate=pl.CostEstimate(flops=cost, bytes_accessed=8192, transcendentals=0),
-        compiler_params=pltpu.CompilerParams(has_side_effects=True),
+        compiler_params=pltpu.CompilerParams(has_side_effects=True, vmem_limit_bytes=2**16),
     )(token)
 
 

time: 94.5 us -> 92.1 us (0.975)
  waiting for transfers between devices: 36.2 us -> 44.5 us
  local copies, waits for them, and re-layouts: 7.97 us -> 1.58 us
  Pallas kernels: 13.3 us -> 10.9 us
  starting transfers between devices: 32.9 us -> 31.2 us
    ppermute x25, waiting for transfers between devices: 36.2 us -> 44.5 us  [flip(): return lax.ppermute(x, axis, [(i, i ^ bits) for i in range(sizes[axis])])]
    unnamed x24 -> x18, local copies, waits for them, and re-layouts: 7.37 us -> 1.58 us
    ppermute x25, starting transfers between devices: 32.9 us -> 31.2 us  [flip(): return lax.ppermute(x, axis, [(i, i ^ bits) for i in range(sizes[axis])])]
    pallas_call x2, Pallas kernels: 4.68 us -> 3.11 us  [output_of(): pl.pallas_call(output_kernel, out_shape=jax.ShapeDtypeStruct((hidden[0].s...]
  transfers between devices with their start and end apart: 25 -> 25, of which waited for: 13 -> 15; matrix products, arithmetic and copies ran while one was open for 4% -> 4% of each run, Pallas kernels for 13% -> 11%
where the time goes in v4:
time: 92.1 us; the launch traced here: 91.9 us
  waiting for transfers between devices  44.5 us (48%)
  starting transfers between devices  31.2 us (34%)
  Pallas kernels  10.9 us (12%)
  other arithmetic  3.56 us (4%)
  local copies, waits for them, and re-layouts  1.58 us (2%)
    ppermute x25, waiting for transfers between devices, flip(): return lax.ppermute(x, axis, [(i, i ^ bits) for i in range(sizes[axis])])  44.5 us
    ppermute x25, starting transfers between devices, flip(): return lax.ppermute(x, axis, [(i, i ^ bits) for i in range(sizes[axis])])  31.2 us
    pallas_call x2, Pallas kernels, hidden_of(): pl.pallas_call(functools.partial(hidden_kernel, rows // 2), out_shape=jax...  6.77 us
    pallas_call x2, Pallas kernels, output_of(): pl.pallas_call(output_kernel, out_shape=jax.ShapeDtypeStruct((hidden[0].s...  3.11 us
  transfers between devices with their start and end apart: 25, of which 15 were waited for; matrix products, arithmetic and copies ran while one was open for 4% of the time, Pallas kernels for 11%

profile of v4, /device:TPU:0, one launch (start us, length us, event | category | flops | bytes accessed | tf_op | source)
XLA Modules:
  0.0 91.9 jit_solution(464075169742545648)
XLA Ops:
  0.5 2.5 %collective-permute-start = (bf16[512,512]{1,0:T(8,128)(2,1)}, bf16[512,512]{1,0:T(8,128)(2,1)}, u32[]{:S(2)}, u32[]{:S(2)}) collective-permute-start(bf16[512,512]{1,0:T(8,128)(2,1)} %refs_0_), channel_id=1, source_target_pairs={{0,2},{1,3},{2,0},{3,1},{4,6},{5,7},{6,4},{7,5},{8,10},{9,11},{10,... | collective-permute-start | bytes 1572872 | tf_op jit(solution)/shard_map/ppermute | solution.py:138
  3.0 1.6 %collective-permute-start.2 = (bf16[512,512]{1,0:T(8,128)(2,1)}, bf16[512,512]{1,0:T(8,128)(2,1)}, u32[]{:S(2)}, u32[]{:S(2)}) collective-permute-start(bf16[512,512]{1,0:T(8,128)(2,1)} %refs_0_), channel_id=1, source_target_pairs={{0,4},{4,0},{8,12},{12,8},{1,5},{5,1},{9,13},{13,9},{2,6},{6,2},{1... | collective-permute-start | bytes 1572872 | tf_op jit(solution)/shard_map/ppermute | solution.py:138
  4.6 1.2 %dynamic-slice_select_fusion.2.refs_4_ = bf16[512,384]{1,0:T(8,128)(2,1)S(1)} fusion(bf16[512,768]{1,0:T(8,128)(2,1)} %param.6, s32[]{:T(128)S(6)} %select_n.78, bf16[512,768]{1,0:T(8,128)(2,1)} %param.5, pred[]{:T(512)S(6)} %eq.8), kind=kLoop, calls=%fused_computation.4 | loop fusion | flops 196608 | bytes 1179653 | tf_op jit(solution)/shard_map/jit(_where)/select_n | solution.py:146
  5.8 2.7 %collective-permute-start.3 = (bf16[512,384]{1,0:T(8,128)(2,1)S(1)}, bf16[512,384]{1,0:T(8,128)(2,1)S(1)}, u32[]{:S(2)}, u32[]{:S(2)}) collective-permute-start(bf16[512,384]{1,0:T(8,128)(2,1)S(1)} %dynamic-slice_select_fusion.2.refs_4_), channel_id=1, source_target_pairs={{0,8},{4,12},{8,0},{12,4},{1,9},{5,13},{9,1},{13,5},{2,10},{6,14},... | collective-permute-start | bytes 1179656 | tf_op jit(solution)/shard_map/ppermute | solution.py:138
  8.5 1.3 %dynamic-slice_select_fusion = (bf16[512,384]{1,0:T(8,128)(2,1)S(1)}, bf16[512,384]{1,0:T(8,128)(2,1)S(1)}) fusion(bf16[512,768]{1,0:T(8,128)(2,1)} %param.5, s32[]{:T(128)S(6)} %select_n.78, bf16[512,768]{1,0:T(8,128)(2,1)S(1)} %copy-done.5, pred[]{:T(512)S(6)} %eq.8, s32[]{:T(128)S(6)} %select_n.80), kind=kLoop, calls=%fused_computation.2 | loop fusion | flops 393216 | bytes 2359305 | tf_op jit(solution)/shard_map/jit(_where)/select_n | solution.py:154
  10.6 5.3 %collective-permute-done.refs_2_ = bf16[512,512]{1,0:T(8,128)(2,1)} collective-permute-done((bf16[512,512]{1,0:T(8,128)(2,1)}, bf16[512,512]{1,0:T(8,128)(2,1)}, u32[]{:S(2)}, u32[]{:S(2)}) %collective-permute-start) | collective-permute-done | bytes 524320 | tf_op jit(solution)/shard_map/ppermute | solution.py:138
  15.9 1.8 %collective-permute-start.4 = (bf16[512,384]{1,0:T(8,128)(2,1)S(1)}, bf16[512,384]{1,0:T(8,128)(2,1)S(1)}, u32[]{:S(2)}, u32[]{:S(2)}) collective-permute-start(bf16[512,384]{1,0:T(8,128)(2,1)S(1)} %get-tuple-element.84), channel_id=1, source_target_pairs={{0,4},{4,0},{8,12},{12,8},{1,5},{5,1},{9,13},{13,9},{2,6},{6,2},{1... | collective-permute-start | bytes 1179656 | tf_op jit(solution)/shard_map/ppermute | solution.py:138
  17.7 7.8 %collective-permute-done.3.refs_6_ = bf16[512,384]{1,0:T(8,128)(2,1)S(1)} collective-permute-done((bf16[512,384]{1,0:T(8,128)(2,1)S(1)}, bf16[512,384]{1,0:T(8,128)(2,1)S(1)}, u32[]{:S(2)}, u32[]{:S(2)}) %collective-permute-start.3) | collective-permute-done | bytes 393248 | tf_op jit(solution)/shard_map/ppermute | solution.py:138
  25.5 1.0 %collective-permute-done.2.refs_0_ = bf16[512,512]{1,0:T(8,128)(2,1)} collective-permute-done((bf16[512,512]{1,0:T(8,128)(2,1)}, bf16[512,512]{1,0:T(8,128)(2,1)}, u32[]{:S(2)}, u32[]{:S(2)}) %collective-permute-start.2) | collective-permute-done | bytes 524320 | tf_op jit(solution)/shard_map/ppermute | solution.py:138
  26.7 4.1 %collective-permute-start.8 = (bf16[512,384]{1,0:T(8,128)(2,1)S(1)}, bf16[512,384]{1,0:T(8,128)(2,1)S(1)}, u32[]{:S(2)}, u32[]{:S(2)}) collective-permute-start(bf16[512,384]{1,0:T(8,128)(2,1)S(1)} %get-tuple-element.84), channel_id=1, source_target_pairs={{0,12},{4,8},{8,4},{12,0},{1,13},{5,9},{9,5},{13,1},{2,14},{6,10},... | collective-permute-start | bytes 1179656 | tf_op jit(solution)/shard_map/ppermute | solution.py:138
  30.8 1.5 %collective-permute-start.6 = (bf16[512,384]{1,0:T(8,128)(2,1)S(1)}, bf16[512,384]{1,0:T(8,128)(2,1)S(1)}, u32[]{:S(2)}, u32[]{:S(2)}) collective-permute-start(bf16[512,384]{1,0:T(8,128)(2,1)S(1)} %collective-permute-done.3.refs_6_), channel_id=1, source_target_pairs={{0,16},{16,0},{1,17},{17,1},{2,18},{18,2},{3,19},{19,3},{4,20},{20... | collective-permute-start | bytes 1179656 | tf_op jit(solution)/shard_map/ppermute | solution.py:138
  34.1 1.5 %collective-permute-start.9 = (bf16[512,384]{1,0:T(8,128)(2,1)S(1)}, bf16[512,384]{1,0:T(8,128)(2,1)S(1)}, u32[]{:S(2)}, u32[]{:S(2)}) collective-permute-start(bf16[512,384]{1,0:T(8,128)(2,1)S(1)} %collective-permute-done.4.refs_5_), channel_id=1, source_target_pairs={{0,16},{16,0},{1,17},{17,1},{2,18},{18,2},{3,19},{19,3},{4,20},{20... | collective-permute-start | bytes 1179656 | tf_op jit(solution)/shard_map/ppermute | solution.py:138
  35.6 7.2 %collective-permute-done.6.refs_10_ = bf16[512,384]{1,0:T(8,128)(2,1)S(1)} collective-permute-done((bf16[512,384]{1,0:T(8,128)(2,1)S(1)}, bf16[512,384]{1,0:T(8,128)(2,1)S(1)}, u32[]{:S(2)}, u32[]{:S(2)}) %collective-permute-start.6) | collective-permute-done | bytes 393248 | tf_op jit(solution)/shard_map/ppermute | solution.py:138
  43.6 1.1 %collective-permute-done.8.refs_7_ = bf16[512,384]{1,0:T(8,128)(2,1)S(1)} collective-permute-done((bf16[512,384]{1,0:T(8,128)(2,1)S(1)}, bf16[512,384]{1,0:T(8,128)(2,1)S(1)}, u32[]{:S(2)}, u32[]{:S(2)}) %collective-permute-start.8) | collective-permute-done | bytes 393248 | tf_op jit(solution)/shard_map/ppermute | solution.py:138
  45.1 1.5 %collective-permute-start.12 = (bf16[512,384]{1,0:T(8,128)(2,1)S(1)}, bf16[512,384]{1,0:T(8,128)(2,1)S(1)}, u32[]{:S(2)}, u32[]{:S(2)}) collective-permute-start(bf16[512,384]{1,0:T(8,128)(2,1)S(1)} %collective-permute-done.8.refs_7_), channel_id=1, source_target_pairs={{0,16},{16,0},{1,17},{17,1},{2,18},{18,2},{3,19},{19,3},{4,20},{20... | collective-permute-start | bytes 1179656 | tf_op jit(solution)/shard_map/ppermute | solution.py:138
  46.7 4.5 %collective-permute-done.9.refs_9_ = bf16[512,384]{1,0:T(8,128)(2,1)S(1)} collective-permute-done((bf16[512,384]{1,0:T(8,128)(2,1)S(1)}, bf16[512,384]{1,0:T(8,128)(2,1)S(1)}, u32[]{:S(2)}, u32[]{:S(2)}) %collective-permute-start.9) | collective-permute-done | bytes 393248 | tf_op jit(solution)/shard_map/ppermute | solution.py:138
  51.3 5.5 %collective-permute-start.14 = (bf16[4,384,128]{2,1,0:T(8,128)(2,1)S(1)}, bf16[4,384,128]{2,1,0:T(8,128)(2,1)S(1)}, u32[]{:S(2)}, u32[]{:S(2)}) collective-permute-start(bf16[4,384,128]{2,1,0:T(8,128)(2,1)S(1)} %bitcast.26), channel_id=1, source_target_pairs={{0,4},{4,0},{8,12},{12,8},{1,5},{5,1},{9,13},{13,9},{2,6},{6,2},{1... | collective-permute-start | bytes 1179656 | tf_op jit(solution)/shard_map/ppermute | solution.py:138
  57.0 1.6 %collective-permute-done.12.refs_11_ = bf16[512,384]{1,0:T(8,128)(2,1)S(1)} collective-permute-done((bf16[512,384]{1,0:T(8,128)(2,1)S(1)}, bf16[512,384]{1,0:T(8,128)(2,1)S(1)}, u32[]{:S(2)}, u32[]{:S(2)}) %collective-permute-start.12) | collective-permute-done | bytes 393248 | tf_op jit(solution)/shard_map/ppermute | solution.py:138
  58.6 3.6 %shard_map.55.refs_0_ = bf16[512,384]{1,0:T(8,128)(2,1)S(1)} custom-call(s32[2]{0:T(128)S(1)} %pad_add_fusion.at_ref, bf16[512,512]{1,0:T(8,128)(2,1)} %collective-permute-done.2.refs_0_, bf16[512,512]{1,0:T(8,128)(2,1)} %collective-permute-done.10.refs_1_, bf16[512,512]{1,0:T(8,128)(2,1)} %collective-permute-done.5.refs_2_, ...), custom_call_target="tpu_custom_call" | custom-call | bytes 5242880 | tf_op jit(solution)/shard_map/pallas_call | solution.py:64
  62.2 1.6 %collective-permute-start.16 = (bf16[512,384]{1,0:T(8,128)(2,1)S(1)}, bf16[512,384]{1,0:T(8,128)(2,1)S(1)}, u32[]{:S(2)}, u32[]{:S(2)}) collective-permute-start(bf16[512,384]{1,0:T(8,128)(2,1)S(1)} %shard_map.55.refs_0_), channel_id=1, source_target_pairs={{0,2},{1,3},{2,0},{3,1},{4,6},{5,7},{6,4},{7,5},{8,10},{9,11},{10,... | collective-permute-start | bytes 1179656 | tf_op jit(solution)/shard_map/ppermute | solution.py:138
  63.8 1.5 %collective-permute-start.17 = (bf16[2,384,128]{2,1,0:T(8,128)(2,1)S(1)}, bf16[2,384,128]{2,1,0:T(8,128)(2,1)S(1)}, u32[]{:S(2)}, u32[]{:S(2)}) collective-permute-start(bf16[2,384,128]{2,1,0:T(8,128)(2,1)S(1)} %collective-permute-done.13.refs_6_), channel_id=1, source_target_pairs={{0,16},{16,0},{1,17},{17,1},{2,18},{18,2},{3,19},{19,3},{4,20},{20... | collective-permute-start | bytes 589832 | tf_op jit(solution)/shard_map/ppermute | solution.py:138
  65.3 3.2 %shard_map.58.refs_0_ = bf16[512,384]{1,0:T(8,128)(2,1)S(1)} custom-call(s32[2]{0:T(128)S(1)} %pad_add_fusion.at_ref, bf16[512,512]{1,0:T(8,128)(2,1)S(1)} %copy-done, bf16[512,512]{1,0:T(8,128)(2,1)S(1)} %copy-done.2, bf16[512,512]{1,0:T(8,128)(2,1)} %collective-permute-done.refs_2_, bf16[512,512]{1,0:T(8,128)(2,1)S(1)} %copy-done.4, ...), custom_call_target="tpu_custom_call" | custom-call | bytes 5242880 | tf_op jit(solution)/shard_map/pallas_call | solution.py:64
  68.5 2.5 %collective-permute-done.15.refs_8_ = bf16[2,384,128]{2,1,0:T(8,128)(2,1)S(1)} collective-permute-done((bf16[2,384,128]{2,1,0:T(8,128)(2,1)S(1)}, bf16[2,384,128]{2,1,0:T(8,128)(2,1)S(1)}, u32[]{:S(2)}, u32[]{:S(2)}) %collective-permute-start.15) | collective-permute-done | bytes 196640 | tf_op jit(solution)/shard_map/ppermute | solution.py:138
  71.0 1.2 %collective-permute-start.18 = (bf16[2,384,128]{2,1,0:T(8,128)(2,1)S(1)}, bf16[2,384,128]{2,1,0:T(8,128)(2,1)S(1)}, u32[]{:S(2)}, u32[]{:S(2)}) collective-permute-start(bf16[2,384,128]{2,1,0:T(8,128)(2,1)S(1)} %collective-permute-done.15.refs_8_), channel_id=1, source_target_pairs={{0,16},{16,0},{1,17},{17,1},{2,18},{18,2},{3,19},{19,3},{4,20},{20... | collective-permute-start | bytes 589832 | tf_op jit(solution)/shard_map/ppermute | solution.py:138
  73.0 1.5 %collective-permute-start.21 = (bf16[512,384]{1,0:T(8,128)(2,1)S(1)}, bf16[512,384]{1,0:T(8,128)(2,1)S(1)}, u32[]{:S(2)}, u32[]{:S(2)}) collective-permute-start(bf16[512,384]{1,0:T(8,128)(2,1)S(1)} %shard_map.58.refs_0_), channel_id=1, source_target_pairs={{0,2},{1,3},{2,0},{3,1},{4,6},{5,7},{6,4},{7,5},{8,10},{9,11},{10,... | collective-permute-start | bytes 1179656 | tf_op jit(solution)/shard_map/ppermute | solution.py:138
  74.5 2.2 %collective-permute-done.18.refs_9_ = bf16[2,384,128]{2,1,0:T(8,128)(2,1)S(1)} collective-permute-done((bf16[2,384,128]{2,1,0:T(8,128)(2,1)S(1)}, bf16[2,384,128]{2,1,0:T(8,128)(2,1)S(1)}, u32[]{:S(2)}, u32[]{:S(2)}) %collective-permute-start.18) | collective-permute-done | bytes 196640 | tf_op jit(solution)/shard_map/ppermute | solution.py:138
  76.7 1.6 %shard_map.67 = bf16[512,512]{1,0:T(8,128)(2,1)S(1)} custom-call(s32[2]{0:T(128)S(1)} %pad_add_fusion.1.at_ref, bf16[512,384]{1,0:T(8,128)(2,1)S(1)} %shard_map.55.refs_0_, bf16[512,384]{1,0:T(8,128)(2,1)S(1)} %collective-permute-done.19.refs_1_, bf16[512,384]{1,0:T(8,128)(2,1)S(1)} %collective-permute-done.16.refs_2_, ...), custom_call_target="tpu_custom_call" | custom-call | bytes 3145728 | tf_op jit(solution)/shard_map/pallas_call | solution.py:97
  78.7 5.4 %collective-permute-done.21.refs_2_ = bf16[512,384]{1,0:T(8,128)(2,1)S(1)} collective-permute-done((bf16[512,384]{1,0:T(8,128)(2,1)S(1)}, bf16[512,384]{1,0:T(8,128)(2,1)S(1)}, u32[]{:S(2)}, u32[]{:S(2)}) %collective-permute-start.21) | collective-permute-done | bytes 393248 | tf_op jit(solution)/shard_map/ppermute | solution.py:138
  84.5 1.2 %collective-permute-done.22.refs_1_ = bf16[512,384]{1,0:T(8,128)(2,1)S(1)} collective-permute-done((bf16[512,384]{1,0:T(8,128)(2,1)S(1)}, bf16[512,384]{1,0:T(8,128)(2,1)S(1)}, u32[]{:S(2)}, u32[]{:S(2)}) %collective-permute-start.22) | collective-permute-done | bytes 393248 | tf_op jit(solution)/shard_map/ppermute | solution.py:138
  86.3 1.6 %shard_map.66.mine_ref = f32[512,512]{1,0:T(8,128)S(1)} custom-call(s32[2]{0:T(128)S(1)} %pad_add_fusion.1.at_ref, bf16[512,384]{1,0:T(8,128)(2,1)S(1)} %shard_map.58.refs_0_, bf16[512,384]{1,0:T(8,128)(2,1)S(1)} %collective-permute-done.22.refs_1_, bf16[512,384]{1,0:T(8,128)(2,1)S(1)} %collective-permute-done.21.refs_2_, ...), custom_call_target="tpu_custom_call" | custom-call | bytes 3145728 | tf_op jit(solution)/shard_map/pallas_call | solution.py:97
  87.9 3.0 %collective-permute-done.24.theirs_ref = bf16[512,512]{1,0:T(8,128)(2,1)S(1)} collective-permute-done((bf16[512,512]{1,0:T(8,128)(2,1)S(1)}, bf16[512,512]{1,0:T(8,128)(2,1)S(1)}, u32[]{:S(2)}, u32[]{:S(2)}) %collective-permute-start.24) | collective-permute-done | bytes 524320 | tf_op jit(solution)/shard_map/ppermute | solution.py:138
  90.9 1.0 %shard_map.69 = bf16[512,512]{1,0:T(8,128)(2,1)} custom-call(s32[1]{0:T(128)} %bitcast.9.at_ref, f32[512,512]{1,0:T(8,128)S(1)} %shard_map.66.mine_ref, bf16[512,512]{1,0:T(8,128)(2,1)S(1)} %collective-permute-done.24.theirs_ref), custom_call_target="tpu_custom_call" | custom-call | tf_op jit(solution)/shard_map/pallas_call | solution.py:115
  (67 shorter events, 7.1 us)
Async XLA Ops:
  0.0 8.5 %copy-start.5 = (bf16[512,768]{1,0:T(8,128)(2,1)S(1)}, bf16[512,768]{1,0:T(8,128)(2,1)}, u32[]{:S(2)}) copy-start(bf16[512,768]{1,0:T(8,128)(2,1)} %param.6) | copy-start | bytes 2359300
  0.0 9.8 %collective-permute-start.1 = (bf16[512,512]{1,0:T(8,128)(2,1)}, bf16[512,512]{1,0:T(8,128)(2,1)S(1)}, u32[]{:S(2)}, u32[]{:S(2)}) collective-permute-start(bf16[512,512]{1,0:T(8,128)(2,1)} %refs_0_), channel_id=1, source_target_pairs={{0,1},{1,0},{2,3},{3,2},{4,5},{5,4},{6,7},{7,6},{8,9},{9,8},{10,11... | collective-permute-start | bytes 1572872 | tf_op jit(solution)/shard_map/ppermute | solution.py:138
  0.5 15.4 %collective-permute-start = (bf16[512,512]{1,0:T(8,128)(2,1)}, bf16[512,512]{1,0:T(8,128)(2,1)}, u32[]{:S(2)}, u32[]{:S(2)}) collective-permute-start(bf16[512,512]{1,0:T(8,128)(2,1)} %refs_0_), channel_id=1, source_target_pairs={{0,2},{1,3},{2,0},{3,1},{4,6},{5,7},{6,4},{7,5},{8,10},{9,11},{10,... | collective-permute-start | bytes 1572872 | tf_op jit(solution)/shard_map/ppermute | solution.py:138
  3.0 23.5 %collective-permute-start.2 = (bf16[512,512]{1,0:T(8,128)(2,1)}, bf16[512,512]{1,0:T(8,128)(2,1)}, u32[]{:S(2)}, u32[]{:S(2)}) collective-permute-start(bf16[512,512]{1,0:T(8,128)(2,1)} %refs_0_), channel_id=1, source_target_pairs={{0,4},{4,0},{8,12},{12,8},{1,5},{5,1},{9,13},{13,9},{2,6},{6,2},{1... | collective-permute-start | bytes 1572872 | tf_op jit(solution)/shard_map/ppermute | solution.py:138
  5.8 19.7 %collective-permute-start.3 = (bf16[512,384]{1,0:T(8,128)(2,1)S(1)}, bf16[512,384]{1,0:T(8,128)(2,1)S(1)}, u32[]{:S(2)}, u32[]{:S(2)}) collective-permute-start(bf16[512,384]{1,0:T(8,128)(2,1)S(1)} %dynamic-slice_select_fusion.2.refs_4_), channel_id=1, source_target_pairs={{0,8},{4,12},{8,0},{12,4},{1,9},{5,13},{9,1},{13,5},{2,10},{6,14},... | collective-permute-start | bytes 1179656 | tf_op jit(solution)/shard_map/ppermute | solution.py:138
  15.9 10.7 %copy-start.6 = (bf16[3072,128]{1,0:T(8,128)(2,1)S(1)}, bf16[3072,128]{1,0:T(8,128)(2,1)}, u32[]{:S(2)}) copy-start(bf16[3072,128]{1,0:T(8,128)(2,1)} %param.7) | copy-start | bytes 2359300
  15.9 18.2 %collective-permute-start.4 = (bf16[512,384]{1,0:T(8,128)(2,1)S(1)}, bf16[512,384]{1,0:T(8,128)(2,1)S(1)}, u32[]{:S(2)}, u32[]{:S(2)}) collective-permute-start(bf16[512,384]{1,0:T(8,128)(2,1)S(1)} %get-tuple-element.84), channel_id=1, source_target_pairs={{0,4},{4,0},{8,12},{12,8},{1,5},{5,1},{9,13},{13,9},{2,6},{6,2},{1... | collective-permute-start | bytes 1179656 | tf_op jit(solution)/shard_map/ppermute | solution.py:138
  26.5 16.3 %collective-permute-start.7 = (bf16[512,512]{1,0:T(8,128)(2,1)}, bf16[512,512]{1,0:T(8,128)(2,1)S(1)}, u32[]{:S(2)}, u32[]{:S(2)}) collective-permute-start(bf16[512,512]{1,0:T(8,128)(2,1)} %collective-permute-done.refs_2_), channel_id=1, source_target_pairs={{0,1},{1,0},{2,3},{3,2},{4,5},{5,4},{6,7},{7,6},{8,9},{9,8},{10,11... | collective-permute-start | bytes 1572872 | tf_op jit(solution)/shard_map/ppermute | solution.py:138
  26.5 16.3 %collective-permute-start.5 = (bf16[512,512]{1,0:T(8,128)(2,1)}, bf16[512,512]{1,0:T(8,128)(2,1)}, u32[]{:S(2)}, u32[]{:S(2)}) collective-permute-start(bf16[512,512]{1,0:T(8,128)(2,1)} %collective-permute-done.2.refs_0_), channel_id=1, source_target_pairs={{0,2},{1,3},{2,0},{3,1},{4,6},{5,7},{6,4},{7,5},{8,10},{9,11},{10,... | collective-permute-start | bytes 1572872 | tf_op jit(solution)/shard_map/ppermute | solution.py:138
  26.7 18.0 %collective-permute-start.8 = (bf16[512,384]{1,0:T(8,128)(2,1)S(1)}, bf16[512,384]{1,0:T(8,128)(2,1)S(1)}, u32[]{:S(2)}, u32[]{:S(2)}) collective-permute-start(bf16[512,384]{1,0:T(8,128)(2,1)S(1)} %get-tuple-element.84), channel_id=1, source_target_pairs={{0,12},{4,8},{8,4},{12,0},{1,13},{5,9},{9,5},{13,1},{2,14},{6,10},... | collective-permute-start | bytes 1179656 | tf_op jit(solution)/shard_map/ppermute | solution.py:138
  30.8 12.0 %collective-permute-start.6 = (bf16[512,384]{1,0:T(8,128)(2,1)S(1)}, bf16[512,384]{1,0:T(8,128)(2,1)S(1)}, u32[]{:S(2)}, u32[]{:S(2)}) collective-permute-start(bf16[512,384]{1,0:T(8,128)(2,1)S(1)} %collective-permute-done.3.refs_6_), channel_id=1, source_target_pairs={{0,16},{16,0},{1,17},{17,1},{2,18},{18,2},{3,19},{19,3},{4,20},{20... | collective-permute-start | bytes 1179656 | tf_op jit(solution)/shard_map/ppermute | solution.py:138
  34.1 17.1 %collective-permute-start.9 = (bf16[512,384]{1,0:T(8,128)(2,1)S(1)}, bf16[512,384]{1,0:T(8,128)(2,1)S(1)}, u32[]{:S(2)}, u32[]{:S(2)}) collective-permute-start(bf16[512,384]{1,0:T(8,128)(2,1)S(1)} %collective-permute-done.4.refs_5_), channel_id=1, source_target_pairs={{0,16},{16,0},{1,17},{17,1},{2,18},{18,2},{3,19},{19,3},{4,20},{20... | collective-permute-start | bytes 1179656 | tf_op jit(solution)/shard_map/ppermute | solution.py:138
  44.6 12.2 %collective-permute-start.10 = (bf16[512,512]{1,0:T(8,128)(2,1)}, bf16[512,512]{1,0:T(8,128)(2,1)}, u32[]{:S(2)}, u32[]{:S(2)}) collective-permute-start(bf16[512,512]{1,0:T(8,128)(2,1)} %collective-permute-done.2.refs_0_), channel_id=1, source_target_pairs={{0,1},{1,0},{2,3},{3,2},{4,5},{5,4},{6,7},{7,6},{8,9},{9,8},{10,11... | collective-permute-start | bytes 1572872 | tf_op jit(solution)/shard_map/ppermute | solution.py:138
  44.6 12.2 %collective-permute-start.11 = (bf16[512,512]{1,0:T(8,128)(2,1)}, bf16[512,512]{1,0:T(8,128)(2,1)}, u32[]{:S(2)}, u32[]{:S(2)}) collective-permute-start(bf16[512,512]{1,0:T(8,128)(2,1)} %collective-permute-done.5.refs_2_), channel_id=1, source_target_pairs={{0,1},{1,0},{2,3},{3,2},{4,5},{5,4},{6,7},{7,6},{8,9},{9,8},{10,11... | collective-permute-start | bytes 1572872 | tf_op jit(solution)/shard_map/ppermute | solution.py:138
  45.1 6.1 %copy-start.8 = (bf16[2,384,128]{2,1,0:T(8,128)(2,1)S(1)}, bf16[2,384,128]{2,1,0:T(8,128)(2,1)}, u32[]{:S(2)}) copy-start(bf16[2,384,128]{2,1,0:T(8,128)(2,1)} %get-tuple-element.104) | copy-start | bytes 589828
  45.1 13.5 %collective-permute-start.12 = (bf16[512,384]{1,0:T(8,128)(2,1)S(1)}, bf16[512,384]{1,0:T(8,128)(2,1)S(1)}, u32[]{:S(2)}, u32[]{:S(2)}) collective-permute-start(bf16[512,384]{1,0:T(8,128)(2,1)S(1)} %collective-permute-done.8.refs_7_), channel_id=1, source_target_pairs={{0,16},{16,0},{1,17},{17,1},{2,18},{18,2},{3,19},{19,3},{4,20},{20... | collective-permute-start | bytes 1179656 | tf_op jit(solution)/shard_map/ppermute | solution.py:138
  46.7 10.2 %copy-start.7 = (bf16[2,384,128]{2,1,0:T(8,128)(2,1)S(1)}, bf16[2,384,128]{2,1,0:T(8,128)(2,1)}, u32[]{:S(2)}) copy-start(bf16[2,384,128]{2,1,0:T(8,128)(2,1)} %get-tuple-element.107) | copy-start | bytes 589828
  51.2 12.6 %collective-permute-start.13 = (bf16[2,384,128]{2,1,0:T(8,128)(2,1)S(1)}, bf16[2,384,128]{2,1,0:T(8,128)(2,1)S(1)}, u32[]{:S(2)}, u32[]{:S(2)}) collective-permute-start(bf16[2,384,128]{2,1,0:T(8,128)(2,1)S(1)} %copy-done.8), channel_id=1, source_target_pairs={{0,8},{4,12},{8,0},{12,4},{1,9},{5,13},{9,1},{13,5},{2,10},{6,14},... | collective-permute-start | bytes 589832 | tf_op jit(solution)/shard_map/ppermute | solution.py:138
  51.3 17.2 %collective-permute-start.14 = (bf16[4,384,128]{2,1,0:T(8,128)(2,1)S(1)}, bf16[4,384,128]{2,1,0:T(8,128)(2,1)S(1)}, u32[]{:S(2)}, u32[]{:S(2)}) collective-permute-start(bf16[4,384,128]{2,1,0:T(8,128)(2,1)S(1)} %bitcast.26), channel_id=1, source_target_pairs={{0,4},{4,0},{8,12},{12,8},{1,5},{5,1},{9,13},{13,9},{2,6},{6,2},{1... | collective-permute-start | bytes 1179656 | tf_op jit(solution)/shard_map/ppermute | solution.py:138
  56.9 14.1 %collective-permute-start.15 = (bf16[2,384,128]{2,1,0:T(8,128)(2,1)S(1)}, bf16[2,384,128]{2,1,0:T(8,128)(2,1)S(1)}, u32[]{:S(2)}, u32[]{:S(2)}) collective-permute-start(bf16[2,384,128]{2,1,0:T(8,128)(2,1)S(1)} %copy-done.7), channel_id=1, source_target_pairs={{0,12},{4,8},{8,4},{12,0},{1,13},{5,9},{9,5},{13,1},{2,14},{6,10},... | collective-permute-start | bytes 589832 | tf_op jit(solution)/shard_map/ppermute | solution.py:138
  58.6 6.7 %copy-start = (bf16[512,512]{1,0:T(8,128)(2,1)S(1)}, bf16[512,512]{1,0:T(8,128)(2,1)}, u32[]{:S(2)}) copy-start(bf16[512,512]{1,0:T(8,128)(2,1)} %refs_0_) | copy-start | bytes 1572868
  58.6 6.7 %copy-start.2 = (bf16[512,512]{1,0:T(8,128)(2,1)S(1)}, bf16[512,512]{1,0:T(8,128)(2,1)}, u32[]{:S(2)}) copy-start(bf16[512,512]{1,0:T(8,128)(2,1)} %copy-done.1) | copy-start | bytes 1572868
  58.6 6.7 %copy-start.4 = (bf16[512,512]{1,0:T(8,128)(2,1)S(1)}, bf16[512,512]{1,0:T(8,128)(2,1)}, u32[]{:S(2)}) copy-start(bf16[512,512]{1,0:T(8,128)(2,1)} %copy-done.3) | copy-start | bytes 1572868
  62.2 10.2 %collective-permute-start.16 = (bf16[512,384]{1,0:T(8,128)(2,1)S(1)}, bf16[512,384]{1,0:T(8,128)(2,1)S(1)}, u32[]{:S(2)}, u32[]{:S(2)}) collective-permute-start(bf16[512,384]{1,0:T(8,128)(2,1)S(1)} %shard_map.55.refs_0_), channel_id=1, source_target_pairs={{0,2},{1,3},{2,0},{3,1},{4,6},{5,7},{6,4},{7,5},{8,10},{9,11},{10,... | collective-permute-start | bytes 1179656 | tf_op jit(solution)/shard_map/ppermute | solution.py:138
  63.8 10.7 %collective-permute-start.17 = (bf16[2,384,128]{2,1,0:T(8,128)(2,1)S(1)}, bf16[2,384,128]{2,1,0:T(8,128)(2,1)S(1)}, u32[]{:S(2)}, u32[]{:S(2)}) collective-permute-start(bf16[2,384,128]{2,1,0:T(8,128)(2,1)S(1)} %collective-permute-done.13.refs_6_), channel_id=1, source_target_pairs={{0,16},{16,0},{1,17},{17,1},{2,18},{18,2},{3,19},{19,3},{4,20},{20... | collective-permute-start | bytes 589832 | tf_op jit(solution)/shard_map/ppermute | solution.py:138
  71.0 5.7 %collective-permute-start.18 = (bf16[2,384,128]{2,1,0:T(8,128)(2,1)S(1)}, bf16[2,384,128]{2,1,0:T(8,128)(2,1)S(1)}, u32[]{:S(2)}, u32[]{:S(2)}) collective-permute-start(bf16[2,384,128]{2,1,0:T(8,128)(2,1)S(1)} %collective-permute-done.15.refs_8_), channel_id=1, source_target_pairs={{0,16},{16,0},{1,17},{17,1},{2,18},{18,2},{3,19},{19,3},{4,20},{20... | collective-permute-start | bytes 589832 | tf_op jit(solution)/shard_map/ppermute | solution.py:138
  72.4 4.3 %collective-permute-start.19 = (bf16[512,384]{1,0:T(8,128)(2,1)S(1)}, bf16[512,384]{1,0:T(8,128)(2,1)S(1)}, u32[]{:S(2)}, u32[]{:S(2)}) collective-permute-start(bf16[512,384]{1,0:T(8,128)(2,1)S(1)} %shard_map.55.refs_0_), channel_id=1, source_target_pairs={{0,1},{1,0},{2,3},{3,2},{4,5},{5,4},{6,7},{7,6},{8,9},{9,8},{10,11... | collective-permute-start | bytes 1179656 | tf_op jit(solution)/shard_map/ppermute | solution.py:138
  72.4 4.3 %collective-permute-start.20 = (bf16[512,384]{1,0:T(8,128)(2,1)S(1)}, bf16[512,384]{1,0:T(8,128)(2,1)S(1)}, u32[]{:S(2)}, u32[]{:S(2)}) collective-permute-start(bf16[512,384]{1,0:T(8,128)(2,1)S(1)} %collective-permute-done.16.refs_2_), channel_id=1, source_target_pairs={{0,1},{1,0},{2,3},{3,2},{4,5},{5,4},{6,7},{7,6},{8,9},{9,8},{10,11... | collective-permute-start | bytes 1179656 | tf_op jit(solution)/shard_map/ppermute | solution.py:138
  73.0 11.0 %collective-permute-start.21 = (bf16[512,384]{1,0:T(8,128)(2,1)S(1)}, bf16[512,384]{1,0:T(8,128)(2,1)S(1)}, u32[]{:S(2)}, u32[]{:S(2)}) collective-permute-start(bf16[512,384]{1,0:T(8,128)(2,1)S(1)} %shard_map.58.refs_0_), channel_id=1, source_target_pairs={{0,2},{1,3},{2,0},{3,1},{4,6},{5,7},{6,4},{7,5},{8,10},{9,11},{10,... | collective-permute-start | bytes 1179656 | tf_op jit(solution)/shard_map/ppermute | solution.py:138
  78.2 12.6 %collective-permute-start.24 = (bf16[512,512]{1,0:T(8,128)(2,1)S(1)}, bf16[512,512]{1,0:T(8,128)(2,1)S(1)}, u32[]{:S(2)}, u32[]{:S(2)}) collective-permute-start(bf16[512,512]{1,0:T(8,128)(2,1)S(1)} %shard_map.67), channel_id=1, source_target_pairs={{0,4},{4,0},{8,12},{12,8},{1,5},{5,1},{9,13},{13,9},{2,6},{6,2},{1... | collective-permute-start | bytes 1572872 | tf_op jit(solution)/shard_map/ppermute | solution.py:138
  84.0 1.7 %collective-permute-start.22 = (bf16[512,384]{1,0:T(8,128)(2,1)S(1)}, bf16[512,384]{1,0:T(8,128)(2,1)S(1)}, u32[]{:S(2)}, u32[]{:S(2)}) collective-permute-start(bf16[512,384]{1,0:T(8,128)(2,1)S(1)} %shard_map.58.refs_0_), channel_id=1, source_target_pairs={{0,1},{1,0},{2,3},{3,2},{4,5},{5,4},{6,7},{7,6},{8,9},{9,8},{10,11... | collective-permute-start | bytes 1179656 | tf_op jit(solution)/shard_map/ppermute | solution.py:138
  84.0 2.3 %collective-permute-start.23 = (bf16[512,384]{1,0:T(8,128)(2,1)S(1)}, bf16[512,384]{1,0:T(8,128)(2,1)S(1)}, u32[]{:S(2)}, u32[]{:S(2)}) collective-permute-start(bf16[512,384]{1,0:T(8,128)(2,1)S(1)} %collective-permute-done.21.refs_2_), channel_id=1, source_target_pairs={{0,1},{1,0},{2,3},{3,2},{4,5},{5,4},{6,7},{7,6},{8,9},{9,8},{10,11... | collective-permute-start | bytes 1179656 | tf_op jit(solution)/shard_map/ppermute | solution.py:138
  (2 other events, 1.6 us)

commit v5 on v4

--- a/solution.py
+++ b/solution.py
@@ -11,6 +11,59 @@
 BF16 = jnp.bfloat16
 VMEM = pl.BlockSpec(memory_space=pltpu.VMEM)
 SMEM = pl.BlockSpec(memory_space=pltpu.SMEM)
+ANY = pl.BlockSpec(memory_space=pl.ANY)
+
+TRANSFERS = dict(
+    tokens_x=("tokens", "weight", 2),
+    tokens_core=("tokens", "weight", 1),
+    tokens_x_core=("tokens_x", "weight", 1),
+    pair=("tokens", "batch", 1),
+    pair_x=("pair", "weight", 2),
+    pair_core=("pair", "weight", 1),
+    pair_x_core=("pair_x", "weight", 1),
+    direct_1=("send_other", "batch", 1),
+    direct_2=("send_own", "batch", 2),
+    direct_3=("send_other", "batch", 3),
+    swapped_1=("direct_1", "groups", 1),
+    swapped_2=("direct_2", "groups", 1),
+    swapped_3=("direct_3", "groups", 1),
+    down_1=("down_other", "batch", 1),
+    down_2=("down_send_2", "batch", 2),
+    down_3=("down_send_3", "batch", 3),
+    down_swapped_2=("down_2", "groups", 1),
+    down_swapped_3=("down_3", "groups", 1),
+    hidden_pair_x=("hidden_pair", "weight", 2),
+    hidden_pair_core=("hidden_pair", "weight", 1),
+    hidden_pair_x_core=("hidden_pair_x", "weight", 1),
+    hidden_own_x=("hidden_own", "weight", 2),
+    hidden_own_core=("hidden_own", "weight", 1),
+    hidden_own_x_core=("hidden_own_x", "weight", 1),
+    theirs=("part", "batch", 1),
+)
+PARTS = ("keep_own", "down_own", "down_other", "down_send_2", "down_send_3")
+LATE = ("hidden_pair", "hidden_own", "part")
+STAGES = (
+    ((), ("tokens_x", "pair", "tokens_core"), None),
+    (("gate_weight", "up_weight"), ("direct_2",), 0),
+    (("tokens_x", "tokens_core"), ("direct_1",), 500),
+    (("pair", "direct_2"), ("direct_3", "swapped_2", "pair_x", "tokens_x_core"), 500),
+    (("direct_1", *PARTS), ("swapped_1",), 2600),
+    (("pair_x", "swapped_2", "tokens_x_core"), (), 500),
+    (("direct_3",), ("swapped_3", "pair_core", "pair_x_core"), 500),
+    (("swapped_1",), ("down_1", "down_2"), 2000),
+    (("pair_core", "pair_x_core"), ("down_3",), 500),
+    (("swapped_3",), ("hidden_pair_x",), 0),
+    (("hidden_pair",), (), 0),
+    (("down_2",), ("down_swapped_2",), 500),
+    (("down_1", "down_3", "hidden_own"), ("down_swapped_3",), 4500),
+    (("hidden_pair_x",), ("hidden_pair_core", "hidden_pair_x_core", "hidden_own_x"), 500),
+    (("down_swapped_2",), (), 500),
+    (("down_swapped_3",), (), 3000),
+    (("hidden_pair_core", "hidden_pair_x_core"), ("theirs",), 500),
+    (("hidden_own_x",), ("hidden_own_core", "hidden_own_x_core"), 500),
+    (("hidden_own_core", "hidden_own_x_core"), (), 500),
+    (("mine", "theirs"), (), 500),
+)
 
 
 def dot(a, b):
@@ -25,17 +78,12 @@
     return pl.pallas_call(
         nothing,
         out_shape=jax.ShapeDtypeStruct((8, 128), F32),
-        in_specs=[pl.BlockSpec(memory_space=pl.ANY)],
-        out_specs=pl.BlockSpec(memory_space=pl.ANY),
+        in_specs=[ANY],
+        out_specs=ANY,
         input_output_aliases={0: 0},
         cost_estimate=pl.CostEstimate(flops=cost, bytes_accessed=8192, transcendentals=0),
         compiler_params=pltpu.CompilerParams(has_side_effects=True, vmem_limit_bytes=2**16),
     )(token)
-
-
-def stage(token, *values, cost=5 * 10**8):
-    token, *values = lax.optimization_barrier((token, *values))
-    return span(token, cost), *values
 
 
 def hidden_kernel(tile, at_ref, *refs):
@@ -125,13 +173,11 @@
     n_batch, n_weight = sizes["batch"], sizes["weight"]
     plane = lax.axis_index("batch")
     place = lax.axis_index("weight")
-    group = lax.axis_index("groups")
-    first = group == 0
+    first = lax.axis_index("groups") == 0
     parity = plane % 2
     even = parity == 0
-    rows, features = tokens.shape
-    depth, units = gate_weight.shape
-    half = units // 2
+    rows = tokens.shape[0]
+    half = gate_weight.shape[1] // 2
     columns = down_weight.shape[1]
 
     def flip(x, axis, bits):
@@ -140,71 +186,65 @@
     def half_of(weight, parity):
         return lax.dynamic_slice_in_dim(weight, parity * half, half, axis=1)
 
-    down_blocks = down_weight.reshape(n_weight, 2, half, columns)
+    def one_of(mine, theirs, parity):
+        return jnp.where(first, half_of(mine, parity), half_of(theirs, parity))
 
     if n_batch == n_weight == 4:
-        send_own = jnp.where(first, half_of(gate_weight, parity), half_of(up_weight, parity))
+        have = dict(tokens=tokens, gate_weight=gate_weight, up_weight=up_weight)
+        have["send_own"] = one_of(gate_weight, up_weight, parity)
+        blocks = down_weight.reshape(n_weight, 2, half, columns)
+        low, high = slice(0, n_weight // 2), slice(n_weight // 2, n_weight)
+
+        def names(kind):
+            return [have[f"{kind}_{j}"] for j in (1, 2, 3)]
+
+        def hidden(kind):
+            at = jnp.stack([place ^ plane, jnp.where(first, 1, 0)]).astype(jnp.int32)
+            tokens = [have[kind], have[f"{kind}_core"], have[f"{kind}_x"], have[f"{kind}_x_core"]]
+            direct = [have["send_own"], *names("direct")]
+            return hidden_of(at, tokens, direct, [have["keep_own"], *names("swapped")])
+
+        def output(kind, type):
+            at = jnp.stack([place, place ^ jnp.where(first, 0, 2)]).astype(jnp.int32)
+            kind = f"hidden_{kind}"
+            hidden = [have[kind], have[f"{kind}_core"], have[f"{kind}_x"], have[f"{kind}_x_core"]]
+            down = [have["down_own"], have["down_1"]]
+            for j in (2, 3):
+                down += [have[f"down_{j}"], have[f"down_swapped_{j}"]]
+            return output_of(at, hidden, down, type)
+
+        results = dict(
+            send_other=lambda: one_of(have["gate_weight"], have["up_weight"], 1 - parity),
+            keep_own=lambda: one_of(have["up_weight"], have["gate_weight"], parity),
+            down_own=lambda: jnp.where(even, blocks[:, 0], blocks[:, 1]),
+            down_other=lambda: jnp.where(even, blocks[:, 1], blocks[:, 0]),
+            down_send_2=lambda: jnp.where(first, get("down_own")[low], get("down_own")[high]),
+            down_send_3=lambda: jnp.where(first, get("down_other")[low], get("down_other")[high]),
+            hidden_pair=lambda: hidden("pair"),
+            hidden_own=lambda: hidden("tokens"),
+            part=lambda: output("pair", BF16),
+            mine=lambda: output("own", F32),
+        )
+
+        def get(name):
+            if name not in have:
+                have[name] = results[name]()
+            return have[name]
+
         token = jnp.zeros((8, 128), F32)
-        tokens_x = flip(tokens, "weight", 2)
-        tokens_pair = flip(tokens, "batch", 1)
-        tokens_core = flip(tokens, "weight", 1)
-        token, gate_weight, up_weight, send_own = stage(token, gate_weight, up_weight, send_own, cost=0)
-        direct_2 = flip(send_own, "batch", 2)
-        send_other = jnp.where(first, half_of(gate_weight, 1 - parity), half_of(up_weight, 1 - parity))
-        keep_own = jnp.where(first, half_of(up_weight, parity), half_of(gate_weight, parity))
-        low, high = slice(0, n_weight // 2), slice(n_weight // 2, n_weight)
-        down_own = jnp.where(even, down_blocks[:, 0], down_blocks[:, 1])
-        down_other = jnp.where(even, down_blocks[:, 1], down_blocks[:, 0])
-        down_send_2 = jnp.where(first, down_own[low], down_own[high])
-        down_send_3 = jnp.where(first, down_other[low], down_other[high])
-        token, tokens_x, tokens_core, send_other = stage(token, tokens_x, tokens_core, send_other)
-        direct_1 = flip(send_other, "batch", 1)
-        token, tokens_pair, direct_2, send_other, tokens_x = stage(token, tokens_pair, direct_2, send_other, tokens_x)
-        direct_3 = flip(send_other, "batch", 3)
-        swapped_2 = flip(direct_2, "groups", 1)
-        tokens_pair_x = flip(tokens_pair, "weight", 2)
-        tokens_x_core = flip(tokens_x, "weight", 1)
-        token, direct_1, keep_own, down_own, down_other, down_send_2, down_send_3 = stage(
-            token, direct_1, keep_own, down_own, down_other, down_send_2, down_send_3, cost=2 * 10**9
-        )
-        swapped_1 = flip(direct_1, "groups", 1)
-        token, tokens_pair_x, swapped_2, tokens_x_core = stage(token, tokens_pair_x, swapped_2, tokens_x_core)
-        token, direct_3, x, y = stage(token, direct_3, tokens_pair, tokens_pair_x)
-        swapped_3 = flip(direct_3, "groups", 1)
-        pair_core = [flip(x, "weight", 1), flip(y, "weight", 1)]
-        token, swapped_1, x, y = stage(token, swapped_1, down_other, down_send_2, cost=2 * 10**9)
-        down_1 = flip(x, "batch", 1)
-        down_2 = flip(y, "batch", 2)
-        token, x, *pair_core = stage(token, down_send_3, *pair_core)
-        down_3 = flip(x, "batch", 3)
-        token, swapped_3 = stage(token, swapped_3, cost=0)
-        at = jnp.stack([place ^ plane, jnp.where(first, 1, 0)]).astype(jnp.int32)
-        direct = [send_own, direct_1, direct_2, direct_3]
-        swapped = [keep_own, swapped_1, swapped_2, swapped_3]
-        hidden_pair = hidden_of(at, [tokens_pair, pair_core[0], tokens_pair_x, pair_core[1]], direct, swapped)
-        far_pair = flip(hidden_pair, "weight", 2)
-        token, hidden_pair = stage(token, hidden_pair, cost=0)
-        token, down_2, x = stage(token, down_2, tokens)
-        swapped_down_2 = flip(down_2, "groups", 1)
-        hidden_own = hidden_of(at, [x, tokens_core, tokens_x, tokens_x_core], direct, swapped)
-        token, down_1, down_3, hidden_own = stage(token, down_1, down_3, hidden_own, cost=45 * 10**8)
-        swapped_down_3 = flip(down_3, "groups", 1)
-        token, far_pair, hidden_pair = stage(token, far_pair, hidden_pair)
-        core_pair = [flip(x, "weight", 1) for x in (hidden_pair, far_pair)]
-        far_own = flip(hidden_own, "weight", 2)
-        token, swapped_down_2 = stage(token, swapped_down_2)
-        token, swapped_down_3 = stage(token, swapped_down_3, cost=3 * 10**9)
-        token, *core_pair = stage(token, *core_pair)
-        at = jnp.stack([place, place ^ jnp.where(first, 0, 2)]).astype(jnp.int32)
-        down = [down_own, down_1, down_2, swapped_down_2, down_3, swapped_down_3]
-        part = output_of(at, [hidden_pair, core_pair[0], far_pair, core_pair[1]], down, BF16)
-        theirs = flip(part, "batch", 1)
-        token, far_own, x = stage(token, far_own, hidden_own)
-        core_own = [flip(x, "weight", 1) for x in (x, far_own)]
-        token, *core_own = stage(token, *core_own)
-        mine = output_of(at, [hidden_own, core_own[0], far_own, core_own[1]], down, F32)
-        token, mine, theirs = stage(token, mine, theirs)
-        return add(plane.astype(jnp.int32).reshape(1), columns, mine, theirs)
+        for arrived, leaving, cost in STAGES:
+            sent = [TRANSFERS[name][0] for name in leaving]
+            held = dict.fromkeys((*arrived, *sent))
+            held = {name: get(name) for name in held if name in arrived or name not in LATE}
+            if cost is not None:
+                token, *values = lax.optimization_barrier((token, *held.values()))
+                held = dict(zip(held, values))
+                have.update((name, held[name]) for name in arrived)
+                token = span(token, cost * 10**6)
+            for name in leaving:
+                source, *way = TRANSFERS[name]
+                have[name] = flip(held[source] if source in held else get(source), *way)
+        return add(plane.astype(jnp.int32).reshape(1), columns, have["mine"], have["theirs"])
 
     tokens_pair = flip(tokens, "batch", 1)
     both = lax.all_gather(jnp.concatenate([tokens_pair, tokens], axis=0), "weight", axis=1, tiled=True)

time: 92.1 us -> 90.4 us (0.982)
  transfers between devices with their start and end apart: 25 -> 25, of which waited for: 15 -> 14; matrix products, arithmetic and copies ran while one was open for 4% -> 4% of each run, Pallas kernels for 11% -> 11%
where the time goes in v5:
time: 90.4 us; the launch traced here: 90.2 us
  waiting for transfers between devices  43.9 us (49%)
  starting transfers between devices  30.8 us (34%)
  Pallas kernels  10.9 us (12%)
  other arithmetic  3.63 us (4%)
    ppermute x25, waiting for transfers between devices, flip(): return lax.ppermute(x, axis, [(i, i ^ bits) for i in range(sizes[axis])])  43.9 us
    ppermute x25, starting transfers between devices, flip(): return lax.ppermute(x, axis, [(i, i ^ bits) for i in range(sizes[axis])])  30.8 us
    pallas_call x2, Pallas kernels, hidden_of(): pl.pallas_call(functools.partial(hidden_kernel, rows // 2), out_shape=jax...  6.79 us
    pallas_call x2, Pallas kernels, output_of(): pl.pallas_call(output_kernel, out_shape=jax.ShapeDtypeStruct((hidden[0].s...  3.11 us
    select_n x2, other arithmetic, one_of(): return jnp.where(first, half_of(mine, parity), half_of(theirs, parity))  2.62 us
  transfers between devices with their start and end apart: 25, of which 14 were waited for; matrix products, arithmetic and copies ran while one was open for 4% of the time, Pallas kernels for 11%

profile of v5, /device:TPU:0, one launch (start us, length us, event | category | flops | bytes accessed | tf_op | source)
XLA Modules:
  0.0 90.2 jit_solution(7857808963692487350)
XLA Ops:
  0.5 2.5 %collective-permute-start = (bf16[512,512]{1,0:T(8,128)(2,1)}, bf16[512,512]{1,0:T(8,128)(2,1)}, u32[]{:S(2)}, u32[]{:S(2)}) collective-permute-start(bf16[512,512]{1,0:T(8,128)(2,1)} %refs_0_.1), channel_id=1, source_target_pairs={{0,2},{1,3},{2,0},{3,1},{4,6},{5,7},{6,4},{7,5},{8,10},{9,11},{10,... | collective-permute-start | bytes 1572872 | tf_op jit(solution)/shard_map/ppermute | solution.py:184
  3.0 1.6 %collective-permute-start.2 = (bf16[512,512]{1,0:T(8,128)(2,1)}, bf16[512,512]{1,0:T(8,128)(2,1)}, u32[]{:S(2)}, u32[]{:S(2)}) collective-permute-start(bf16[512,512]{1,0:T(8,128)(2,1)} %refs_0_.1), channel_id=1, source_target_pairs={{0,4},{4,0},{8,12},{12,8},{1,5},{5,1},{9,13},{13,9},{2,6},{6,2},{1... | collective-permute-start | bytes 1572872 | tf_op jit(solution)/shard_map/ppermute | solution.py:184
  4.6 1.2 %dynamic-slice_select_fusion.2.refs_4_ = bf16[512,384]{1,0:T(8,128)(2,1)S(1)} fusion(bf16[512,768]{1,0:T(8,128)(2,1)} %param.6, s32[]{:T(128)S(6)} %select_n.80, bf16[512,768]{1,0:T(8,128)(2,1)} %param.5, pred[]{:T(512)S(6)} %eq.8), kind=kLoop, calls=%fused_computation.4 | loop fusion | flops 196608 | bytes 1179653 | tf_op jit(solution)/shard_map/jit(_where)/select_n | solution.py:190
  5.8 2.7 %collective-permute-start.3 = (bf16[512,384]{1,0:T(8,128)(2,1)S(1)}, bf16[512,384]{1,0:T(8,128)(2,1)S(1)}, u32[]{:S(2)}, u32[]{:S(2)}) collective-permute-start(bf16[512,384]{1,0:T(8,128)(2,1)S(1)} %dynamic-slice_select_fusion.2.refs_4_), channel_id=1, source_target_pairs={{0,8},{4,12},{8,0},{12,4},{1,9},{5,13},{9,1},{13,5},{2,10},{6,14},... | collective-permute-start | bytes 1179656 | tf_op jit(solution)/shard_map/ppermute | solution.py:184
  8.5 1.4 %dynamic-slice_select_fusion = (bf16[512,384]{1,0:T(8,128)(2,1)S(1)}, bf16[512,384]{1,0:T(8,128)(2,1)S(1)}) fusion(bf16[512,768]{1,0:T(8,128)(2,1)} %param.5, s32[]{:T(128)S(6)} %select_n.80, bf16[512,768]{1,0:T(8,128)(2,1)S(1)} %copy-done.5, pred[]{:T(512)S(6)} %eq.8, s32[]{:T(128)S(6)} %select_n.82), kind=kLoop, calls=%fused_computation.2 | loop fusion | flops 393216 | bytes 2359305 | tf_op jit(solution)/shard_map/jit(_where)/select_n | solution.py:190
  10.7 5.2 %collective-permute-done.refs_2_ = bf16[512,512]{1,0:T(8,128)(2,1)} collective-permute-done((bf16[512,512]{1,0:T(8,128)(2,1)}, bf16[512,512]{1,0:T(8,128)(2,1)}, u32[]{:S(2)}, u32[]{:S(2)}) %collective-permute-start) | collective-permute-done | bytes 524320 | tf_op jit(solution)/shard_map/ppermute | solution.py:184
  15.9 1.8 %collective-permute-start.4 = (bf16[512,384]{1,0:T(8,128)(2,1)S(1)}, bf16[512,384]{1,0:T(8,128)(2,1)S(1)}, u32[]{:S(2)}, u32[]{:S(2)}) collective-permute-start(bf16[512,384]{1,0:T(8,128)(2,1)S(1)} %get-tuple-element.81), channel_id=1, source_target_pairs={{0,4},{4,0},{8,12},{12,8},{1,5},{5,1},{9,13},{13,9},{2,6},{6,2},{1... | collective-permute-start | bytes 1179656 | tf_op jit(solution)/shard_map/ppermute | solution.py:184
  17.8 7.8 %collective-permute-done.3.refs_6_ = bf16[512,384]{1,0:T(8,128)(2,1)S(1)} collective-permute-done((bf16[512,384]{1,0:T(8,128)(2,1)S(1)}, bf16[512,384]{1,0:T(8,128)(2,1)S(1)}, u32[]{:S(2)}, u32[]{:S(2)}) %collective-permute-start.3) | collective-permute-done | bytes 393248 | tf_op jit(solution)/shard_map/ppermute | solution.py:184
  25.5 1.0 %collective-permute-done.2.refs_0_ = bf16[512,512]{1,0:T(8,128)(2,1)} collective-permute-done((bf16[512,512]{1,0:T(8,128)(2,1)}, bf16[512,512]{1,0:T(8,128)(2,1)}, u32[]{:S(2)}, u32[]{:S(2)}) %collective-permute-start.2) | collective-permute-done | bytes 524320 | tf_op jit(solution)/shard_map/ppermute | solution.py:184
  26.5 3.6 %collective-permute-start.8 = (bf16[512,384]{1,0:T(8,128)(2,1)S(1)}, bf16[512,384]{1,0:T(8,128)(2,1)S(1)}, u32[]{:S(2)}, u32[]{:S(2)}) collective-permute-start(bf16[512,384]{1,0:T(8,128)(2,1)S(1)} %get-tuple-element.81), channel_id=1, source_target_pairs={{0,12},{4,8},{8,4},{12,0},{1,13},{5,9},{9,5},{13,1},{2,14},{6,10},... | collective-permute-start | bytes 1179656 | tf_op jit(solution)/shard_map/ppermute | solution.py:184
  30.1 1.5 %collective-permute-start.6 = (bf16[512,384]{1,0:T(8,128)(2,1)S(1)}, bf16[512,384]{1,0:T(8,128)(2,1)S(1)}, u32[]{:S(2)}, u32[]{:S(2)}) collective-permute-start(bf16[512,384]{1,0:T(8,128)(2,1)S(1)} %collective-permute-done.3.refs_6_), channel_id=1, source_target_pairs={{0,16},{16,0},{1,17},{17,1},{2,18},{18,2},{3,19},{19,3},{4,20},{20... | collective-permute-start | bytes 1179656 | tf_op jit(solution)/shard_map/ppermute | solution.py:184
  32.2 0.8 fusion
  33.0 1.1 %collective-permute-done.4.refs_5_ = bf16[512,384]{1,0:T(8,128)(2,1)S(1)} collective-permute-done((bf16[512,384]{1,0:T(8,128)(2,1)S(1)}, bf16[512,384]{1,0:T(8,128)(2,1)S(1)}, u32[]{:S(2)}, u32[]{:S(2)}) %collective-permute-start.4) | collective-permute-done | bytes 393248 | tf_op jit(solution)/shard_map/ppermute | solution.py:184
  34.1 1.5 %collective-permute-start.9 = (bf16[512,384]{1,0:T(8,128)(2,1)S(1)}, bf16[512,384]{1,0:T(8,128)(2,1)S(1)}, u32[]{:S(2)}, u32[]{:S(2)}) collective-permute-start(bf16[512,384]{1,0:T(8,128)(2,1)S(1)} %collective-permute-done.4.refs_5_), channel_id=1, source_target_pairs={{0,16},{16,0},{1,17},{17,1},{2,18},{18,2},{3,19},{19,3},{4,20},{20... | collective-permute-start | bytes 1179656 | tf_op jit(solution)/shard_map/ppermute | solution.py:184
  35.6 6.6 %collective-permute-done.6.refs_10_ = bf16[512,384]{1,0:T(8,128)(2,1)S(1)} collective-permute-done((bf16[512,384]{1,0:T(8,128)(2,1)S(1)}, bf16[512,384]{1,0:T(8,128)(2,1)S(1)}, u32[]{:S(2)}, u32[]{:S(2)}) %collective-permute-start.6) | collective-permute-done | bytes 393248 | tf_op jit(solution)/shard_map/ppermute | solution.py:184
  42.2 4.1 %collective-permute-done.5.refs_2_ = bf16[512,512]{1,0:T(8,128)(2,1)} collective-permute-done((bf16[512,512]{1,0:T(8,128)(2,1)}, bf16[512,512]{1,0:T(8,128)(2,1)}, u32[]{:S(2)}, u32[]{:S(2)}) %collective-permute-start.5) | collective-permute-done | bytes 524320 | tf_op jit(solution)/shard_map/ppermute | solution.py:184
  47.9 1.2 %collective-permute-start.13 = (bf16[2,384,128]{2,1,0:T(8,128)(2,1)S(1)}, bf16[2,384,128]{2,1,0:T(8,128)(2,1)S(1)}, u32[]{:S(2)}, u32[]{:S(2)}) collective-permute-start(bf16[2,384,128]{2,1,0:T(8,128)(2,1)S(1)} %copy-done.8), channel_id=1, source_target_pairs={{0,8},{4,12},{8,0},{12,4},{1,9},{5,13},{9,1},{13,5},{2,10},{6,14},... | collective-permute-start | bytes 589832 | tf_op jit(solution)/shard_map/ppermute | solution.py:184
  49.0 7.8 %collective-permute-start.14 = (bf16[4,384,128]{2,1,0:T(8,128)(2,1)S(1)}, bf16[4,384,128]{2,1,0:T(8,128)(2,1)S(1)}, u32[]{:S(2)}, u32[]{:S(2)}) collective-permute-start(bf16[4,384,128]{2,1,0:T(8,128)(2,1)S(1)} %bitcast.26), channel_id=1, source_target_pairs={{0,4},{4,0},{8,12},{12,8},{1,5},{5,1},{9,13},{13,9},{2,6},{6,2},{1... | collective-permute-start | bytes 1179656 | tf_op jit(solution)/shard_map/ppermute | solution.py:184
  57.0 0.9 collective-permute-done.12.refs_11_
  57.9 3.6 %shard_map.55.refs_0_ = bf16[512,384]{1,0:T(8,128)(2,1)S(1)} custom-call(s32[2]{0:T(128)S(1)} %pad_add_fusion.at_ref, bf16[512,512]{1,0:T(8,128)(2,1)} %collective-permute-done.2.refs_0_, bf16[512,512]{1,0:T(8,128)(2,1)} %collective-permute-done.10.refs_1_, bf16[512,512]{1,0:T(8,128)(2,1)} %collective-permute-done.5.refs_2_, ...), custom_call_target="tpu_custom_call" | custom-call | bytes 5242880 | tf_op jit(solution)/shard_map/pallas_call | solution.py:112
  62.1 1.6 %collective-permute-start.17 = (bf16[2,384,128]{2,1,0:T(8,128)(2,1)S(1)}, bf16[2,384,128]{2,1,0:T(8,128)(2,1)S(1)}, u32[]{:S(2)}, u32[]{:S(2)}) collective-permute-start(bf16[2,384,128]{2,1,0:T(8,128)(2,1)S(1)} %collective-permute-done.13.refs_6_), channel_id=1, source_target_pairs={{0,16},{16,0},{1,17},{17,1},{2,18},{18,2},{3,19},{19,3},{4,20},{20... | collective-permute-start | bytes 589832 | tf_op jit(solution)/shard_map/ppermute | solution.py:184
  63.8 3.2 %shard_map.58.refs_0_ = bf16[512,384]{1,0:T(8,128)(2,1)S(1)} custom-call(s32[2]{0:T(128)S(1)} %pad_add_fusion.at_ref, bf16[512,512]{1,0:T(8,128)(2,1)S(1)} %copy-done, bf16[512,512]{1,0:T(8,128)(2,1)S(1)} %copy-done.2, bf16[512,512]{1,0:T(8,128)(2,1)} %collective-permute-done.refs_2_, bf16[512,512]{1,0:T(8,128)(2,1)S(1)} %copy-done.4, ...), custom_call_target="tpu_custom_call" | custom-call | bytes 5242880 | tf_op jit(solution)/shard_map/pallas_call | solution.py:112
  67.0 1.7 %collective-permute-done.15.refs_8_ = bf16[2,384,128]{2,1,0:T(8,128)(2,1)S(1)} collective-permute-done((bf16[2,384,128]{2,1,0:T(8,128)(2,1)S(1)}, bf16[2,384,128]{2,1,0:T(8,128)(2,1)S(1)}, u32[]{:S(2)}, u32[]{:S(2)}) %collective-permute-start.15) | collective-permute-done | bytes 196640 | tf_op jit(solution)/shard_map/ppermute | solution.py:184
  68.7 1.1 %collective-permute-start.18 = (bf16[2,384,128]{2,1,0:T(8,128)(2,1)S(1)}, bf16[2,384,128]{2,1,0:T(8,128)(2,1)S(1)}, u32[]{:S(2)}, u32[]{:S(2)}) collective-permute-start(bf16[2,384,128]{2,1,0:T(8,128)(2,1)S(1)} %collective-permute-done.15.refs_8_), channel_id=1, source_target_pairs={{0,16},{16,0},{1,17},{17,1},{2,18},{18,2},{3,19},{19,3},{4,20},{20... | collective-permute-start | bytes 589832 | tf_op jit(solution)/shard_map/ppermute | solution.py:184
  69.9 2.0 %collective-permute-done.16.refs_2_ = bf16[512,384]{1,0:T(8,128)(2,1)S(1)} collective-permute-done((bf16[512,384]{1,0:T(8,128)(2,1)S(1)}, bf16[512,384]{1,0:T(8,128)(2,1)S(1)}, u32[]{:S(2)}, u32[]{:S(2)}) %collective-permute-start.16) | collective-permute-done | bytes 393248 | tf_op jit(solution)/shard_map/ppermute | solution.py:184
  72.5 1.9 %collective-permute-done.18.refs_9_ = bf16[2,384,128]{2,1,0:T(8,128)(2,1)S(1)} collective-permute-done((bf16[2,384,128]{2,1,0:T(8,128)(2,1)S(1)}, bf16[2,384,128]{2,1,0:T(8,128)(2,1)S(1)}, u32[]{:S(2)}, u32[]{:S(2)}) %collective-permute-start.18) | collective-permute-done | bytes 196640 | tf_op jit(solution)/shard_map/ppermute | solution.py:184
  74.4 1.6 %shard_map.67 = bf16[512,512]{1,0:T(8,128)(2,1)S(1)} custom-call(s32[2]{0:T(128)S(1)} %pad_add_fusion.1.at_ref, bf16[512,384]{1,0:T(8,128)(2,1)S(1)} %shard_map.55.refs_0_, bf16[512,384]{1,0:T(8,128)(2,1)S(1)} %collective-permute-done.19.refs_1_, bf16[512,384]{1,0:T(8,128)(2,1)S(1)} %collective-permute-done.16.refs_2_, ...), custom_call_target="tpu_custom_call" | custom-call | bytes 3145728 | tf_op jit(solution)/shard_map/pallas_call | solution.py:145
  76.6 6.9 %collective-permute-done.21.refs_2_ = bf16[512,384]{1,0:T(8,128)(2,1)S(1)} collective-permute-done((bf16[512,384]{1,0:T(8,128)(2,1)S(1)}, bf16[512,384]{1,0:T(8,128)(2,1)S(1)}, u32[]{:S(2)}, u32[]{:S(2)}) %collective-permute-start.21) | collective-permute-done | bytes 393248 | tf_op jit(solution)/shard_map/ppermute | solution.py:184
  83.5 1.7 %collective-permute-done.23.refs_3_ = bf16[512,384]{1,0:T(8,128)(2,1)S(1)} collective-permute-done((bf16[512,384]{1,0:T(8,128)(2,1)S(1)}, bf16[512,384]{1,0:T(8,128)(2,1)S(1)}, u32[]{:S(2)}, u32[]{:S(2)}) %collective-permute-start.23) | collective-permute-done | bytes 393248 | tf_op jit(solution)/shard_map/ppermute | solution.py:184
  85.2 1.6 %shard_map.66.mine_ref = f32[512,512]{1,0:T(8,128)S(1)} custom-call(s32[2]{0:T(128)S(1)} %pad_add_fusion.1.at_ref, bf16[512,384]{1,0:T(8,128)(2,1)S(1)} %shard_map.58.refs_0_, bf16[512,384]{1,0:T(8,128)(2,1)S(1)} %collective-permute-done.22.refs_1_, bf16[512,384]{1,0:T(8,128)(2,1)S(1)} %collective-permute-done.21.refs_2_, ...), custom_call_target="tpu_custom_call" | custom-call | bytes 3145728 | tf_op jit(solution)/shard_map/pallas_call | solution.py:145
  86.8 2.4 %collective-permute-done.24.theirs_ref = bf16[512,512]{1,0:T(8,128)(2,1)S(1)} collective-permute-done((bf16[512,512]{1,0:T(8,128)(2,1)S(1)}, bf16[512,512]{1,0:T(8,128)(2,1)S(1)}, u32[]{:S(2)}, u32[]{:S(2)}) %collective-permute-start.24) | collective-permute-done | bytes 524320 | tf_op jit(solution)/shard_map/ppermute | solution.py:184
  89.2 1.0 %shard_map.69 = bf16[512,512]{1,0:T(8,128)(2,1)} custom-call(s32[1]{0:T(128)} %bitcast.9.at_ref, f32[512,512]{1,0:T(8,128)S(1)} %shard_map.66.mine_ref, bf16[512,512]{1,0:T(8,128)(2,1)S(1)} %collective-permute-done.24.theirs_ref), custom_call_target="tpu_custom_call" | custom-call | tf_op jit(solution)/shard_map/pallas_call | solution.py:163
  (67 shorter events, 5.4 us)
Async XLA Ops:
  0.0 8.5 %copy-start.5 = (bf16[512,768]{1,0:T(8,128)(2,1)S(1)}, bf16[512,768]{1,0:T(8,128)(2,1)}, u32[]{:S(2)}) copy-start(bf16[512,768]{1,0:T(8,128)(2,1)} %param.6) | copy-start | bytes 2359300
  0.0 9.9 %collective-permute-start.1 = (bf16[512,512]{1,0:T(8,128)(2,1)}, bf16[512,512]{1,0:T(8,128)(2,1)S(1)}, u32[]{:S(2)}, u32[]{:S(2)}) collective-permute-start(bf16[512,512]{1,0:T(8,128)(2,1)} %refs_0_.1), channel_id=1, source_target_pairs={{0,1},{1,0},{2,3},{3,2},{4,5},{5,4},{6,7},{7,6},{8,9},{9,8},{10,11... | collective-permute-start | bytes 1572872 | tf_op jit(solution)/shard_map/ppermute | solution.py:184
  0.5 15.4 %collective-permute-start = (bf16[512,512]{1,0:T(8,128)(2,1)}, bf16[512,512]{1,0:T(8,128)(2,1)}, u32[]{:S(2)}, u32[]{:S(2)}) collective-permute-start(bf16[512,512]{1,0:T(8,128)(2,1)} %refs_0_.1), channel_id=1, source_target_pairs={{0,2},{1,3},{2,0},{3,1},{4,6},{5,7},{6,4},{7,5},{8,10},{9,11},{10,... | collective-permute-start | bytes 1572872 | tf_op jit(solution)/shard_map/ppermute | solution.py:184
  3.0 23.5 %collective-permute-start.2 = (bf16[512,512]{1,0:T(8,128)(2,1)}, bf16[512,512]{1,0:T(8,128)(2,1)}, u32[]{:S(2)}, u32[]{:S(2)}) collective-permute-start(bf16[512,512]{1,0:T(8,128)(2,1)} %refs_0_.1), channel_id=1, source_target_pairs={{0,4},{4,0},{8,12},{12,8},{1,5},{5,1},{9,13},{13,9},{2,6},{6,2},{1... | collective-permute-start | bytes 1572872 | tf_op jit(solution)/shard_map/ppermute | solution.py:184
  5.8 19.7 %collective-permute-start.3 = (bf16[512,384]{1,0:T(8,128)(2,1)S(1)}, bf16[512,384]{1,0:T(8,128)(2,1)S(1)}, u32[]{:S(2)}, u32[]{:S(2)}) collective-permute-start(bf16[512,384]{1,0:T(8,128)(2,1)S(1)} %dynamic-slice_select_fusion.2.refs_4_), channel_id=1, source_target_pairs={{0,8},{4,12},{8,0},{12,4},{1,9},{5,13},{9,1},{13,5},{2,10},{6,14},... | collective-permute-start | bytes 1179656 | tf_op jit(solution)/shard_map/ppermute | solution.py:184
  8.5 9.2 %copy-start.6 = (bf16[3072,128]{1,0:T(8,128)(2,1)S(1)}, bf16[3072,128]{1,0:T(8,128)(2,1)}, u32[]{:S(2)}) copy-start(bf16[3072,128]{1,0:T(8,128)(2,1)} %param.7) | copy-start | bytes 2359300
  15.9 18.2 %collective-permute-start.4 = (bf16[512,384]{1,0:T(8,128)(2,1)S(1)}, bf16[512,384]{1,0:T(8,128)(2,1)S(1)}, u32[]{:S(2)}, u32[]{:S(2)}) collective-permute-start(bf16[512,384]{1,0:T(8,128)(2,1)S(1)} %get-tuple-element.81), channel_id=1, source_target_pairs={{0,4},{4,0},{8,12},{12,8},{1,5},{5,1},{9,13},{13,9},{2,6},{6,2},{1... | collective-permute-start | bytes 1179656 | tf_op jit(solution)/shard_map/ppermute | solution.py:184
  26.5 19.8 %collective-permute-start.8 = (bf16[512,384]{1,0:T(8,128)(2,1)S(1)}, bf16[512,384]{1,0:T(8,128)(2,1)S(1)}, u32[]{:S(2)}, u32[]{:S(2)}) collective-permute-start(bf16[512,384]{1,0:T(8,128)(2,1)S(1)} %get-tuple-element.81), channel_id=1, source_target_pairs={{0,12},{4,8},{8,4},{12,0},{1,13},{5,9},{9,5},{13,1},{2,14},{6,10},... | collective-permute-start | bytes 1179656 | tf_op jit(solution)/shard_map/ppermute | solution.py:184
  30.1 12.1 %collective-permute-start.6 = (bf16[512,384]{1,0:T(8,128)(2,1)S(1)}, bf16[512,384]{1,0:T(8,128)(2,1)S(1)}, u32[]{:S(2)}, u32[]{:S(2)}) collective-permute-start(bf16[512,384]{1,0:T(8,128)(2,1)S(1)} %collective-permute-done.3.refs_6_), channel_id=1, source_target_pairs={{0,16},{16,0},{1,17},{17,1},{2,18},{18,2},{3,19},{19,3},{4,20},{20... | collective-permute-start | bytes 1179656 | tf_op jit(solution)/shard_map/ppermute | solution.py:184
  31.6 10.5 %collective-permute-start.7 = (bf16[512,512]{1,0:T(8,128)(2,1)}, bf16[512,512]{1,0:T(8,128)(2,1)S(1)}, u32[]{:S(2)}, u32[]{:S(2)}) collective-permute-start(bf16[512,512]{1,0:T(8,128)(2,1)} %collective-permute-done.refs_2_), channel_id=1, source_target_pairs={{0,1},{1,0},{2,3},{3,2},{4,5},{5,4},{6,7},{7,6},{8,9},{9,8},{10,11... | collective-permute-start | bytes 1572872 | tf_op jit(solution)/shard_map/ppermute | solution.py:184
  31.6 14.7 %collective-permute-start.5 = (bf16[512,512]{1,0:T(8,128)(2,1)}, bf16[512,512]{1,0:T(8,128)(2,1)}, u32[]{:S(2)}, u32[]{:S(2)}) collective-permute-start(bf16[512,512]{1,0:T(8,128)(2,1)} %collective-permute-done.2.refs_0_), channel_id=1, source_target_pairs={{0,2},{1,3},{2,0},{3,1},{4,6},{5,7},{6,4},{7,5},{8,10},{9,11},{10,... | collective-permute-start | bytes 1572872 | tf_op jit(solution)/shard_map/ppermute | solution.py:184
  34.1 13.8 %collective-permute-start.9 = (bf16[512,384]{1,0:T(8,128)(2,1)S(1)}, bf16[512,384]{1,0:T(8,128)(2,1)S(1)}, u32[]{:S(2)}, u32[]{:S(2)}) collective-permute-start(bf16[512,384]{1,0:T(8,128)(2,1)S(1)} %collective-permute-done.4.refs_5_), channel_id=1, source_target_pairs={{0,16},{16,0},{1,17},{17,1},{2,18},{18,2},{3,19},{19,3},{4,20},{20... | collective-permute-start | bytes 1179656 | tf_op jit(solution)/shard_map/ppermute | solution.py:184
  42.2 4.1 %copy-start.3 = (bf16[512,512]{1,0:T(8,128)(2,1)}, bf16[512,512]{1,0:T(8,128)(2,1)S(1)}, u32[]{:S(2)}) copy-start(bf16[512,512]{1,0:T(8,128)(2,1)S(1)} %collective-permute-done.7.refs_3_) | copy-start | bytes 1572868
  46.3 10.6 %collective-permute-start.10 = (bf16[512,512]{1,0:T(8,128)(2,1)}, bf16[512,512]{1,0:T(8,128)(2,1)}, u32[]{:S(2)}, u32[]{:S(2)}) collective-permute-start(bf16[512,512]{1,0:T(8,128)(2,1)} %collective-permute-done.2.refs_0_), channel_id=1, source_target_pairs={{0,1},{1,0},{2,3},{3,2},{4,5},{5,4},{6,7},{7,6},{8,9},{9,8},{10,11... | collective-permute-start | bytes 1572872 | tf_op jit(solution)/shard_map/ppermute | solution.py:184
  46.3 10.6 %collective-permute-start.11 = (bf16[512,512]{1,0:T(8,128)(2,1)}, bf16[512,512]{1,0:T(8,128)(2,1)}, u32[]{:S(2)}, u32[]{:S(2)}) collective-permute-start(bf16[512,512]{1,0:T(8,128)(2,1)} %collective-permute-done.5.refs_2_), channel_id=1, source_target_pairs={{0,1},{1,0},{2,3},{3,2},{4,5},{5,4},{6,7},{7,6},{8,9},{9,8},{10,11... | collective-permute-start | bytes 1572872 | tf_op jit(solution)/shard_map/ppermute | solution.py:184
  46.8 11.1 %collective-permute-start.12 = (bf16[512,384]{1,0:T(8,128)(2,1)S(1)}, bf16[512,384]{1,0:T(8,128)(2,1)S(1)}, u32[]{:S(2)}, u32[]{:S(2)}) collective-permute-start(bf16[512,384]{1,0:T(8,128)(2,1)S(1)} %collective-permute-done.8.refs_7_), channel_id=1, source_target_pairs={{0,16},{16,0},{1,17},{17,1},{2,18},{18,2},{3,19},{19,3},{4,20},{20... | collective-permute-start | bytes 1179656 | tf_op jit(solution)/shard_map/ppermute | solution.py:184
  47.3 9.5 %copy-start.7 = (bf16[2,384,128]{2,1,0:T(8,128)(2,1)S(1)}, bf16[2,384,128]{2,1,0:T(8,128)(2,1)}, u32[]{:S(2)}) copy-start(bf16[2,384,128]{2,1,0:T(8,128)(2,1)} %get-tuple-element.104) | copy-start | bytes 589828
  47.9 14.3 %collective-permute-start.13 = (bf16[2,384,128]{2,1,0:T(8,128)(2,1)S(1)}, bf16[2,384,128]{2,1,0:T(8,128)(2,1)S(1)}, u32[]{:S(2)}, u32[]{:S(2)}) collective-permute-start(bf16[2,384,128]{2,1,0:T(8,128)(2,1)S(1)} %copy-done.8), channel_id=1, source_target_pairs={{0,8},{4,12},{8,0},{12,4},{1,9},{5,13},{9,1},{13,5},{2,10},{6,14},... | collective-permute-start | bytes 589832 | tf_op jit(solution)/shard_map/ppermute | solution.py:184
  49.0 18.0 %collective-permute-start.14 = (bf16[4,384,128]{2,1,0:T(8,128)(2,1)S(1)}, bf16[4,384,128]{2,1,0:T(8,128)(2,1)S(1)}, u32[]{:S(2)}, u32[]{:S(2)}) collective-permute-start(bf16[4,384,128]{2,1,0:T(8,128)(2,1)S(1)} %bitcast.26), channel_id=1, source_target_pairs={{0,4},{4,0},{8,12},{12,8},{1,5},{5,1},{9,13},{13,9},{2,6},{6,2},{1... | collective-permute-start | bytes 1179656 | tf_op jit(solution)/shard_map/ppermute | solution.py:184
  56.9 11.9 %collective-permute-start.15 = (bf16[2,384,128]{2,1,0:T(8,128)(2,1)S(1)}, bf16[2,384,128]{2,1,0:T(8,128)(2,1)S(1)}, u32[]{:S(2)}, u32[]{:S(2)}) collective-permute-start(bf16[2,384,128]{2,1,0:T(8,128)(2,1)S(1)} %copy-done.7), channel_id=1, source_target_pairs={{0,12},{4,8},{8,4},{12,0},{1,13},{5,9},{9,5},{13,1},{2,14},{6,10},... | collective-permute-start | bytes 589832 | tf_op jit(solution)/shard_map/ppermute | solution.py:184
  57.9 5.9 %copy-start = (bf16[512,512]{1,0:T(8,128)(2,1)S(1)}, bf16[512,512]{1,0:T(8,128)(2,1)}, u32[]{:S(2)}) copy-start(bf16[512,512]{1,0:T(8,128)(2,1)} %refs_0_.1) | copy-start | bytes 1572868
  57.9 5.9 %copy-start.2 = (bf16[512,512]{1,0:T(8,128)(2,1)S(1)}, bf16[512,512]{1,0:T(8,128)(2,1)}, u32[]{:S(2)}) copy-start(bf16[512,512]{1,0:T(8,128)(2,1)} %copy-done.1) | copy-start | bytes 1572868
  57.9 5.9 %copy-start.4 = (bf16[512,512]{1,0:T(8,128)(2,1)S(1)}, bf16[512,512]{1,0:T(8,128)(2,1)}, u32[]{:S(2)}) copy-start(bf16[512,512]{1,0:T(8,128)(2,1)} %copy-done.3) | copy-start | bytes 1572868
  61.6 10.3 %collective-permute-start.16 = (bf16[512,384]{1,0:T(8,128)(2,1)S(1)}, bf16[512,384]{1,0:T(8,128)(2,1)S(1)}, u32[]{:S(2)}, u32[]{:S(2)}) collective-permute-start(bf16[512,384]{1,0:T(8,128)(2,1)S(1)} %shard_map.55.refs_0_), channel_id=1, source_target_pairs={{0,2},{1,3},{2,0},{3,1},{4,6},{5,7},{6,4},{7,5},{8,10},{9,11},{10,... | collective-permute-start | bytes 1179656 | tf_op jit(solution)/shard_map/ppermute | solution.py:184
  62.1 10.3 %collective-permute-start.17 = (bf16[2,384,128]{2,1,0:T(8,128)(2,1)S(1)}, bf16[2,384,128]{2,1,0:T(8,128)(2,1)S(1)}, u32[]{:S(2)}, u32[]{:S(2)}) collective-permute-start(bf16[2,384,128]{2,1,0:T(8,128)(2,1)S(1)} %collective-permute-done.13.refs_6_), channel_id=1, source_target_pairs={{0,16},{16,0},{1,17},{17,1},{2,18},{18,2},{3,19},{19,3},{4,20},{20... | collective-permute-start | bytes 589832 | tf_op jit(solution)/shard_map/ppermute | solution.py:184
  63.8 10.6 %collective-permute-start.19 = (bf16[512,384]{1,0:T(8,128)(2,1)S(1)}, bf16[512,384]{1,0:T(8,128)(2,1)S(1)}, u32[]{:S(2)}, u32[]{:S(2)}) collective-permute-start(bf16[512,384]{1,0:T(8,128)(2,1)S(1)} %shard_map.55.refs_0_), channel_id=1, source_target_pairs={{0,1},{1,0},{2,3},{3,2},{4,5},{5,4},{6,7},{7,6},{8,9},{9,8},{10,11... | collective-permute-start | bytes 1179656 | tf_op jit(solution)/shard_map/ppermute | solution.py:184
  68.7 5.7 %collective-permute-start.18 = (bf16[2,384,128]{2,1,0:T(8,128)(2,1)S(1)}, bf16[2,384,128]{2,1,0:T(8,128)(2,1)S(1)}, u32[]{:S(2)}, u32[]{:S(2)}) collective-permute-start(bf16[2,384,128]{2,1,0:T(8,128)(2,1)S(1)} %collective-permute-done.15.refs_8_), channel_id=1, source_target_pairs={{0,16},{16,0},{1,17},{17,1},{2,18},{18,2},{3,19},{19,3},{4,20},{20... | collective-permute-start | bytes 589832 | tf_op jit(solution)/shard_map/ppermute | solution.py:184
  71.9 2.5 %collective-permute-start.20 = (bf16[512,384]{1,0:T(8,128)(2,1)S(1)}, bf16[512,384]{1,0:T(8,128)(2,1)S(1)}, u32[]{:S(2)}, u32[]{:S(2)}) collective-permute-start(bf16[512,384]{1,0:T(8,128)(2,1)S(1)} %collective-permute-done.16.refs_2_), channel_id=1, source_target_pairs={{0,1},{1,0},{2,3},{3,2},{4,5},{5,4},{6,7},{7,6},{8,9},{9,8},{10,11... | collective-permute-start | bytes 1179656 | tf_op jit(solution)/shard_map/ppermute | solution.py:184
  71.9 11.5 %collective-permute-start.21 = (bf16[512,384]{1,0:T(8,128)(2,1)S(1)}, bf16[512,384]{1,0:T(8,128)(2,1)S(1)}, u32[]{:S(2)}, u32[]{:S(2)}) collective-permute-start(bf16[512,384]{1,0:T(8,128)(2,1)S(1)} %shard_map.58.refs_0_), channel_id=1, source_target_pairs={{0,2},{1,3},{2,0},{3,1},{4,6},{5,7},{6,4},{7,5},{8,10},{9,11},{10,... | collective-permute-start | bytes 1179656 | tf_op jit(solution)/shard_map/ppermute | solution.py:184
  76.0 13.2 %collective-permute-start.24 = (bf16[512,512]{1,0:T(8,128)(2,1)S(1)}, bf16[512,512]{1,0:T(8,128)(2,1)S(1)}, u32[]{:S(2)}, u32[]{:S(2)}) collective-permute-start(bf16[512,512]{1,0:T(8,128)(2,1)S(1)} %shard_map.67), channel_id=1, source_target_pairs={{0,4},{4,0},{8,12},{12,8},{1,5},{5,1},{9,13},{13,9},{2,6},{6,2},{1... | collective-permute-start | bytes 1572872 | tf_op jit(solution)/shard_map/ppermute | solution.py:184
  76.5 6.9 %collective-permute-start.22 = (bf16[512,384]{1,0:T(8,128)(2,1)S(1)}, bf16[512,384]{1,0:T(8,128)(2,1)S(1)}, u32[]{:S(2)}, u32[]{:S(2)}) collective-permute-start(bf16[512,384]{1,0:T(8,128)(2,1)S(1)} %shard_map.58.refs_0_), channel_id=1, source_target_pairs={{0,1},{1,0},{2,3},{3,2},{4,5},{5,4},{6,7},{7,6},{8,9},{9,8},{10,11... | collective-permute-start | bytes 1179656 | tf_op jit(solution)/shard_map/ppermute | solution.py:184
  83.5 1.7 %collective-permute-start.23 = (bf16[512,384]{1,0:T(8,128)(2,1)S(1)}, bf16[512,384]{1,0:T(8,128)(2,1)S(1)}, u32[]{:S(2)}, u32[]{:S(2)}) collective-permute-start(bf16[512,384]{1,0:T(8,128)(2,1)S(1)} %collective-permute-done.21.refs_2_), channel_id=1, source_target_pairs={{0,1},{1,0},{2,3},{3,2},{4,5},{5,4},{6,7},{7,6},{8,9},{9,8},{10,11... | collective-permute-start | bytes 1179656 | tf_op jit(solution)/shard_map/ppermute | solution.py:184
  (2 other events, 1.8 us)

commit v6 on v5

--- a/solution.py
+++ b/solution.py
@@ -1,3 +1,4 @@
+import enum
 import functools
 
 import jax
@@ -13,56 +14,108 @@
 SMEM = pl.BlockSpec(memory_space=pltpu.SMEM)
 ANY = pl.BlockSpec(memory_space=pl.ANY)
 
-TRANSFERS = dict(
-    tokens_x=("tokens", "weight", 2),
-    tokens_core=("tokens", "weight", 1),
-    tokens_x_core=("tokens_x", "weight", 1),
-    pair=("tokens", "batch", 1),
-    pair_x=("pair", "weight", 2),
-    pair_core=("pair", "weight", 1),
-    pair_x_core=("pair_x", "weight", 1),
-    direct_1=("send_other", "batch", 1),
-    direct_2=("send_own", "batch", 2),
-    direct_3=("send_other", "batch", 3),
-    swapped_1=("direct_1", "groups", 1),
-    swapped_2=("direct_2", "groups", 1),
-    swapped_3=("direct_3", "groups", 1),
-    down_1=("down_other", "batch", 1),
-    down_2=("down_send_2", "batch", 2),
-    down_3=("down_send_3", "batch", 3),
-    down_swapped_2=("down_2", "groups", 1),
-    down_swapped_3=("down_3", "groups", 1),
-    hidden_pair_x=("hidden_pair", "weight", 2),
-    hidden_pair_core=("hidden_pair", "weight", 1),
-    hidden_pair_x_core=("hidden_pair_x", "weight", 1),
-    hidden_own_x=("hidden_own", "weight", 2),
-    hidden_own_core=("hidden_own", "weight", 1),
-    hidden_own_x_core=("hidden_own_x", "weight", 1),
-    theirs=("part", "batch", 1),
-)
-PARTS = ("keep_own", "down_own", "down_other", "down_send_2", "down_send_3")
-LATE = ("hidden_pair", "hidden_own", "part")
+BATCH, GROUPS, WEIGHT = "batch", "groups", "weight"
+
+
+class N(enum.Enum):
+    tokens = enum.auto()
+    gate_weight = enum.auto()
+    up_weight = enum.auto()
+    send_own = enum.auto()
+    send_other = enum.auto()
+    keep_own = enum.auto()
+    down_own = enum.auto()
+    down_other = enum.auto()
+    down_send_2 = enum.auto()
+    down_send_3 = enum.auto()
+    tokens_x = enum.auto()
+    tokens_core = enum.auto()
+    tokens_x_core = enum.auto()
+    pair = enum.auto()
+    pair_x = enum.auto()
+    pair_core = enum.auto()
+    pair_x_core = enum.auto()
+    direct_1 = enum.auto()
+    direct_2 = enum.auto()
+    direct_3 = enum.auto()
+    swapped_1 = enum.auto()
+    swapped_2 = enum.auto()
+    swapped_3 = enum.auto()
+    down_1 = enum.auto()
+    down_2 = enum.auto()
+    down_3 = enum.auto()
+    down_swapped_2 = enum.auto()
+    down_swapped_3 = enum.auto()
+    hidden_pair = enum.auto()
+    hidden_pair_x = enum.auto()
+    hidden_pair_core = enum.auto()
+    hidden_pair_x_core = enum.auto()
+    hidden_own = enum.auto()
+    hidden_own_x = enum.auto()
+    hidden_own_core = enum.auto()
+    hidden_own_x_core = enum.auto()
+    part = enum.auto()
+    mine = enum.auto()
+    theirs = enum.auto()
+
+
+TRANSFERS = {
+    N.tokens_x: (N.tokens, WEIGHT, 2),
+    N.tokens_core: (N.tokens, WEIGHT, 1),
+    N.tokens_x_core: (N.tokens_x, WEIGHT, 1),
+    N.pair: (N.tokens, BATCH, 1),
+    N.pair_x: (N.pair, WEIGHT, 2),
+    N.pair_core: (N.pair, WEIGHT, 1),
+    N.pair_x_core: (N.pair_x, WEIGHT, 1),
+    N.direct_1: (N.send_other, BATCH, 1),
+    N.direct_2: (N.send_own, BATCH, 2),
+    N.direct_3: (N.send_other, BATCH, 3),
+    N.swapped_1: (N.direct_1, GROUPS, 1),
+    N.swapped_2: (N.direct_2, GROUPS, 1),
+    N.swapped_3: (N.direct_3, GROUPS, 1),
+    N.down_1: (N.down_other, BATCH, 1),
+    N.down_2: (N.down_send_2, BATCH, 2),
+    N.down_3: (N.down_send_3, BATCH, 3),
+    N.down_swapped_2: (N.down_2, GROUPS, 1),
+    N.down_swapped_3: (N.down_3, GROUPS, 1),
+    N.hidden_pair_x: (N.hidden_pair, WEIGHT, 2),
+    N.hidden_pair_core: (N.hidden_pair, WEIGHT, 1),
+    N.hidden_pair_x_core: (N.hidden_pair_x, WEIGHT, 1),
+    N.hidden_own_x: (N.hidden_own, WEIGHT, 2),
+    N.hidden_own_core: (N.hidden_own, WEIGHT, 1),
+    N.hidden_own_x_core: (N.hidden_own_x, WEIGHT, 1),
+    N.theirs: (N.part, BATCH, 1),
+}
+PARTS = (N.keep_own, N.down_own, N.down_other, N.down_send_2, N.down_send_3)
+LATE = (N.hidden_pair, N.hidden_own, N.part)
+OWN = (N.tokens, N.tokens_core, N.tokens_x, N.tokens_x_core)
+PAIR = (N.pair, N.pair_core, N.pair_x, N.pair_x_core)
+HIDDEN_OWN = (N.hidden_own, N.hidden_own_core, N.hidden_own_x, N.hidden_own_x_core)
+HIDDEN_PAIR = (N.hidden_pair, N.hidden_pair_core, N.hidden_pair_x, N.hidden_pair_x_core)
+DIRECT = (N.send_own, N.direct_1, N.direct_2, N.direct_3)
+SWAPPED = (N.keep_own, N.swapped_1, N.swapped_2, N.swapped_3)
+DOWN = (N.down_own, N.down_1, N.down_2, N.down_swapped_2, N.down_3, N.down_swapped_3)
 STAGES = (
-    ((), ("tokens_x", "pair", "tokens_core"), None),
-    (("gate_weight", "up_weight"), ("direct_2",), 0),
-    (("tokens_x", "tokens_core"), ("direct_1",), 500),
-    (("pair", "direct_2"), ("direct_3", "swapped_2", "pair_x", "tokens_x_core"), 500),
-    (("direct_1", *PARTS), ("swapped_1",), 2600),
-    (("pair_x", "swapped_2", "tokens_x_core"), (), 500),
-    (("direct_3",), ("swapped_3", "pair_core", "pair_x_core"), 500),
-    (("swapped_1",), ("down_1", "down_2"), 2000),
-    (("pair_core", "pair_x_core"), ("down_3",), 500),
-    (("swapped_3",), ("hidden_pair_x",), 0),
-    (("hidden_pair",), (), 0),
-    (("down_2",), ("down_swapped_2",), 500),
-    (("down_1", "down_3", "hidden_own"), ("down_swapped_3",), 4500),
-    (("hidden_pair_x",), ("hidden_pair_core", "hidden_pair_x_core", "hidden_own_x"), 500),
-    (("down_swapped_2",), (), 500),
-    (("down_swapped_3",), (), 3000),
-    (("hidden_pair_core", "hidden_pair_x_core"), ("theirs",), 500),
-    (("hidden_own_x",), ("hidden_own_core", "hidden_own_x_core"), 500),
-    (("hidden_own_core", "hidden_own_x_core"), (), 500),
-    (("mine", "theirs"), (), 500),
+    ((), (N.tokens_x, N.pair, N.tokens_core), None),
+    ((N.gate_weight, N.up_weight), (N.direct_2,), 0),
+    ((N.tokens_x, N.tokens_core), (N.direct_1,), 500),
+    ((N.pair, N.direct_2), (N.direct_3, N.swapped_2, N.pair_x, N.tokens_x_core), 500),
+    ((N.direct_1, *PARTS), (N.swapped_1,), 2600),
+    ((N.pair_x, N.swapped_2, N.tokens_x_core), (), 500),
+    ((N.direct_3,), (N.swapped_3, N.pair_core, N.pair_x_core), 500),
+    ((N.swapped_1,), (N.down_1, N.down_2), 2000),
+    ((N.pair_core, N.pair_x_core), (N.down_3,), 500),
+    ((N.swapped_3,), (N.hidden_pair_x,), 0),
+    ((N.hidden_pair,), (), 0),
+    ((N.down_2,), (N.down_swapped_2,), 500),
+    ((N.down_1, N.down_3, N.hidden_own), (N.down_swapped_3,), 4500),
+    ((N.hidden_pair_x,), (N.hidden_pair_core, N.hidden_pair_x_core, N.hidden_own_x), 500),
+    ((N.down_swapped_2,), (), 500),
+    ((N.down_swapped_3,), (), 3000),
+    ((N.hidden_pair_core, N.hidden_pair_x_core), (N.theirs,), 500),
+    ((N.hidden_own_x,), (N.hidden_own_core, N.hidden_own_x_core), 500),
+    ((N.hidden_own_core, N.hidden_own_x_core), (), 500),
+    ((N.mine, N.theirs), (), 500),
 )
 
 
@@ -170,10 +223,10 @@
 
 
 def shards(sizes, tokens, gate_weight, up_weight, down_weight):
-    n_batch, n_weight = sizes["batch"], sizes["weight"]
-    plane = lax.axis_index("batch")
-    place = lax.axis_index("weight")
-    first = lax.axis_index("groups") == 0
+    n_batch, n_weight = sizes[BATCH], sizes[WEIGHT]
+    plane = lax.axis_index(BATCH)
+    place = lax.axis_index(WEIGHT)
+    first = lax.axis_index(GROUPS) == 0
     parity = plane % 2
     even = parity == 0
     rows = tokens.shape[0]
@@ -190,41 +243,34 @@
         return jnp.where(first, half_of(mine, parity), half_of(theirs, parity))
 
     if n_batch == n_weight == 4:
-        have = dict(tokens=tokens, gate_weight=gate_weight, up_weight=up_weight)
-        have["send_own"] = one_of(gate_weight, up_weight, parity)
+        have = {N.tokens: tokens, N.gate_weight: gate_weight, N.up_weight: up_weight}
+        have[N.send_own] = one_of(gate_weight, up_weight, parity)
         blocks = down_weight.reshape(n_weight, 2, half, columns)
         low, high = slice(0, n_weight // 2), slice(n_weight // 2, n_weight)
 
-        def names(kind):
-            return [have[f"{kind}_{j}"] for j in (1, 2, 3)]
-
-        def hidden(kind):
+        def every(names):
+            return [have[name] for name in names]
+
+        def hidden(tokens):
             at = jnp.stack([place ^ plane, jnp.where(first, 1, 0)]).astype(jnp.int32)
-            tokens = [have[kind], have[f"{kind}_core"], have[f"{kind}_x"], have[f"{kind}_x_core"]]
-            direct = [have["send_own"], *names("direct")]
-            return hidden_of(at, tokens, direct, [have["keep_own"], *names("swapped")])
-
-        def output(kind, type):
+            return hidden_of(at, every(tokens), every(DIRECT), every(SWAPPED))
+
+        def output(hidden, kind):
             at = jnp.stack([place, place ^ jnp.where(first, 0, 2)]).astype(jnp.int32)
-            kind = f"hidden_{kind}"
-            hidden = [have[kind], have[f"{kind}_core"], have[f"{kind}_x"], have[f"{kind}_x_core"]]
-            down = [have["down_own"], have["down_1"]]
-            for j in (2, 3):
-                down += [have[f"down_{j}"], have[f"down_swapped_{j}"]]
-            return output_of(at, hidden, down, type)
-
-        results = dict(
-            send_other=lambda: one_of(have["gate_weight"], have["up_weight"], 1 - parity),
-            keep_own=lambda: one_of(have["up_weight"], have["gate_weight"], parity),
-            down_own=lambda: jnp.where(even, blocks[:, 0], blocks[:, 1]),
-            down_other=lambda: jnp.where(even, blocks[:, 1], blocks[:, 0]),
-            down_send_2=lambda: jnp.where(first, get("down_own")[low], get("down_own")[high]),
-            down_send_3=lambda: jnp.where(first, get("down_other")[low], get("down_other")[high]),
-            hidden_pair=lambda: hidden("pair"),
-            hidden_own=lambda: hidden("tokens"),
-            part=lambda: output("pair", BF16),
-            mine=lambda: output("own", F32),
-        )
+            return output_of(at, every(hidden), every(DOWN), kind)
+
+        results = {
+            N.send_other: lambda: one_of(have[N.gate_weight], have[N.up_weight], 1 - parity),
+            N.keep_own: lambda: one_of(have[N.up_weight], have[N.gate_weight], parity),
+            N.down_own: lambda: jnp.where(even, blocks[:, 0], blocks[:, 1]),
+            N.down_other: lambda: jnp.where(even, blocks[:, 1], blocks[:, 0]),
+            N.down_send_2: lambda: jnp.where(first, get(N.down_own)[low], get(N.down_own)[high]),
+            N.down_send_3: lambda: jnp.where(first, get(N.down_other)[low], get(N.down_other)[high]),
+            N.hidden_pair: lambda: hidden(PAIR),
+            N.hidden_own: lambda: hidden(OWN),
+            N.part: lambda: output(HIDDEN_PAIR, BF16),
+            N.mine: lambda: output(HIDDEN_OWN, F32),
+        }
 
         def get(name):
             if name not in have:
@@ -244,30 +290,30 @@
             for name in leaving:
                 source, *way = TRANSFERS[name]
                 have[name] = flip(held[source] if source in held else get(source), *way)
-        return add(plane.astype(jnp.int32).reshape(1), columns, have["mine"], have["theirs"])
-
-    tokens_pair = flip(tokens, "batch", 1)
-    both = lax.all_gather(jnp.concatenate([tokens_pair, tokens], axis=0), "weight", axis=1, tiled=True)
-    mine = lax.all_gather(jnp.where(first, gate_weight, up_weight), "batch", axis=0, tiled=True)
+        return add(plane.astype(jnp.int32).reshape(1), columns, have[N.mine], have[N.theirs])
+
+    tokens_pair = flip(tokens, BATCH, 1)
+    both = lax.all_gather(jnp.concatenate([tokens_pair, tokens], axis=0), WEIGHT, axis=1, tiled=True)
+    mine = lax.all_gather(jnp.where(first, gate_weight, up_weight), BATCH, axis=0, tiled=True)
     mine = half_of(mine, parity)
-    mine, theirs = dot(both, mine), dot(both, flip(mine, "groups", 1))
+    mine, theirs = dot(both, mine), dot(both, flip(mine, GROUPS, 1))
     gate_sum, up_sum = jnp.where(first, mine, theirs), jnp.where(first, theirs, mine)
-    hidden = lax.all_gather((jax.nn.silu(gate_sum) * up_sum).astype(BF16), "weight", axis=1, tiled=True)
-    down_all = lax.all_gather(down_weight, "batch", axis=1, tiled=True)
+    hidden = lax.all_gather((jax.nn.silu(gate_sum) * up_sum).astype(BF16), WEIGHT, axis=1, tiled=True)
+    down_all = lax.all_gather(down_weight, BATCH, axis=1, tiled=True)
     down_all = down_all.reshape(n_weight, 2, half, n_batch * columns)
     down_all = jnp.where(even, down_all[:, 0], down_all[:, 1]).reshape(n_weight * half, n_batch * columns)
-    theirs = flip(dot(hidden[:rows], down_all).astype(BF16), "batch", 1)
+    theirs = flip(dot(hidden[:rows], down_all).astype(BF16), BATCH, 1)
     return (dot(hidden[rows:], down_all) + theirs).astype(BF16)
 
 
 def solution(mesh):
     in_specs = (
-        P(("groups", "batch"), "weight"),
-        P("batch", "weight"),
-        P("batch", "weight"),
-        P(None, ("weight", "batch")),
+        P((GROUPS, BATCH), WEIGHT),
+        P(BATCH, WEIGHT),
+        P(BATCH, WEIGHT),
+        P(None, (WEIGHT, BATCH)),
     )
-    out_specs = P(("groups", "batch"), "weight")
+    out_specs = P((GROUPS, BATCH), WEIGHT)
     sizes = dict(mesh.shape)
 
     def body(*args):

time: 90.4 us -> 90.4 us (level)
  no operation moved by 1% of the time
where the time goes in v6:
time: 90.4 us; the launch traced here: 90.2 us
  waiting for transfers between devices  43.9 us (49%)
  starting transfers between devices  30.8 us (34%)
  Pallas kernels  10.9 us (12%)
  other arithmetic  3.63 us (4%)
    ppermute x25, waiting for transfers between devices, flip(): return lax.ppermute(x, axis, [(i, i ^ bits) for i in range(sizes[axis])])  43.9 us
    ppermute x25, starting transfers between devices, flip(): return lax.ppermute(x, axis, [(i, i ^ bits) for i in range(sizes[axis])])  30.8 us
    pallas_call x2, Pallas kernels, hidden_of(): pl.pallas_call(functools.partial(hidden_kernel, rows // 2), out_shape=jax...  6.79 us
    pallas_call x2, Pallas kernels, output_of(): pl.pallas_call(output_kernel, out_shape=jax.ShapeDtypeStruct((hidden[0].s...  3.11 us
    select_n x2, other arithmetic, one_of(): return jnp.where(first, half_of(mine, parity), half_of(theirs, parity))  2.62 us
  transfers between devices with their start and end apart: 25, of which 14 were waited for; matrix products, arithmetic and copies ran while one was open for 4% of the time, Pallas kernels for 11%

profile of v6, /device:TPU:0, one launch (start us, length us, event | category | flops | bytes accessed | tf_op | source)
XLA Modules:
  0.0 90.2 jit_solution(7857808963692487350)
XLA Ops:
  0.5 2.5 %collective-permute-start = (bf16[512,512]{1,0:T(8,128)(2,1)}, bf16[512,512]{1,0:T(8,128)(2,1)}, u32[]{:S(2)}, u32[]{:S(2)}) collective-permute-start(bf16[512,512]{1,0:T(8,128)(2,1)} %refs_0_.1), channel_id=1, source_target_pairs={{0,2},{1,3},{2,0},{3,1},{4,6},{5,7},{6,4},{7,5},{8,10},{9,11},{10,... | collective-permute-start | bytes 1572872 | tf_op jit(solution)/shard_map/ppermute | solution.py:237
  3.0 1.6 %collective-permute-start.2 = (bf16[512,512]{1,0:T(8,128)(2,1)}, bf16[512,512]{1,0:T(8,128)(2,1)}, u32[]{:S(2)}, u32[]{:S(2)}) collective-permute-start(bf16[512,512]{1,0:T(8,128)(2,1)} %refs_0_.1), channel_id=1, source_target_pairs={{0,4},{4,0},{8,12},{12,8},{1,5},{5,1},{9,13},{13,9},{2,6},{6,2},{1... | collective-permute-start | bytes 1572872 | tf_op jit(solution)/shard_map/ppermute | solution.py:237
  4.6 1.2 %dynamic-slice_select_fusion.2.refs_4_ = bf16[512,384]{1,0:T(8,128)(2,1)S(1)} fusion(bf16[512,768]{1,0:T(8,128)(2,1)} %param.6, s32[]{:T(128)S(6)} %select_n.80, bf16[512,768]{1,0:T(8,128)(2,1)} %param.5, pred[]{:T(512)S(6)} %eq.8), kind=kLoop, calls=%fused_computation.4 | loop fusion | flops 196608 | bytes 1179653 | tf_op jit(solution)/shard_map/jit(_where)/select_n | solution.py:243
  5.8 2.7 %collective-permute-start.3 = (bf16[512,384]{1,0:T(8,128)(2,1)S(1)}, bf16[512,384]{1,0:T(8,128)(2,1)S(1)}, u32[]{:S(2)}, u32[]{:S(2)}) collective-permute-start(bf16[512,384]{1,0:T(8,128)(2,1)S(1)} %dynamic-slice_select_fusion.2.refs_4_), channel_id=1, source_target_pairs={{0,8},{4,12},{8,0},{12,4},{1,9},{5,13},{9,1},{13,5},{2,10},{6,14},... | collective-permute-start | bytes 1179656 | tf_op jit(solution)/shard_map/ppermute | solution.py:237
  8.5 1.4 %dynamic-slice_select_fusion = (bf16[512,384]{1,0:T(8,128)(2,1)S(1)}, bf16[512,384]{1,0:T(8,128)(2,1)S(1)}) fusion(bf16[512,768]{1,0:T(8,128)(2,1)} %param.5, s32[]{:T(128)S(6)} %select_n.80, bf16[512,768]{1,0:T(8,128)(2,1)S(1)} %copy-done.5, pred[]{:T(512)S(6)} %eq.8, s32[]{:T(128)S(6)} %select_n.82), kind=kLoop, calls=%fused_computation.2 | loop fusion | flops 393216 | bytes 2359305 | tf_op jit(solution)/shard_map/jit(_where)/select_n | solution.py:243
  10.7 5.2 %collective-permute-done.refs_2_ = bf16[512,512]{1,0:T(8,128)(2,1)} collective-permute-done((bf16[512,512]{1,0:T(8,128)(2,1)}, bf16[512,512]{1,0:T(8,128)(2,1)}, u32[]{:S(2)}, u32[]{:S(2)}) %collective-permute-start) | collective-permute-done | bytes 524320 | tf_op jit(solution)/shard_map/ppermute | solution.py:237
  15.9 1.8 %collective-permute-start.4 = (bf16[512,384]{1,0:T(8,128)(2,1)S(1)}, bf16[512,384]{1,0:T(8,128)(2,1)S(1)}, u32[]{:S(2)}, u32[]{:S(2)}) collective-permute-start(bf16[512,384]{1,0:T(8,128)(2,1)S(1)} %get-tuple-element.81), channel_id=1, source_target_pairs={{0,4},{4,0},{8,12},{12,8},{1,5},{5,1},{9,13},{13,9},{2,6},{6,2},{1... | collective-permute-start | bytes 1179656 | tf_op jit(solution)/shard_map/ppermute | solution.py:237
  17.8 7.8 %collective-permute-done.3.refs_6_ = bf16[512,384]{1,0:T(8,128)(2,1)S(1)} collective-permute-done((bf16[512,384]{1,0:T(8,128)(2,1)S(1)}, bf16[512,384]{1,0:T(8,128)(2,1)S(1)}, u32[]{:S(2)}, u32[]{:S(2)}) %collective-permute-start.3) | collective-permute-done | bytes 393248 | tf_op jit(solution)/shard_map/ppermute | solution.py:237
  25.5 1.0 %collective-permute-done.2.refs_0_ = bf16[512,512]{1,0:T(8,128)(2,1)} collective-permute-done((bf16[512,512]{1,0:T(8,128)(2,1)}, bf16[512,512]{1,0:T(8,128)(2,1)}, u32[]{:S(2)}, u32[]{:S(2)}) %collective-permute-start.2) | collective-permute-done | bytes 524320 | tf_op jit(solution)/shard_map/ppermute | solution.py:237
  26.5 3.6 %collective-permute-start.8 = (bf16[512,384]{1,0:T(8,128)(2,1)S(1)}, bf16[512,384]{1,0:T(8,128)(2,1)S(1)}, u32[]{:S(2)}, u32[]{:S(2)}) collective-permute-start(bf16[512,384]{1,0:T(8,128)(2,1)S(1)} %get-tuple-element.81), channel_id=1, source_target_pairs={{0,12},{4,8},{8,4},{12,0},{1,13},{5,9},{9,5},{13,1},{2,14},{6,10},... | collective-permute-start | bytes 1179656 | tf_op jit(solution)/shard_map/ppermute | solution.py:237
  30.1 1.5 %collective-permute-start.6 = (bf16[512,384]{1,0:T(8,128)(2,1)S(1)}, bf16[512,384]{1,0:T(8,128)(2,1)S(1)}, u32[]{:S(2)}, u32[]{:S(2)}) collective-permute-start(bf16[512,384]{1,0:T(8,128)(2,1)S(1)} %collective-permute-done.3.refs_6_), channel_id=1, source_target_pairs={{0,16},{16,0},{1,17},{17,1},{2,18},{18,2},{3,19},{19,3},{4,20},{20... | collective-permute-start | bytes 1179656 | tf_op jit(solution)/shard_map/ppermute | solution.py:237
  32.2 0.8 fusion
  33.0 1.1 %collective-permute-done.4.refs_5_ = bf16[512,384]{1,0:T(8,128)(2,1)S(1)} collective-permute-done((bf16[512,384]{1,0:T(8,128)(2,1)S(1)}, bf16[512,384]{1,0:T(8,128)(2,1)S(1)}, u32[]{:S(2)}, u32[]{:S(2)}) %collective-permute-start.4) | collective-permute-done | bytes 393248 | tf_op jit(solution)/shard_map/ppermute | solution.py:237
  34.1 1.5 %collective-permute-start.9 = (bf16[512,384]{1,0:T(8,128)(2,1)S(1)}, bf16[512,384]{1,0:T(8,128)(2,1)S(1)}, u32[]{:S(2)}, u32[]{:S(2)}) collective-permute-start(bf16[512,384]{1,0:T(8,128)(2,1)S(1)} %collective-permute-done.4.refs_5_), channel_id=1, source_target_pairs={{0,16},{16,0},{1,17},{17,1},{2,18},{18,2},{3,19},{19,3},{4,20},{20... | collective-permute-start | bytes 1179656 | tf_op jit(solution)/shard_map/ppermute | solution.py:237
  35.6 6.6 %collective-permute-done.6.refs_10_ = bf16[512,384]{1,0:T(8,128)(2,1)S(1)} collective-permute-done((bf16[512,384]{1,0:T(8,128)(2,1)S(1)}, bf16[512,384]{1,0:T(8,128)(2,1)S(1)}, u32[]{:S(2)}, u32[]{:S(2)}) %collective-permute-start.6) | collective-permute-done | bytes 393248 | tf_op jit(solution)/shard_map/ppermute | solution.py:237
  42.2 4.1 %collective-permute-done.5.refs_2_ = bf16[512,512]{1,0:T(8,128)(2,1)} collective-permute-done((bf16[512,512]{1,0:T(8,128)(2,1)}, bf16[512,512]{1,0:T(8,128)(2,1)}, u32[]{:S(2)}, u32[]{:S(2)}) %collective-permute-start.5) | collective-permute-done | bytes 524320 | tf_op jit(solution)/shard_map/ppermute | solution.py:237
  47.9 1.2 %collective-permute-start.13 = (bf16[2,384,128]{2,1,0:T(8,128)(2,1)S(1)}, bf16[2,384,128]{2,1,0:T(8,128)(2,1)S(1)}, u32[]{:S(2)}, u32[]{:S(2)}) collective-permute-start(bf16[2,384,128]{2,1,0:T(8,128)(2,1)S(1)} %copy-done.8), channel_id=1, source_target_pairs={{0,8},{4,12},{8,0},{12,4},{1,9},{5,13},{9,1},{13,5},{2,10},{6,14},... | collective-permute-start | bytes 589832 | tf_op jit(solution)/shard_map/ppermute | solution.py:237
  49.0 7.8 %collective-permute-start.14 = (bf16[4,384,128]{2,1,0:T(8,128)(2,1)S(1)}, bf16[4,384,128]{2,1,0:T(8,128)(2,1)S(1)}, u32[]{:S(2)}, u32[]{:S(2)}) collective-permute-start(bf16[4,384,128]{2,1,0:T(8,128)(2,1)S(1)} %bitcast.26), channel_id=1, source_target_pairs={{0,4},{4,0},{8,12},{12,8},{1,5},{5,1},{9,13},{13,9},{2,6},{6,2},{1... | collective-permute-start | bytes 1179656 | tf_op jit(solution)/shard_map/ppermute | solution.py:237
  57.0 0.9 collective-permute-done.12.refs_11_
  57.9 3.6 %shard_map.55.refs_0_ = bf16[512,384]{1,0:T(8,128)(2,1)S(1)} custom-call(s32[2]{0:T(128)S(1)} %pad_add_fusion.at_ref, bf16[512,512]{1,0:T(8,128)(2,1)} %collective-permute-done.2.refs_0_, bf16[512,512]{1,0:T(8,128)(2,1)} %collective-permute-done.10.refs_1_, bf16[512,512]{1,0:T(8,128)(2,1)} %collective-permute-done.5.refs_2_, ...), custom_call_target="tpu_custom_call" | custom-call | bytes 5242880 | tf_op jit(solution)/shard_map/pallas_call | solution.py:165
  62.1 1.6 %collective-permute-start.17 = (bf16[2,384,128]{2,1,0:T(8,128)(2,1)S(1)}, bf16[2,384,128]{2,1,0:T(8,128)(2,1)S(1)}, u32[]{:S(2)}, u32[]{:S(2)}) collective-permute-start(bf16[2,384,128]{2,1,0:T(8,128)(2,1)S(1)} %collective-permute-done.13.refs_6_), channel_id=1, source_target_pairs={{0,16},{16,0},{1,17},{17,1},{2,18},{18,2},{3,19},{19,3},{4,20},{20... | collective-permute-start | bytes 589832 | tf_op jit(solution)/shard_map/ppermute | solution.py:237
  63.8 3.2 %shard_map.58.refs_0_ = bf16[512,384]{1,0:T(8,128)(2,1)S(1)} custom-call(s32[2]{0:T(128)S(1)} %pad_add_fusion.at_ref, bf16[512,512]{1,0:T(8,128)(2,1)S(1)} %copy-done, bf16[512,512]{1,0:T(8,128)(2,1)S(1)} %copy-done.2, bf16[512,512]{1,0:T(8,128)(2,1)} %collective-permute-done.refs_2_, bf16[512,512]{1,0:T(8,128)(2,1)S(1)} %copy-done.4, ...), custom_call_target="tpu_custom_call" | custom-call | bytes 5242880 | tf_op jit(solution)/shard_map/pallas_call | solution.py:165
  67.0 1.7 %collective-permute-done.15.refs_8_ = bf16[2,384,128]{2,1,0:T(8,128)(2,1)S(1)} collective-permute-done((bf16[2,384,128]{2,1,0:T(8,128)(2,1)S(1)}, bf16[2,384,128]{2,1,0:T(8,128)(2,1)S(1)}, u32[]{:S(2)}, u32[]{:S(2)}) %collective-permute-start.15) | collective-permute-done | bytes 196640 | tf_op jit(solution)/shard_map/ppermute | solution.py:237
  68.7 1.1 %collective-permute-start.18 = (bf16[2,384,128]{2,1,0:T(8,128)(2,1)S(1)}, bf16[2,384,128]{2,1,0:T(8,128)(2,1)S(1)}, u32[]{:S(2)}, u32[]{:S(2)}) collective-permute-start(bf16[2,384,128]{2,1,0:T(8,128)(2,1)S(1)} %collective-permute-done.15.refs_8_), channel_id=1, source_target_pairs={{0,16},{16,0},{1,17},{17,1},{2,18},{18,2},{3,19},{19,3},{4,20},{20... | collective-permute-start | bytes 589832 | tf_op jit(solution)/shard_map/ppermute | solution.py:237
  69.9 2.0 %collective-permute-done.16.refs_2_ = bf16[512,384]{1,0:T(8,128)(2,1)S(1)} collective-permute-done((bf16[512,384]{1,0:T(8,128)(2,1)S(1)}, bf16[512,384]{1,0:T(8,128)(2,1)S(1)}, u32[]{:S(2)}, u32[]{:S(2)}) %collective-permute-start.16) | collective-permute-done | bytes 393248 | tf_op jit(solution)/shard_map/ppermute | solution.py:237
  72.5 1.9 %collective-permute-done.18.refs_9_ = bf16[2,384,128]{2,1,0:T(8,128)(2,1)S(1)} collective-permute-done((bf16[2,384,128]{2,1,0:T(8,128)(2,1)S(1)}, bf16[2,384,128]{2,1,0:T(8,128)(2,1)S(1)}, u32[]{:S(2)}, u32[]{:S(2)}) %collective-permute-start.18) | collective-permute-done | bytes 196640 | tf_op jit(solution)/shard_map/ppermute | solution.py:237
  74.4 1.6 %shard_map.67 = bf16[512,512]{1,0:T(8,128)(2,1)S(1)} custom-call(s32[2]{0:T(128)S(1)} %pad_add_fusion.1.at_ref, bf16[512,384]{1,0:T(8,128)(2,1)S(1)} %shard_map.55.refs_0_, bf16[512,384]{1,0:T(8,128)(2,1)S(1)} %collective-permute-done.19.refs_1_, bf16[512,384]{1,0:T(8,128)(2,1)S(1)} %collective-permute-done.16.refs_2_, ...), custom_call_target="tpu_custom_call" | custom-call | bytes 3145728 | tf_op jit(solution)/shard_map/pallas_call | solution.py:198
  76.6 6.9 %collective-permute-done.21.refs_2_ = bf16[512,384]{1,0:T(8,128)(2,1)S(1)} collective-permute-done((bf16[512,384]{1,0:T(8,128)(2,1)S(1)}, bf16[512,384]{1,0:T(8,128)(2,1)S(1)}, u32[]{:S(2)}, u32[]{:S(2)}) %collective-permute-start.21) | collective-permute-done | bytes 393248 | tf_op jit(solution)/shard_map/ppermute | solution.py:237
  83.5 1.7 %collective-permute-done.23.refs_3_ = bf16[512,384]{1,0:T(8,128)(2,1)S(1)} collective-permute-done((bf16[512,384]{1,0:T(8,128)(2,1)S(1)}, bf16[512,384]{1,0:T(8,128)(2,1)S(1)}, u32[]{:S(2)}, u32[]{:S(2)}) %collective-permute-start.23) | collective-permute-done | bytes 393248 | tf_op jit(solution)/shard_map/ppermute | solution.py:237
  85.2 1.6 %shard_map.66.mine_ref = f32[512,512]{1,0:T(8,128)S(1)} custom-call(s32[2]{0:T(128)S(1)} %pad_add_fusion.1.at_ref, bf16[512,384]{1,0:T(8,128)(2,1)S(1)} %shard_map.58.refs_0_, bf16[512,384]{1,0:T(8,128)(2,1)S(1)} %collective-permute-done.22.refs_1_, bf16[512,384]{1,0:T(8,128)(2,1)S(1)} %collective-permute-done.21.refs_2_, ...), custom_call_target="tpu_custom_call" | custom-call | bytes 3145728 | tf_op jit(solution)/shard_map/pallas_call | solution.py:198
  86.8 2.4 %collective-permute-done.24.theirs_ref = bf16[512,512]{1,0:T(8,128)(2,1)S(1)} collective-permute-done((bf16[512,512]{1,0:T(8,128)(2,1)S(1)}, bf16[512,512]{1,0:T(8,128)(2,1)S(1)}, u32[]{:S(2)}, u32[]{:S(2)}) %collective-permute-start.24) | collective-permute-done | bytes 524320 | tf_op jit(solution)/shard_map/ppermute | solution.py:237
  89.2 1.0 %shard_map.69 = bf16[512,512]{1,0:T(8,128)(2,1)} custom-call(s32[1]{0:T(128)} %bitcast.9.at_ref, f32[512,512]{1,0:T(8,128)S(1)} %shard_map.66.mine_ref, bf16[512,512]{1,0:T(8,128)(2,1)S(1)} %collective-permute-done.24.theirs_ref), custom_call_target="tpu_custom_call" | custom-call | tf_op jit(solution)/shard_map/pallas_call | solution.py:216
  (67 shorter events, 5.4 us)
Async XLA Ops:
  0.0 8.5 %copy-start.5 = (bf16[512,768]{1,0:T(8,128)(2,1)S(1)}, bf16[512,768]{1,0:T(8,128)(2,1)}, u32[]{:S(2)}) copy-start(bf16[512,768]{1,0:T(8,128)(2,1)} %param.6) | copy-start | bytes 2359300
  0.0 9.9 %collective-permute-start.1 = (bf16[512,512]{1,0:T(8,128)(2,1)}, bf16[512,512]{1,0:T(8,128)(2,1)S(1)}, u32[]{:S(2)}, u32[]{:S(2)}) collective-permute-start(bf16[512,512]{1,0:T(8,128)(2,1)} %refs_0_.1), channel_id=1, source_target_pairs={{0,1},{1,0},{2,3},{3,2},{4,5},{5,4},{6,7},{7,6},{8,9},{9,8},{10,11... | collective-permute-start | bytes 1572872 | tf_op jit(solution)/shard_map/ppermute | solution.py:237
  0.5 15.4 %collective-permute-start = (bf16[512,512]{1,0:T(8,128)(2,1)}, bf16[512,512]{1,0:T(8,128)(2,1)}, u32[]{:S(2)}, u32[]{:S(2)}) collective-permute-start(bf16[512,512]{1,0:T(8,128)(2,1)} %refs_0_.1), channel_id=1, source_target_pairs={{0,2},{1,3},{2,0},{3,1},{4,6},{5,7},{6,4},{7,5},{8,10},{9,11},{10,... | collective-permute-start | bytes 1572872 | tf_op jit(solution)/shard_map/ppermute | solution.py:237
  3.0 23.5 %collective-permute-start.2 = (bf16[512,512]{1,0:T(8,128)(2,1)}, bf16[512,512]{1,0:T(8,128)(2,1)}, u32[]{:S(2)}, u32[]{:S(2)}) collective-permute-start(bf16[512,512]{1,0:T(8,128)(2,1)} %refs_0_.1), channel_id=1, source_target_pairs={{0,4},{4,0},{8,12},{12,8},{1,5},{5,1},{9,13},{13,9},{2,6},{6,2},{1... | collective-permute-start | bytes 1572872 | tf_op jit(solution)/shard_map/ppermute | solution.py:237
  5.8 19.7 %collective-permute-start.3 = (bf16[512,384]{1,0:T(8,128)(2,1)S(1)}, bf16[512,384]{1,0:T(8,128)(2,1)S(1)}, u32[]{:S(2)}, u32[]{:S(2)}) collective-permute-start(bf16[512,384]{1,0:T(8,128)(2,1)S(1)} %dynamic-slice_select_fusion.2.refs_4_), channel_id=1, source_target_pairs={{0,8},{4,12},{8,0},{12,4},{1,9},{5,13},{9,1},{13,5},{2,10},{6,14},... | collective-permute-start | bytes 1179656 | tf_op jit(solution)/shard_map/ppermute | solution.py:237
  8.5 9.2 %copy-start.6 = (bf16[3072,128]{1,0:T(8,128)(2,1)S(1)}, bf16[3072,128]{1,0:T(8,128)(2,1)}, u32[]{:S(2)}) copy-start(bf16[3072,128]{1,0:T(8,128)(2,1)} %param.7) | copy-start | bytes 2359300
  15.9 18.2 %collective-permute-start.4 = (bf16[512,384]{1,0:T(8,128)(2,1)S(1)}, bf16[512,384]{1,0:T(8,128)(2,1)S(1)}, u32[]{:S(2)}, u32[]{:S(2)}) collective-permute-start(bf16[512,384]{1,0:T(8,128)(2,1)S(1)} %get-tuple-element.81), channel_id=1, source_target_pairs={{0,4},{4,0},{8,12},{12,8},{1,5},{5,1},{9,13},{13,9},{2,6},{6,2},{1... | collective-permute-start | bytes 1179656 | tf_op jit(solution)/shard_map/ppermute | solution.py:237
  26.5 19.8 %collective-permute-start.8 = (bf16[512,384]{1,0:T(8,128)(2,1)S(1)}, bf16[512,384]{1,0:T(8,128)(2,1)S(1)}, u32[]{:S(2)}, u32[]{:S(2)}) collective-permute-start(bf16[512,384]{1,0:T(8,128)(2,1)S(1)} %get-tuple-element.81), channel_id=1, source_target_pairs={{0,12},{4,8},{8,4},{12,0},{1,13},{5,9},{9,5},{13,1},{2,14},{6,10},... | collective-permute-start | bytes 1179656 | tf_op jit(solution)/shard_map/ppermute | solution.py:237
  30.1 12.1 %collective-permute-start.6 = (bf16[512,384]{1,0:T(8,128)(2,1)S(1)}, bf16[512,384]{1,0:T(8,128)(2,1)S(1)}, u32[]{:S(2)}, u32[]{:S(2)}) collective-permute-start(bf16[512,384]{1,0:T(8,128)(2,1)S(1)} %collective-permute-done.3.refs_6_), channel_id=1, source_target_pairs={{0,16},{16,0},{1,17},{17,1},{2,18},{18,2},{3,19},{19,3},{4,20},{20... | collective-permute-start | bytes 1179656 | tf_op jit(solution)/shard_map/ppermute | solution.py:237
  31.6 10.5 %collective-permute-start.7 = (bf16[512,512]{1,0:T(8,128)(2,1)}, bf16[512,512]{1,0:T(8,128)(2,1)S(1)}, u32[]{:S(2)}, u32[]{:S(2)}) collective-permute-start(bf16[512,512]{1,0:T(8,128)(2,1)} %collective-permute-done.refs_2_), channel_id=1, source_target_pairs={{0,1},{1,0},{2,3},{3,2},{4,5},{5,4},{6,7},{7,6},{8,9},{9,8},{10,11... | collective-permute-start | bytes 1572872 | tf_op jit(solution)/shard_map/ppermute | solution.py:237
  31.6 14.7 %collective-permute-start.5 = (bf16[512,512]{1,0:T(8,128)(2,1)}, bf16[512,512]{1,0:T(8,128)(2,1)}, u32[]{:S(2)}, u32[]{:S(2)}) collective-permute-start(bf16[512,512]{1,0:T(8,128)(2,1)} %collective-permute-done.2.refs_0_), channel_id=1, source_target_pairs={{0,2},{1,3},{2,0},{3,1},{4,6},{5,7},{6,4},{7,5},{8,10},{9,11},{10,... | collective-permute-start | bytes 1572872 | tf_op jit(solution)/shard_map/ppermute | solution.py:237
  34.1 13.8 %collective-permute-start.9 = (bf16[512,384]{1,0:T(8,128)(2,1)S(1)}, bf16[512,384]{1,0:T(8,128)(2,1)S(1)}, u32[]{:S(2)}, u32[]{:S(2)}) collective-permute-start(bf16[512,384]{1,0:T(8,128)(2,1)S(1)} %collective-permute-done.4.refs_5_), channel_id=1, source_target_pairs={{0,16},{16,0},{1,17},{17,1},{2,18},{18,2},{3,19},{19,3},{4,20},{20... | collective-permute-start | bytes 1179656 | tf_op jit(solution)/shard_map/ppermute | solution.py:237
  42.2 4.1 %copy-start.3 = (bf16[512,512]{1,0:T(8,128)(2,1)}, bf16[512,512]{1,0:T(8,128)(2,1)S(1)}, u32[]{:S(2)}) copy-start(bf16[512,512]{1,0:T(8,128)(2,1)S(1)} %collective-permute-done.7.refs_3_) | copy-start | bytes 1572868
  46.3 10.6 %collective-permute-start.10 = (bf16[512,512]{1,0:T(8,128)(2,1)}, bf16[512,512]{1,0:T(8,128)(2,1)}, u32[]{:S(2)}, u32[]{:S(2)}) collective-permute-start(bf16[512,512]{1,0:T(8,128)(2,1)} %collective-permute-done.2.refs_0_), channel_id=1, source_target_pairs={{0,1},{1,0},{2,3},{3,2},{4,5},{5,4},{6,7},{7,6},{8,9},{9,8},{10,11... | collective-permute-start | bytes 1572872 | tf_op jit(solution)/shard_map/ppermute | solution.py:237
  46.3 10.6 %collective-permute-start.11 = (bf16[512,512]{1,0:T(8,128)(2,1)}, bf16[512,512]{1,0:T(8,128)(2,1)}, u32[]{:S(2)}, u32[]{:S(2)}) collective-permute-start(bf16[512,512]{1,0:T(8,128)(2,1)} %collective-permute-done.5.refs_2_), channel_id=1, source_target_pairs={{0,1},{1,0},{2,3},{3,2},{4,5},{5,4},{6,7},{7,6},{8,9},{9,8},{10,11... | collective-permute-start | bytes 1572872 | tf_op jit(solution)/shard_map/ppermute | solution.py:237
  46.8 11.1 %collective-permute-start.12 = (bf16[512,384]{1,0:T(8,128)(2,1)S(1)}, bf16[512,384]{1,0:T(8,128)(2,1)S(1)}, u32[]{:S(2)}, u32[]{:S(2)}) collective-permute-start(bf16[512,384]{1,0:T(8,128)(2,1)S(1)} %collective-permute-done.8.refs_7_), channel_id=1, source_target_pairs={{0,16},{16,0},{1,17},{17,1},{2,18},{18,2},{3,19},{19,3},{4,20},{20... | collective-permute-start | bytes 1179656 | tf_op jit(solution)/shard_map/ppermute | solution.py:237
  47.3 9.5 %copy-start.7 = (bf16[2,384,128]{2,1,0:T(8,128)(2,1)S(1)}, bf16[2,384,128]{2,1,0:T(8,128)(2,1)}, u32[]{:S(2)}) copy-start(bf16[2,384,128]{2,1,0:T(8,128)(2,1)} %get-tuple-element.104) | copy-start | bytes 589828
  47.9 14.3 %collective-permute-start.13 = (bf16[2,384,128]{2,1,0:T(8,128)(2,1)S(1)}, bf16[2,384,128]{2,1,0:T(8,128)(2,1)S(1)}, u32[]{:S(2)}, u32[]{:S(2)}) collective-permute-start(bf16[2,384,128]{2,1,0:T(8,128)(2,1)S(1)} %copy-done.8), channel_id=1, source_target_pairs={{0,8},{4,12},{8,0},{12,4},{1,9},{5,13},{9,1},{13,5},{2,10},{6,14},... | collective-permute-start | bytes 589832 | tf_op jit(solution)/shard_map/ppermute | solution.py:237
  49.0 18.0 %collective-permute-start.14 = (bf16[4,384,128]{2,1,0:T(8,128)(2,1)S(1)}, bf16[4,384,128]{2,1,0:T(8,128)(2,1)S(1)}, u32[]{:S(2)}, u32[]{:S(2)}) collective-permute-start(bf16[4,384,128]{2,1,0:T(8,128)(2,1)S(1)} %bitcast.26), channel_id=1, source_target_pairs={{0,4},{4,0},{8,12},{12,8},{1,5},{5,1},{9,13},{13,9},{2,6},{6,2},{1... | collective-permute-start | bytes 1179656 | tf_op jit(solution)/shard_map/ppermute | solution.py:237
  56.9 11.9 %collective-permute-start.15 = (bf16[2,384,128]{2,1,0:T(8,128)(2,1)S(1)}, bf16[2,384,128]{2,1,0:T(8,128)(2,1)S(1)}, u32[]{:S(2)}, u32[]{:S(2)}) collective-permute-start(bf16[2,384,128]{2,1,0:T(8,128)(2,1)S(1)} %copy-done.7), channel_id=1, source_target_pairs={{0,12},{4,8},{8,4},{12,0},{1,13},{5,9},{9,5},{13,1},{2,14},{6,10},... | collective-permute-start | bytes 589832 | tf_op jit(solution)/shard_map/ppermute | solution.py:237
  57.9 5.9 %copy-start = (bf16[512,512]{1,0:T(8,128)(2,1)S(1)}, bf16[512,512]{1,0:T(8,128)(2,1)}, u32[]{:S(2)}) copy-start(bf16[512,512]{1,0:T(8,128)(2,1)} %refs_0_.1) | copy-start | bytes 1572868
  57.9 5.9 %copy-start.2 = (bf16[512,512]{1,0:T(8,128)(2,1)S(1)}, bf16[512,512]{1,0:T(8,128)(2,1)}, u32[]{:S(2)}) copy-start(bf16[512,512]{1,0:T(8,128)(2,1)} %copy-done.1) | copy-start | bytes 1572868
  57.9 5.9 %copy-start.4 = (bf16[512,512]{1,0:T(8,128)(2,1)S(1)}, bf16[512,512]{1,0:T(8,128)(2,1)}, u32[]{:S(2)}) copy-start(bf16[512,512]{1,0:T(8,128)(2,1)} %copy-done.3) | copy-start | bytes 1572868
  61.6 10.3 %collective-permute-start.16 = (bf16[512,384]{1,0:T(8,128)(2,1)S(1)}, bf16[512,384]{1,0:T(8,128)(2,1)S(1)}, u32[]{:S(2)}, u32[]{:S(2)}) collective-permute-start(bf16[512,384]{1,0:T(8,128)(2,1)S(1)} %shard_map.55.refs_0_), channel_id=1, source_target_pairs={{0,2},{1,3},{2,0},{3,1},{4,6},{5,7},{6,4},{7,5},{8,10},{9,11},{10,... | collective-permute-start | bytes 1179656 | tf_op jit(solution)/shard_map/ppermute | solution.py:237
  62.1 10.3 %collective-permute-start.17 = (bf16[2,384,128]{2,1,0:T(8,128)(2,1)S(1)}, bf16[2,384,128]{2,1,0:T(8,128)(2,1)S(1)}, u32[]{:S(2)}, u32[]{:S(2)}) collective-permute-start(bf16[2,384,128]{2,1,0:T(8,128)(2,1)S(1)} %collective-permute-done.13.refs_6_), channel_id=1, source_target_pairs={{0,16},{16,0},{1,17},{17,1},{2,18},{18,2},{3,19},{19,3},{4,20},{20... | collective-permute-start | bytes 589832 | tf_op jit(solution)/shard_map/ppermute | solution.py:237
  63.8 10.6 %collective-permute-start.19 = (bf16[512,384]{1,0:T(8,128)(2,1)S(1)}, bf16[512,384]{1,0:T(8,128)(2,1)S(1)}, u32[]{:S(2)}, u32[]{:S(2)}) collective-permute-start(bf16[512,384]{1,0:T(8,128)(2,1)S(1)} %shard_map.55.refs_0_), channel_id=1, source_target_pairs={{0,1},{1,0},{2,3},{3,2},{4,5},{5,4},{6,7},{7,6},{8,9},{9,8},{10,11... | collective-permute-start | bytes 1179656 | tf_op jit(solution)/shard_map/ppermute | solution.py:237
  68.7 5.7 %collective-permute-start.18 = (bf16[2,384,128]{2,1,0:T(8,128)(2,1)S(1)}, bf16[2,384,128]{2,1,0:T(8,128)(2,1)S(1)}, u32[]{:S(2)}, u32[]{:S(2)}) collective-permute-start(bf16[2,384,128]{2,1,0:T(8,128)(2,1)S(1)} %collective-permute-done.15.refs_8_), channel_id=1, source_target_pairs={{0,16},{16,0},{1,17},{17,1},{2,18},{18,2},{3,19},{19,3},{4,20},{20... | collective-permute-start | bytes 589832 | tf_op jit(solution)/shard_map/ppermute | solution.py:237
  71.9 2.5 %collective-permute-start.20 = (bf16[512,384]{1,0:T(8,128)(2,1)S(1)}, bf16[512,384]{1,0:T(8,128)(2,1)S(1)}, u32[]{:S(2)}, u32[]{:S(2)}) collective-permute-start(bf16[512,384]{1,0:T(8,128)(2,1)S(1)} %collective-permute-done.16.refs_2_), channel_id=1, source_target_pairs={{0,1},{1,0},{2,3},{3,2},{4,5},{5,4},{6,7},{7,6},{8,9},{9,8},{10,11... | collective-permute-start | bytes 1179656 | tf_op jit(solution)/shard_map/ppermute | solution.py:237
  71.9 11.5 %collective-permute-start.21 = (bf16[512,384]{1,0:T(8,128)(2,1)S(1)}, bf16[512,384]{1,0:T(8,128)(2,1)S(1)}, u32[]{:S(2)}, u32[]{:S(2)}) collective-permute-start(bf16[512,384]{1,0:T(8,128)(2,1)S(1)} %shard_map.58.refs_0_), channel_id=1, source_target_pairs={{0,2},{1,3},{2,0},{3,1},{4,6},{5,7},{6,4},{7,5},{8,10},{9,11},{10,... | collective-permute-start | bytes 1179656 | tf_op jit(solution)/shard_map/ppermute | solution.py:237
  76.0 13.2 %collective-permute-start.24 = (bf16[512,512]{1,0:T(8,128)(2,1)S(1)}, bf16[512,512]{1,0:T(8,128)(2,1)S(1)}, u32[]{:S(2)}, u32[]{:S(2)}) collective-permute-start(bf16[512,512]{1,0:T(8,128)(2,1)S(1)} %shard_map.67), channel_id=1, source_target_pairs={{0,4},{4,0},{8,12},{12,8},{1,5},{5,1},{9,13},{13,9},{2,6},{6,2},{1... | collective-permute-start | bytes 1572872 | tf_op jit(solution)/shard_map/ppermute | solution.py:237
  76.5 6.9 %collective-permute-start.22 = (bf16[512,384]{1,0:T(8,128)(2,1)S(1)}, bf16[512,384]{1,0:T(8,128)(2,1)S(1)}, u32[]{:S(2)}, u32[]{:S(2)}) collective-permute-start(bf16[512,384]{1,0:T(8,128)(2,1)S(1)} %shard_map.58.refs_0_), channel_id=1, source_target_pairs={{0,1},{1,0},{2,3},{3,2},{4,5},{5,4},{6,7},{7,6},{8,9},{9,8},{10,11... | collective-permute-start | bytes 1179656 | tf_op jit(solution)/shard_map/ppermute | solution.py:237
  83.5 1.7 %collective-permute-start.23 = (bf16[512,384]{1,0:T(8,128)(2,1)S(1)}, bf16[512,384]{1,0:T(8,128)(2,1)S(1)}, u32[]{:S(2)}, u32[]{:S(2)}) collective-permute-start(bf16[512,384]{1,0:T(8,128)(2,1)S(1)} %collective-permute-done.21.refs_2_), channel_id=1, source_target_pairs={{0,1},{1,0},{2,3},{3,2},{4,5},{5,4},{6,7},{7,6},{8,9},{9,8},{10,11... | collective-permute-start | bytes 1179656 | tf_op jit(solution)/shard_map/ppermute | solution.py:237
  (2 other events, 1.8 us)

commit v7 on v6

--- a/solution.py
+++ b/solution.py
@@ -101,9 +101,9 @@
     ((N.tokens_x, N.tokens_core), (N.direct_1,), 500),
     ((N.pair, N.direct_2), (N.direct_3, N.swapped_2, N.pair_x, N.tokens_x_core), 500),
     ((N.direct_1, *PARTS), (N.swapped_1,), 2600),
-    ((N.pair_x, N.swapped_2, N.tokens_x_core), (), 500),
+    ((N.swapped_2, N.tokens_x_core), (), 500),
     ((N.direct_3,), (N.swapped_3, N.pair_core, N.pair_x_core), 500),
-    ((N.swapped_1,), (N.down_1, N.down_2), 2000),
+    ((N.swapped_1, N.pair_x), (N.down_1, N.down_2), 2000),
     ((N.pair_core, N.pair_x_core), (N.down_3,), 500),
     ((N.swapped_3,), (N.hidden_pair_x,), 0),
     ((N.hidden_pair,), (), 0),
@@ -112,10 +112,10 @@
     ((N.hidden_pair_x,), (N.hidden_pair_core, N.hidden_pair_x_core, N.hidden_own_x), 500),
     ((N.down_swapped_2,), (), 500),
     ((N.down_swapped_3,), (), 3000),
-    ((N.hidden_pair_core, N.hidden_pair_x_core), (N.theirs,), 500),
+    ((N.hidden_pair_core, N.hidden_pair_x_core), (N.theirs,), 2000),
     ((N.hidden_own_x,), (N.hidden_own_core, N.hidden_own_x_core), 500),
     ((N.hidden_own_core, N.hidden_own_x_core), (), 500),
-    ((N.mine, N.theirs), (), 500),
+    ((N.mine, N.theirs), (), 6000),
 )
 
 

time: 90.4 us -> 90.2 us (level)
  waiting for transfers between devices: 43.9 us -> 42.7 us
    ppermute x25, waiting for transfers between devices: 43.9 us -> 42.7 us  [flip(): return lax.ppermute(x, axis, [(i, i ^ bits) for i in range(sizes[axis])])]
  transfers between devices with their start and end apart: 25 -> 25, of which waited for: 14 -> 16; matrix products, arithmetic and copies ran while one was open for 4% -> 4% of each run, Pallas kernels for 11% -> 11%
where the time goes in v7:
time: 90.2 us; the launch traced here: 90 us
  waiting for transfers between devices  42.7 us (47%)
  starting transfers between devices  31.1 us (34%)
  Pallas kernels  10.9 us (12%)
  other arithmetic  3.63 us (4%)
  local copies, waits for them, and re-layouts  1.6 us (2%)
    ppermute x25, waiting for transfers between devices, flip(): return lax.ppermute(x, axis, [(i, i ^ bits) for i in range(sizes[axis])])  42.7 us
    ppermute x25, starting transfers between devices, flip(): return lax.ppermute(x, axis, [(i, i ^ bits) for i in range(sizes[axis])])  31.1 us
    pallas_call x2, Pallas kernels, hidden_of(): pl.pallas_call(functools.partial(hidden_kernel, rows // 2), out_shape=jax...  6.78 us
    pallas_call x2, Pallas kernels, output_of(): pl.pallas_call(output_kernel, out_shape=jax.ShapeDtypeStruct((hidden[0].s...  3.11 us
    select_n x2, other arithmetic, one_of(): return jnp.where(first, half_of(mine, parity), half_of(theirs, parity))  2.62 us
  transfers between devices with their start and end apart: 25, of which 16 were waited for; matrix products, arithmetic and copies ran while one was open for 4% of the time, Pallas kernels for 11%

profile of v7, /device:TPU:0, one launch (start us, length us, event | category | flops | bytes accessed | tf_op | source)
XLA Modules:
  0.0 90.0 jit_solution(7657993325623474232)
XLA Ops:
  0.5 2.5 %collective-permute-start = (bf16[512,512]{1,0:T(8,128)(2,1)}, bf16[512,512]{1,0:T(8,128)(2,1)}, u32[]{:S(2)}, u32[]{:S(2)}) collective-permute-start(bf16[512,512]{1,0:T(8,128)(2,1)} %refs_0_.1), channel_id=1, source_target_pairs={{0,2},{1,3},{2,0},{3,1},{4,6},{5,7},{6,4},{7,5},{8,10},{9,11},{10,... | collective-permute-start | bytes 1572872 | tf_op jit(solution)/shard_map/ppermute | solution.py:237
  3.0 1.6 %collective-permute-start.2 = (bf16[512,512]{1,0:T(8,128)(2,1)}, bf16[512,512]{1,0:T(8,128)(2,1)}, u32[]{:S(2)}, u32[]{:S(2)}) collective-permute-start(bf16[512,512]{1,0:T(8,128)(2,1)} %refs_0_.1), channel_id=1, source_target_pairs={{0,4},{4,0},{8,12},{12,8},{1,5},{5,1},{9,13},{13,9},{2,6},{6,2},{1... | collective-permute-start | bytes 1572872 | tf_op jit(solution)/shard_map/ppermute | solution.py:237
  4.6 1.2 %dynamic-slice_select_fusion.2.refs_4_ = bf16[512,384]{1,0:T(8,128)(2,1)S(1)} fusion(bf16[512,768]{1,0:T(8,128)(2,1)} %param.6, s32[]{:T(128)S(6)} %select_n.80, bf16[512,768]{1,0:T(8,128)(2,1)} %param.5, pred[]{:T(512)S(6)} %eq.8), kind=kLoop, calls=%fused_computation.4 | loop fusion | flops 196608 | bytes 1179653 | tf_op jit(solution)/shard_map/jit(_where)/select_n | solution.py:243
  5.8 2.7 %collective-permute-start.3 = (bf16[512,384]{1,0:T(8,128)(2,1)S(1)}, bf16[512,384]{1,0:T(8,128)(2,1)S(1)}, u32[]{:S(2)}, u32[]{:S(2)}) collective-permute-start(bf16[512,384]{1,0:T(8,128)(2,1)S(1)} %dynamic-slice_select_fusion.2.refs_4_), channel_id=1, source_target_pairs={{0,8},{4,12},{8,0},{12,4},{1,9},{5,13},{9,1},{13,5},{2,10},{6,14},... | collective-permute-start | bytes 1179656 | tf_op jit(solution)/shard_map/ppermute | solution.py:237
  8.5 1.4 %dynamic-slice_select_fusion = (bf16[512,384]{1,0:T(8,128)(2,1)S(1)}, bf16[512,384]{1,0:T(8,128)(2,1)S(1)}) fusion(bf16[512,768]{1,0:T(8,128)(2,1)} %param.5, s32[]{:T(128)S(6)} %select_n.80, bf16[512,768]{1,0:T(8,128)(2,1)S(1)} %copy-done.5, pred[]{:T(512)S(6)} %eq.8, s32[]{:T(128)S(6)} %select_n.82), kind=kLoop, calls=%fused_computation.2 | loop fusion | flops 393216 | bytes 2359305 | tf_op jit(solution)/shard_map/jit(_where)/select_n | solution.py:243
  10.7 5.2 %collective-permute-done.refs_2_ = bf16[512,512]{1,0:T(8,128)(2,1)} collective-permute-done((bf16[512,512]{1,0:T(8,128)(2,1)}, bf16[512,512]{1,0:T(8,128)(2,1)}, u32[]{:S(2)}, u32[]{:S(2)}) %collective-permute-start) | collective-permute-done | bytes 524320 | tf_op jit(solution)/shard_map/ppermute | solution.py:237
  15.9 1.8 %collective-permute-start.4 = (bf16[512,384]{1,0:T(8,128)(2,1)S(1)}, bf16[512,384]{1,0:T(8,128)(2,1)S(1)}, u32[]{:S(2)}, u32[]{:S(2)}) collective-permute-start(bf16[512,384]{1,0:T(8,128)(2,1)S(1)} %get-tuple-element.80), channel_id=1, source_target_pairs={{0,4},{4,0},{8,12},{12,8},{1,5},{5,1},{9,13},{13,9},{2,6},{6,2},{1... | collective-permute-start | bytes 1179656 | tf_op jit(solution)/shard_map/ppermute | solution.py:237
  17.8 7.8 %collective-permute-done.3.refs_6_ = bf16[512,384]{1,0:T(8,128)(2,1)S(1)} collective-permute-done((bf16[512,384]{1,0:T(8,128)(2,1)S(1)}, bf16[512,384]{1,0:T(8,128)(2,1)S(1)}, u32[]{:S(2)}, u32[]{:S(2)}) %collective-permute-start.3) | collective-permute-done | bytes 393248 | tf_op jit(solution)/shard_map/ppermute | solution.py:237
  25.5 1.0 %collective-permute-done.2.refs_0_ = bf16[512,512]{1,0:T(8,128)(2,1)} collective-permute-done((bf16[512,512]{1,0:T(8,128)(2,1)}, bf16[512,512]{1,0:T(8,128)(2,1)}, u32[]{:S(2)}, u32[]{:S(2)}) %collective-permute-start.2) | collective-permute-done | bytes 524320 | tf_op jit(solution)/shard_map/ppermute | solution.py:237
  26.5 3.6 %collective-permute-start.7 = (bf16[512,384]{1,0:T(8,128)(2,1)S(1)}, bf16[512,384]{1,0:T(8,128)(2,1)S(1)}, u32[]{:S(2)}, u32[]{:S(2)}) collective-permute-start(bf16[512,384]{1,0:T(8,128)(2,1)S(1)} %get-tuple-element.80), channel_id=1, source_target_pairs={{0,12},{4,8},{8,4},{12,0},{1,13},{5,9},{9,5},{13,1},{2,14},{6,10},... | collective-permute-start | bytes 1179656 | tf_op jit(solution)/shard_map/ppermute | solution.py:237
  30.1 1.5 %collective-permute-start.5 = (bf16[512,384]{1,0:T(8,128)(2,1)S(1)}, bf16[512,384]{1,0:T(8,128)(2,1)S(1)}, u32[]{:S(2)}, u32[]{:S(2)}) collective-permute-start(bf16[512,384]{1,0:T(8,128)(2,1)S(1)} %collective-permute-done.3.refs_6_), channel_id=1, source_target_pairs={{0,16},{16,0},{1,17},{17,1},{2,18},{18,2},{3,19},{19,3},{4,20},{20... | collective-permute-start | bytes 1179656 | tf_op jit(solution)/shard_map/ppermute | solution.py:237
  33.0 1.1 %collective-permute-done.4.refs_5_ = bf16[512,384]{1,0:T(8,128)(2,1)S(1)} collective-permute-done((bf16[512,384]{1,0:T(8,128)(2,1)S(1)}, bf16[512,384]{1,0:T(8,128)(2,1)S(1)}, u32[]{:S(2)}, u32[]{:S(2)}) %collective-permute-start.4) | collective-permute-done | bytes 393248 | tf_op jit(solution)/shard_map/ppermute | solution.py:237
  34.1 1.5 %collective-permute-start.9 = (bf16[512,384]{1,0:T(8,128)(2,1)S(1)}, bf16[512,384]{1,0:T(8,128)(2,1)S(1)}, u32[]{:S(2)}, u32[]{:S(2)}) collective-permute-start(bf16[512,384]{1,0:T(8,128)(2,1)S(1)} %collective-permute-done.4.refs_5_), channel_id=1, source_target_pairs={{0,16},{16,0},{1,17},{17,1},{2,18},{18,2},{3,19},{19,3},{4,20},{20... | collective-permute-start | bytes 1179656 | tf_op jit(solution)/shard_map/ppermute | solution.py:237
  35.6 6.6 %collective-permute-done.5.refs_10_ = bf16[512,384]{1,0:T(8,128)(2,1)S(1)} collective-permute-done((bf16[512,384]{1,0:T(8,128)(2,1)S(1)}, bf16[512,384]{1,0:T(8,128)(2,1)S(1)}, u32[]{:S(2)}, u32[]{:S(2)}) %collective-permute-start.5) | collective-permute-done | bytes 393248 | tf_op jit(solution)/shard_map/ppermute | solution.py:237
  43.0 1.7 %collective-permute-done.7.refs_7_ = bf16[512,384]{1,0:T(8,128)(2,1)S(1)} collective-permute-done((bf16[512,384]{1,0:T(8,128)(2,1)S(1)}, bf16[512,384]{1,0:T(8,128)(2,1)S(1)}, u32[]{:S(2)}, u32[]{:S(2)}) %collective-permute-start.7) | collective-permute-done | bytes 393248 | tf_op jit(solution)/shard_map/ppermute | solution.py:237
  44.6 1.7 %collective-permute-done.8.refs_2_ = bf16[512,512]{1,0:T(8,128)(2,1)} collective-permute-done((bf16[512,512]{1,0:T(8,128)(2,1)}, bf16[512,512]{1,0:T(8,128)(2,1)}, u32[]{:S(2)}, u32[]{:S(2)}) %collective-permute-start.8) | collective-permute-done | bytes 524320 | tf_op jit(solution)/shard_map/ppermute | solution.py:237
  47.9 1.2 %collective-permute-start.13 = (bf16[2,384,128]{2,1,0:T(8,128)(2,1)S(1)}, bf16[2,384,128]{2,1,0:T(8,128)(2,1)S(1)}, u32[]{:S(2)}, u32[]{:S(2)}) collective-permute-start(bf16[2,384,128]{2,1,0:T(8,128)(2,1)S(1)} %copy-done.8), channel_id=1, source_target_pairs={{0,8},{4,12},{8,0},{12,4},{1,9},{5,13},{9,1},{13,5},{2,10},{6,14},... | collective-permute-start | bytes 589832 | tf_op jit(solution)/shard_map/ppermute | solution.py:237
  49.0 7.8 %collective-permute-start.14 = (bf16[4,384,128]{2,1,0:T(8,128)(2,1)S(1)}, bf16[4,384,128]{2,1,0:T(8,128)(2,1)S(1)}, u32[]{:S(2)}, u32[]{:S(2)}) collective-permute-start(bf16[4,384,128]{2,1,0:T(8,128)(2,1)S(1)} %bitcast.26), channel_id=1, source_target_pairs={{0,4},{4,0},{8,12},{12,8},{1,5},{5,1},{9,13},{13,9},{2,6},{6,2},{1... | collective-permute-start | bytes 1179656 | tf_op jit(solution)/shard_map/ppermute | solution.py:237
  56.9 0.9 collective-permute-done.12.refs_11_
  57.8 3.6 %shard_map.55.refs_0_ = bf16[512,384]{1,0:T(8,128)(2,1)S(1)} custom-call(s32[2]{0:T(128)S(1)} %pad_add_fusion.at_ref, bf16[512,512]{1,0:T(8,128)(2,1)} %collective-permute-done.2.refs_0_, bf16[512,512]{1,0:T(8,128)(2,1)} %collective-permute-done.10.refs_1_, bf16[512,512]{1,0:T(8,128)(2,1)} %collective-permute-done.8.refs_2_, ...), custom_call_target="tpu_custom_call" | custom-call | bytes 5242880 | tf_op jit(solution)/shard_map/pallas_call | solution.py:165
  62.2 1.5 %collective-permute-start.17 = (bf16[2,384,128]{2,1,0:T(8,128)(2,1)S(1)}, bf16[2,384,128]{2,1,0:T(8,128)(2,1)S(1)}, u32[]{:S(2)}, u32[]{:S(2)}) collective-permute-start(bf16[2,384,128]{2,1,0:T(8,128)(2,1)S(1)} %collective-permute-done.13.refs_6_), channel_id=1, source_target_pairs={{0,16},{16,0},{1,17},{17,1},{2,18},{18,2},{3,19},{19,3},{4,20},{20... | collective-permute-start | bytes 589832 | tf_op jit(solution)/shard_map/ppermute | solution.py:237
  63.7 3.2 %shard_map.58.refs_0_ = bf16[512,384]{1,0:T(8,128)(2,1)S(1)} custom-call(s32[2]{0:T(128)S(1)} %pad_add_fusion.at_ref, bf16[512,512]{1,0:T(8,128)(2,1)S(1)} %copy-done, bf16[512,512]{1,0:T(8,128)(2,1)S(1)} %copy-done.2, bf16[512,512]{1,0:T(8,128)(2,1)} %collective-permute-done.refs_2_, bf16[512,512]{1,0:T(8,128)(2,1)S(1)} %copy-done.4, ...), custom_call_target="tpu_custom_call" | custom-call | bytes 5242880 | tf_op jit(solution)/shard_map/pallas_call | solution.py:165
  66.9 1.8 %collective-permute-done.15.refs_8_ = bf16[2,384,128]{2,1,0:T(8,128)(2,1)S(1)} collective-permute-done((bf16[2,384,128]{2,1,0:T(8,128)(2,1)S(1)}, bf16[2,384,128]{2,1,0:T(8,128)(2,1)S(1)}, u32[]{:S(2)}, u32[]{:S(2)}) %collective-permute-start.15) | collective-permute-done | bytes 196640 | tf_op jit(solution)/shard_map/ppermute | solution.py:237
  68.7 1.1 %collective-permute-start.18 = (bf16[2,384,128]{2,1,0:T(8,128)(2,1)S(1)}, bf16[2,384,128]{2,1,0:T(8,128)(2,1)S(1)}, u32[]{:S(2)}, u32[]{:S(2)}) collective-permute-start(bf16[2,384,128]{2,1,0:T(8,128)(2,1)S(1)} %collective-permute-done.15.refs_8_), channel_id=1, source_target_pairs={{0,16},{16,0},{1,17},{17,1},{2,18},{18,2},{3,19},{19,3},{4,20},{20... | collective-permute-start | bytes 589832 | tf_op jit(solution)/shard_map/ppermute | solution.py:237
  69.9 1.9 %collective-permute-done.16.refs_2_ = bf16[512,384]{1,0:T(8,128)(2,1)S(1)} collective-permute-done((bf16[512,384]{1,0:T(8,128)(2,1)S(1)}, bf16[512,384]{1,0:T(8,128)(2,1)S(1)}, u32[]{:S(2)}, u32[]{:S(2)}) %collective-permute-start.16) | collective-permute-done | bytes 393248 | tf_op jit(solution)/shard_map/ppermute | solution.py:237
  72.8 1.6 %collective-permute-done.18.refs_9_ = bf16[2,384,128]{2,1,0:T(8,128)(2,1)S(1)} collective-permute-done((bf16[2,384,128]{2,1,0:T(8,128)(2,1)S(1)}, bf16[2,384,128]{2,1,0:T(8,128)(2,1)S(1)}, u32[]{:S(2)}, u32[]{:S(2)}) %collective-permute-start.18) | collective-permute-done | bytes 196640 | tf_op jit(solution)/shard_map/ppermute | solution.py:237
  74.4 1.6 %shard_map.67 = bf16[512,512]{1,0:T(8,128)(2,1)S(1)} custom-call(s32[2]{0:T(128)S(1)} %pad_add_fusion.1.at_ref, bf16[512,384]{1,0:T(8,128)(2,1)S(1)} %shard_map.55.refs_0_, bf16[512,384]{1,0:T(8,128)(2,1)S(1)} %collective-permute-done.19.refs_1_, bf16[512,384]{1,0:T(8,128)(2,1)S(1)} %collective-permute-done.16.refs_2_, ...), custom_call_target="tpu_custom_call" | custom-call | bytes 3145728 | tf_op jit(solution)/shard_map/pallas_call | solution.py:198
  76.5 6.9 %collective-permute-done.21.refs_2_ = bf16[512,384]{1,0:T(8,128)(2,1)S(1)} collective-permute-done((bf16[512,384]{1,0:T(8,128)(2,1)S(1)}, bf16[512,384]{1,0:T(8,128)(2,1)S(1)}, u32[]{:S(2)}, u32[]{:S(2)}) %collective-permute-start.21) | collective-permute-done | bytes 393248 | tf_op jit(solution)/shard_map/ppermute | solution.py:237
  83.4 1.7 %collective-permute-done.23.refs_3_ = bf16[512,384]{1,0:T(8,128)(2,1)S(1)} collective-permute-done((bf16[512,384]{1,0:T(8,128)(2,1)S(1)}, bf16[512,384]{1,0:T(8,128)(2,1)S(1)}, u32[]{:S(2)}, u32[]{:S(2)}) %collective-permute-start.23) | collective-permute-done | bytes 393248 | tf_op jit(solution)/shard_map/ppermute | solution.py:237
  85.1 1.6 %shard_map.66.mine_ref = f32[512,512]{1,0:T(8,128)S(1)} custom-call(s32[2]{0:T(128)S(1)} %pad_add_fusion.1.at_ref, bf16[512,384]{1,0:T(8,128)(2,1)S(1)} %shard_map.58.refs_0_, bf16[512,384]{1,0:T(8,128)(2,1)S(1)} %collective-permute-done.22.refs_1_, bf16[512,384]{1,0:T(8,128)(2,1)S(1)} %collective-permute-done.21.refs_2_, ...), custom_call_target="tpu_custom_call" | custom-call | bytes 3145728 | tf_op jit(solution)/shard_map/pallas_call | solution.py:198
  86.7 2.3 %collective-permute-done.24.theirs_ref = bf16[512,512]{1,0:T(8,128)(2,1)S(1)} collective-permute-done((bf16[512,512]{1,0:T(8,128)(2,1)S(1)}, bf16[512,512]{1,0:T(8,128)(2,1)S(1)}, u32[]{:S(2)}, u32[]{:S(2)}) %collective-permute-start.24) | collective-permute-done | bytes 524320 | tf_op jit(solution)/shard_map/ppermute | solution.py:237
  89.0 1.0 %shard_map.69 = bf16[512,512]{1,0:T(8,128)(2,1)} custom-call(s32[1]{0:T(128)} %bitcast.9.at_ref, f32[512,512]{1,0:T(8,128)S(1)} %shard_map.66.mine_ref, bf16[512,512]{1,0:T(8,128)(2,1)S(1)} %collective-permute-done.24.theirs_ref), custom_call_target="tpu_custom_call" | custom-call | tf_op jit(solution)/shard_map/pallas_call | solution.py:216
  (67 shorter events, 7.6 us)
Async XLA Ops:
  0.0 8.5 %copy-start.5 = (bf16[512,768]{1,0:T(8,128)(2,1)S(1)}, bf16[512,768]{1,0:T(8,128)(2,1)}, u32[]{:S(2)}) copy-start(bf16[512,768]{1,0:T(8,128)(2,1)} %param.6) | copy-start | bytes 2359300
  0.0 9.9 %collective-permute-start.1 = (bf16[512,512]{1,0:T(8,128)(2,1)}, bf16[512,512]{1,0:T(8,128)(2,1)S(1)}, u32[]{:S(2)}, u32[]{:S(2)}) collective-permute-start(bf16[512,512]{1,0:T(8,128)(2,1)} %refs_0_.1), channel_id=1, source_target_pairs={{0,1},{1,0},{2,3},{3,2},{4,5},{5,4},{6,7},{7,6},{8,9},{9,8},{10,11... | collective-permute-start | bytes 1572872 | tf_op jit(solution)/shard_map/ppermute | solution.py:237
  0.5 15.4 %collective-permute-start = (bf16[512,512]{1,0:T(8,128)(2,1)}, bf16[512,512]{1,0:T(8,128)(2,1)}, u32[]{:S(2)}, u32[]{:S(2)}) collective-permute-start(bf16[512,512]{1,0:T(8,128)(2,1)} %refs_0_.1), channel_id=1, source_target_pairs={{0,2},{1,3},{2,0},{3,1},{4,6},{5,7},{6,4},{7,5},{8,10},{9,11},{10,... | collective-permute-start | bytes 1572872 | tf_op jit(solution)/shard_map/ppermute | solution.py:237
  3.0 23.5 %collective-permute-start.2 = (bf16[512,512]{1,0:T(8,128)(2,1)}, bf16[512,512]{1,0:T(8,128)(2,1)}, u32[]{:S(2)}, u32[]{:S(2)}) collective-permute-start(bf16[512,512]{1,0:T(8,128)(2,1)} %refs_0_.1), channel_id=1, source_target_pairs={{0,4},{4,0},{8,12},{12,8},{1,5},{5,1},{9,13},{13,9},{2,6},{6,2},{1... | collective-permute-start | bytes 1572872 | tf_op jit(solution)/shard_map/ppermute | solution.py:237
  5.8 19.7 %collective-permute-start.3 = (bf16[512,384]{1,0:T(8,128)(2,1)S(1)}, bf16[512,384]{1,0:T(8,128)(2,1)S(1)}, u32[]{:S(2)}, u32[]{:S(2)}) collective-permute-start(bf16[512,384]{1,0:T(8,128)(2,1)S(1)} %dynamic-slice_select_fusion.2.refs_4_), channel_id=1, source_target_pairs={{0,8},{4,12},{8,0},{12,4},{1,9},{5,13},{9,1},{13,5},{2,10},{6,14},... | collective-permute-start | bytes 1179656 | tf_op jit(solution)/shard_map/ppermute | solution.py:237
  8.5 9.2 %copy-start.6 = (bf16[3072,128]{1,0:T(8,128)(2,1)S(1)}, bf16[3072,128]{1,0:T(8,128)(2,1)}, u32[]{:S(2)}) copy-start(bf16[3072,128]{1,0:T(8,128)(2,1)} %param.7) | copy-start | bytes 2359300
  15.9 18.2 %collective-permute-start.4 = (bf16[512,384]{1,0:T(8,128)(2,1)S(1)}, bf16[512,384]{1,0:T(8,128)(2,1)S(1)}, u32[]{:S(2)}, u32[]{:S(2)}) collective-permute-start(bf16[512,384]{1,0:T(8,128)(2,1)S(1)} %get-tuple-element.80), channel_id=1, source_target_pairs={{0,4},{4,0},{8,12},{12,8},{1,5},{5,1},{9,13},{13,9},{2,6},{6,2},{1... | collective-permute-start | bytes 1179656 | tf_op jit(solution)/shard_map/ppermute | solution.py:237
  26.5 18.1 %collective-permute-start.7 = (bf16[512,384]{1,0:T(8,128)(2,1)S(1)}, bf16[512,384]{1,0:T(8,128)(2,1)S(1)}, u32[]{:S(2)}, u32[]{:S(2)}) collective-permute-start(bf16[512,384]{1,0:T(8,128)(2,1)S(1)} %get-tuple-element.80), channel_id=1, source_target_pairs={{0,12},{4,8},{8,4},{12,0},{1,13},{5,9},{9,5},{13,1},{2,14},{6,10},... | collective-permute-start | bytes 1179656 | tf_op jit(solution)/shard_map/ppermute | solution.py:237
  30.1 12.1 %collective-permute-start.5 = (bf16[512,384]{1,0:T(8,128)(2,1)S(1)}, bf16[512,384]{1,0:T(8,128)(2,1)S(1)}, u32[]{:S(2)}, u32[]{:S(2)}) collective-permute-start(bf16[512,384]{1,0:T(8,128)(2,1)S(1)} %collective-permute-done.3.refs_6_), channel_id=1, source_target_pairs={{0,16},{16,0},{1,17},{17,1},{2,18},{18,2},{3,19},{19,3},{4,20},{20... | collective-permute-start | bytes 1179656 | tf_op jit(solution)/shard_map/ppermute | solution.py:237
  31.6 10.5 %collective-permute-start.6 = (bf16[512,512]{1,0:T(8,128)(2,1)}, bf16[512,512]{1,0:T(8,128)(2,1)S(1)}, u32[]{:S(2)}, u32[]{:S(2)}) collective-permute-start(bf16[512,512]{1,0:T(8,128)(2,1)} %collective-permute-done.refs_2_), channel_id=1, source_target_pairs={{0,1},{1,0},{2,3},{3,2},{4,5},{5,4},{6,7},{7,6},{8,9},{9,8},{10,11... | collective-permute-start | bytes 1572872 | tf_op jit(solution)/shard_map/ppermute | solution.py:237
  31.6 14.7 %collective-permute-start.8 = (bf16[512,512]{1,0:T(8,128)(2,1)}, bf16[512,512]{1,0:T(8,128)(2,1)}, u32[]{:S(2)}, u32[]{:S(2)}) collective-permute-start(bf16[512,512]{1,0:T(8,128)(2,1)} %collective-permute-done.2.refs_0_), channel_id=1, source_target_pairs={{0,2},{1,3},{2,0},{3,1},{4,6},{5,7},{6,4},{7,5},{8,10},{9,11},{10,... | collective-permute-start | bytes 1572872 | tf_op jit(solution)/shard_map/ppermute | solution.py:237
  34.1 13.8 %collective-permute-start.9 = (bf16[512,384]{1,0:T(8,128)(2,1)S(1)}, bf16[512,384]{1,0:T(8,128)(2,1)S(1)}, u32[]{:S(2)}, u32[]{:S(2)}) collective-permute-start(bf16[512,384]{1,0:T(8,128)(2,1)S(1)} %collective-permute-done.4.refs_5_), channel_id=1, source_target_pairs={{0,16},{16,0},{1,17},{17,1},{2,18},{18,2},{3,19},{19,3},{4,20},{20... | collective-permute-start | bytes 1179656 | tf_op jit(solution)/shard_map/ppermute | solution.py:237
  46.3 10.5 %collective-permute-start.10 = (bf16[512,512]{1,0:T(8,128)(2,1)}, bf16[512,512]{1,0:T(8,128)(2,1)}, u32[]{:S(2)}, u32[]{:S(2)}) collective-permute-start(bf16[512,512]{1,0:T(8,128)(2,1)} %collective-permute-done.2.refs_0_), channel_id=1, source_target_pairs={{0,1},{1,0},{2,3},{3,2},{4,5},{5,4},{6,7},{7,6},{8,9},{9,8},{10,11... | collective-permute-start | bytes 1572872 | tf_op jit(solution)/shard_map/ppermute | solution.py:237
  46.3 10.5 %collective-permute-start.11 = (bf16[512,512]{1,0:T(8,128)(2,1)}, bf16[512,512]{1,0:T(8,128)(2,1)}, u32[]{:S(2)}, u32[]{:S(2)}) collective-permute-start(bf16[512,512]{1,0:T(8,128)(2,1)} %collective-permute-done.8.refs_2_), channel_id=1, source_target_pairs={{0,1},{1,0},{2,3},{3,2},{4,5},{5,4},{6,7},{7,6},{8,9},{9,8},{10,11... | collective-permute-start | bytes 1572872 | tf_op jit(solution)/shard_map/ppermute | solution.py:237
  46.8 1.0 %copy-start.8 = (bf16[2,384,128]{2,1,0:T(8,128)(2,1)S(1)}, bf16[2,384,128]{2,1,0:T(8,128)(2,1)}, u32[]{:S(2)}) copy-start(bf16[2,384,128]{2,1,0:T(8,128)(2,1)} %get-tuple-element.101) | copy-start | bytes 589828
  46.8 11.0 %collective-permute-start.12 = (bf16[512,384]{1,0:T(8,128)(2,1)S(1)}, bf16[512,384]{1,0:T(8,128)(2,1)S(1)}, u32[]{:S(2)}, u32[]{:S(2)}) collective-permute-start(bf16[512,384]{1,0:T(8,128)(2,1)S(1)} %collective-permute-done.7.refs_7_), channel_id=1, source_target_pairs={{0,16},{16,0},{1,17},{17,1},{2,18},{18,2},{3,19},{19,3},{4,20},{20... | collective-permute-start | bytes 1179656 | tf_op jit(solution)/shard_map/ppermute | solution.py:237
  47.3 9.5 %copy-start.7 = (bf16[2,384,128]{2,1,0:T(8,128)(2,1)S(1)}, bf16[2,384,128]{2,1,0:T(8,128)(2,1)}, u32[]{:S(2)}) copy-start(bf16[2,384,128]{2,1,0:T(8,128)(2,1)} %get-tuple-element.104) | copy-start | bytes 589828
  47.9 14.3 %collective-permute-start.13 = (bf16[2,384,128]{2,1,0:T(8,128)(2,1)S(1)}, bf16[2,384,128]{2,1,0:T(8,128)(2,1)S(1)}, u32[]{:S(2)}, u32[]{:S(2)}) collective-permute-start(bf16[2,384,128]{2,1,0:T(8,128)(2,1)S(1)} %copy-done.8), channel_id=1, source_target_pairs={{0,8},{4,12},{8,0},{12,4},{1,9},{5,13},{9,1},{13,5},{2,10},{6,14},... | collective-permute-start | bytes 589832 | tf_op jit(solution)/shard_map/ppermute | solution.py:237
  49.0 17.9 %collective-permute-start.14 = (bf16[4,384,128]{2,1,0:T(8,128)(2,1)S(1)}, bf16[4,384,128]{2,1,0:T(8,128)(2,1)S(1)}, u32[]{:S(2)}, u32[]{:S(2)}) collective-permute-start(bf16[4,384,128]{2,1,0:T(8,128)(2,1)S(1)} %bitcast.26), channel_id=1, source_target_pairs={{0,4},{4,0},{8,12},{12,8},{1,5},{5,1},{9,13},{13,9},{2,6},{6,2},{1... | collective-permute-start | bytes 1179656 | tf_op jit(solution)/shard_map/ppermute | solution.py:237
  56.8 11.9 %collective-permute-start.15 = (bf16[2,384,128]{2,1,0:T(8,128)(2,1)S(1)}, bf16[2,384,128]{2,1,0:T(8,128)(2,1)S(1)}, u32[]{:S(2)}, u32[]{:S(2)}) collective-permute-start(bf16[2,384,128]{2,1,0:T(8,128)(2,1)S(1)} %copy-done.7), channel_id=1, source_target_pairs={{0,12},{4,8},{8,4},{12,0},{1,13},{5,9},{9,5},{13,1},{2,14},{6,10},... | collective-permute-start | bytes 589832 | tf_op jit(solution)/shard_map/ppermute | solution.py:237
  57.8 5.9 %copy-start = (bf16[512,512]{1,0:T(8,128)(2,1)S(1)}, bf16[512,512]{1,0:T(8,128)(2,1)}, u32[]{:S(2)}) copy-start(bf16[512,512]{1,0:T(8,128)(2,1)} %refs_0_.1) | copy-start | bytes 1572868
  57.8 5.9 %copy-start.2 = (bf16[512,512]{1,0:T(8,128)(2,1)S(1)}, bf16[512,512]{1,0:T(8,128)(2,1)}, u32[]{:S(2)}) copy-start(bf16[512,512]{1,0:T(8,128)(2,1)} %copy-done.1) | copy-start | bytes 1572868
  57.8 5.9 %copy-start.4 = (bf16[512,512]{1,0:T(8,128)(2,1)S(1)}, bf16[512,512]{1,0:T(8,128)(2,1)}, u32[]{:S(2)}) copy-start(bf16[512,512]{1,0:T(8,128)(2,1)} %copy-done.3) | copy-start | bytes 1572868
  61.5 10.2 %collective-permute-start.16 = (bf16[512,384]{1,0:T(8,128)(2,1)S(1)}, bf16[512,384]{1,0:T(8,128)(2,1)S(1)}, u32[]{:S(2)}, u32[]{:S(2)}) collective-permute-start(bf16[512,384]{1,0:T(8,128)(2,1)S(1)} %shard_map.55.refs_0_), channel_id=1, source_target_pairs={{0,2},{1,3},{2,0},{3,1},{4,6},{5,7},{6,4},{7,5},{8,10},{9,11},{10,... | collective-permute-start | bytes 1179656 | tf_op jit(solution)/shard_map/ppermute | solution.py:237
  62.2 10.1 %collective-permute-start.17 = (bf16[2,384,128]{2,1,0:T(8,128)(2,1)S(1)}, bf16[2,384,128]{2,1,0:T(8,128)(2,1)S(1)}, u32[]{:S(2)}, u32[]{:S(2)}) collective-permute-start(bf16[2,384,128]{2,1,0:T(8,128)(2,1)S(1)} %collective-permute-done.13.refs_6_), channel_id=1, source_target_pairs={{0,16},{16,0},{1,17},{17,1},{2,18},{18,2},{3,19},{19,3},{4,20},{20... | collective-permute-start | bytes 589832 | tf_op jit(solution)/shard_map/ppermute | solution.py:237
  63.7 10.7 %collective-permute-start.19 = (bf16[512,384]{1,0:T(8,128)(2,1)S(1)}, bf16[512,384]{1,0:T(8,128)(2,1)S(1)}, u32[]{:S(2)}, u32[]{:S(2)}) collective-permute-start(bf16[512,384]{1,0:T(8,128)(2,1)S(1)} %shard_map.55.refs_0_), channel_id=1, source_target_pairs={{0,1},{1,0},{2,3},{3,2},{4,5},{5,4},{6,7},{7,6},{8,9},{9,8},{10,11... | collective-permute-start | bytes 1179656 | tf_op jit(solution)/shard_map/ppermute | solution.py:237
  68.7 5.7 %collective-permute-start.18 = (bf16[2,384,128]{2,1,0:T(8,128)(2,1)S(1)}, bf16[2,384,128]{2,1,0:T(8,128)(2,1)S(1)}, u32[]{:S(2)}, u32[]{:S(2)}) collective-permute-start(bf16[2,384,128]{2,1,0:T(8,128)(2,1)S(1)} %collective-permute-done.15.refs_8_), channel_id=1, source_target_pairs={{0,16},{16,0},{1,17},{17,1},{2,18},{18,2},{3,19},{19,3},{4,20},{20... | collective-permute-start | bytes 589832 | tf_op jit(solution)/shard_map/ppermute | solution.py:237
  71.7 2.7 %collective-permute-start.20 = (bf16[512,384]{1,0:T(8,128)(2,1)S(1)}, bf16[512,384]{1,0:T(8,128)(2,1)S(1)}, u32[]{:S(2)}, u32[]{:S(2)}) collective-permute-start(bf16[512,384]{1,0:T(8,128)(2,1)S(1)} %collective-permute-done.16.refs_2_), channel_id=1, source_target_pairs={{0,1},{1,0},{2,3},{3,2},{4,5},{5,4},{6,7},{7,6},{8,9},{9,8},{10,11... | collective-permute-start | bytes 1179656 | tf_op jit(solution)/shard_map/ppermute | solution.py:237
  71.8 11.6 %collective-permute-start.22 = (bf16[512,384]{1,0:T(8,128)(2,1)S(1)}, bf16[512,384]{1,0:T(8,128)(2,1)S(1)}, u32[]{:S(2)}, u32[]{:S(2)}) collective-permute-start(bf16[512,384]{1,0:T(8,128)(2,1)S(1)} %shard_map.58.refs_0_), channel_id=1, source_target_pairs={{0,1},{1,0},{2,3},{3,2},{4,5},{5,4},{6,7},{7,6},{8,9},{9,8},{10,11... | collective-permute-start | bytes 1179656 | tf_op jit(solution)/shard_map/ppermute | solution.py:237
  72.3 11.1 %collective-permute-start.21 = (bf16[512,384]{1,0:T(8,128)(2,1)S(1)}, bf16[512,384]{1,0:T(8,128)(2,1)S(1)}, u32[]{:S(2)}, u32[]{:S(2)}) collective-permute-start(bf16[512,384]{1,0:T(8,128)(2,1)S(1)} %shard_map.58.refs_0_), channel_id=1, source_target_pairs={{0,2},{1,3},{2,0},{3,1},{4,6},{5,7},{6,4},{7,5},{8,10},{9,11},{10,... | collective-permute-start | bytes 1179656 | tf_op jit(solution)/shard_map/ppermute | solution.py:237
  76.0 13.1 %collective-permute-start.24 = (bf16[512,512]{1,0:T(8,128)(2,1)S(1)}, bf16[512,512]{1,0:T(8,128)(2,1)S(1)}, u32[]{:S(2)}, u32[]{:S(2)}) collective-permute-start(bf16[512,512]{1,0:T(8,128)(2,1)S(1)} %shard_map.67), channel_id=1, source_target_pairs={{0,4},{4,0},{8,12},{12,8},{1,5},{5,1},{9,13},{13,9},{2,6},{6,2},{1... | collective-permute-start | bytes 1572872 | tf_op jit(solution)/shard_map/ppermute | solution.py:237
  83.4 1.7 %collective-permute-start.23 = (bf16[512,384]{1,0:T(8,128)(2,1)S(1)}, bf16[512,384]{1,0:T(8,128)(2,1)S(1)}, u32[]{:S(2)}, u32[]{:S(2)}) collective-permute-start(bf16[512,384]{1,0:T(8,128)(2,1)S(1)} %collective-permute-done.21.refs_2_), channel_id=1, source_target_pairs={{0,1},{1,0},{2,3},{3,2},{4,5},{5,4},{6,7},{7,6},{8,9},{9,8},{10,11... | collective-permute-start | bytes 1179656 | tf_op jit(solution)/shard_map/ppermute | solution.py:237
  (2 other events, 1.6 us)
